TPU v7x, 32 devices: a whole 2x2x4 slice. The times are simulated.
32 devices in a mesh: sx: 4 (over z), sy: 4 (over x, core), fq: 2 (over y).
Axes of the slice: x: 2, y: 2, z: 4, core: 2. Of those that a mesh axis runs over, the one named last changes fastest.
Arguments:
- spectra: bfloat16 [16, 2, 128, 64, 512], P('fq', None, 'sx', 'sy'), may hold values from -0.125 to 0.125
- noise_weight: float32 [512, 32], P(('sx', 'sy')), may hold values from 0.5 to 2
- class_map: int32 [128, 64], P('sx', 'sy'), may hold values from 0 to 7
- class_kappa: float32 [8], replicated, may hold values from 0.25 to 4
- solution: float32 [16, 512, 32], P('fq', ('sx', 'sy')), may hold values from -6 to 6
- residual: float32 [16, 512, 32], P('fq', ('sx', 'sy')), may hold values from -6 to 6
- direction: float32 [16, 512, 32], P('fq', ('sx', 'sy')), may hold values from -6 to 6
- step_length: float32 [16], P('fq'), may hold values from 0.2 to 1
- old_norm: float32 [16], P('fq'), may hold values from 16384 to 65536
Outputs:
- new_solution: float32 [16, 512, 32], P('fq', ('sx', 'sy'))
- new_residual: float32 [16, 512, 32], P('fq', ('sx', 'sy'))
- new_direction: float32 [16, 512, 32], P('fq', ('sx', 'sy'))
- new_norm: float32 [16], P('fq')
All inputs are finite; a program needn't handle non-finite values.
Results may differ from a plain program's by a relative error of at most 0.0022.
Values may be sent and summed in bfloat16 or wider, within the bound.
No kernel may reach another device: no remote copies, remote signals or barrier semaphores. Data moves between devices by JAX's collectives and lax.ppermute only.
A program may use at most 128 MiB of HBM per device.

v0:
```python
import functools
import math

import jax
import jax.numpy as jnp
from jax import lax
from jax.experimental import pallas as pl
from jax.experimental.pallas import tpu as pltpu
from jax.sharding import PartitionSpec as P
import numpy as np

SWEEPS = 4
DEPTH = SWEEPS - 1
HIGHEST = lax.Precision.HIGHEST
F32 = jnp.float32
BF16 = jnp.bfloat16
GRID_AXES = ("sx", "sy")
ALL_AXES = ("sx", "sy", "fq")
LANES = 128
VMEM_LIMIT = 48 * 1024 * 1024
VMEM = pl.BlockSpec(memory_space=pltpu.VMEM)
SMEM = pl.BlockSpec(memory_space=pltpu.SMEM)
ANY = pl.BlockSpec(memory_space=pl.ANY)


def params():
    return pltpu.CompilerParams(vmem_limit_bytes=VMEM_LIMIT)


def tables(freq_count, local_freqs, local_cols, time_steps):
    freq = np.arange(freq_count)[:, None]
    step = np.arange(time_steps)[None, :]
    phases = (freq * step % time_steps) * (2.0 * math.pi / time_steps)
    factor = 1.0 / math.sqrt(time_steps)
    pair = np.stack([np.cos(phases) * factor, -np.sin(phases) * factor], 1)
    forward = np.repeat(pair.reshape(2 * freq_count, time_steps), local_cols, 0)
    doubling = np.where(np.arange(freq_count) == 0, 1.0, 2.0)[:, None, None]
    inverse = np.repeat((pair * doubling).reshape(2 * freq_count, time_steps), local_cols, 0)
    return forward.T.astype(np.float32), inverse.astype(np.float32)


def lane_ids(lanes):
    return lax.broadcasted_iota(jnp.int32, (1, lanes), 1)


def spectrum_kernel(tiles, fq_blocks, direction_ref, noise_ref, table_ref, out_ref):
    cols, sensors, steps = direction_ref.shape
    lanes = table_ref.shape[1]
    weighted = (noise_ref[...][None] * direction_ref[...]).reshape(cols * sensors, steps)
    full = jnp.dot(weighted, table_ref[...], precision=HIGHEST, preferred_element_type=F32)
    col_of = lane_ids(lanes) % cols
    spec = full[0:sensors]
    for col in range(1, cols):
        spec = jnp.where(col_of == col, full[col * sensors : (col + 1) * sensors], spec)
    spec = spec.astype(BF16)
    block = lanes // fq_blocks
    for b in range(fq_blocks):
        part = spec[:, b * block : (b + 1) * block]
        out_ref[:, b] = jnp.broadcast_to(part[None], (tiles, sensors, block))


def adjoint_kernel(
    freqs, cols, spectra_ref, spec_ref, class_ref, out_ref, low_ref, high_ref, ends_ref, held, sems
):
    _, _, cells_x, cells_y, all_sensors = spectra_ref.shape
    cells = cells_x * cells_y
    stride = out_ref.shape[2] // cells_x
    lanes = spec_ref.shape[1] * spec_ref.shape[3]

    def fetch(f):
        return pltpu.make_async_copy(spectra_ref.at[f], held.at[f], sems.at[f])

    @pl.when(pl.program_id(0) == 0)
    def _():
        for f in range(freqs):
            fetch(f).start()

    parts = [
        spec_ref[:, b].reshape(all_sensors, spec_ref.shape[3]) for b in range(spec_ref.shape[1])
    ]
    direct = jnp.concatenate(parts, axis=1)
    wide = direct.astype(F32)
    is_real = (lane_ids(lanes) // cols) % 2 == 0
    turned = jnp.where(
        is_real, pltpu.roll(wide, lanes - cols, 1), -pltpu.roll(wide, cols, 1)
    ).astype(BF16)
    stacked = jnp.concatenate([direct, turned], axis=0)
    freq_of = (lane_ids(lanes) // (2 * cols)) % freqs

    row = lax.broadcasted_iota(jnp.int32, (cells, cells_x), 0)
    pick = (row // cells_y == lax.broadcasted_iota(jnp.int32, (cells, cells_x), 1)).astype(F32)
    by_row = jnp.dot(pick, class_ref[...].astype(F32) + 1.0, preferred_element_type=F32)
    at = lax.broadcasted_iota(jnp.int32, (cells, cells_y), 0) % cells_y
    own = (at == lax.broadcasted_iota(jnp.int32, (cells, cells_y), 1)).astype(F32)
    classes = jnp.dot(
        by_row * own, jnp.ones((cells_y, LANES), F32), preferred_element_type=F32
    )

    acc = None
    for f in range(freqs):

        @pl.when(pl.program_id(0) == 0)
        def _():
            fetch(f).wait()

        both = held[f].reshape(2, cells, all_sensors)
        both = jnp.concatenate([both[0], both[1]], axis=1)
        got = jnp.dot(both, stacked, preferred_element_type=F32)
        acc = got if acc is None else jnp.where(freq_of == f, got, acc)
    for k in range(out_ref.shape[1]):
        part = classes if k * LANES == lanes else acc[:, k * LANES : (k + 1) * LANES]
        for x in range(cells_x):
            base = x * stride
            out_ref[0, k, base : base + cells_y] = part[x * cells_y : (x + 1) * cells_y]
            out_ref[0, k, base + cells_y : base + stride] = jnp.zeros((stride - cells_y, LANES), F32)
        at = slice(k * LANES, (k + 1) * LANES)
        for j in range(DEPTH):
            low = out_ref[0, k, pl.ds(j, cells_x, stride=stride), :]
            high = out_ref[0, k, pl.ds(cells_y - DEPTH + j, cells_x, stride=stride), :]
            low_ref[0, j * cells_x : (j + 1) * cells_x, at] = low.astype(BF16)
            high_ref[0, j * cells_x : (j + 1) * cells_x, at] = high.astype(BF16)
        ends_ref[0, 0, :, at] = out_ref[0, k, 0 : DEPTH * stride]
        ends_ref[0, 1, :, at] = out_ref[0, k, (cells_x - DEPTH) * stride : cells_x * stride]


def ends_kernel(ends_ref, before_ref, after_ref, top_ref, bottom_ref, held):
    span = ends_ref.shape[2]
    stride = span // DEPTH
    cells_x = before_ref.shape[1] // DEPTH
    cells_y = stride - 8
    before = before_ref[0].astype(F32)
    after = after_ref[0].astype(F32)
    for side, out in ((0, top_ref), (1, bottom_ref)):
        held[...] = jnp.zeros_like(held)
        held[8 : 8 + span] = ends_ref[0, side]
        first = 0 if side == 0 else cells_x - DEPTH
        for x in range(DEPTH):
            for j in range(DEPTH):
                take = j * cells_x + first + x
                to = 8 + x * stride
                held[to + cells_y + j : to + cells_y + j + 1] = after[take : take + 1]
                held[to - DEPTH + j : to - DEPTH + j + 1] = before[take : take + 1]
        out[0] = held[8 - DEPTH : 8 - DEPTH + span].astype(BF16)


def field_kernel(
    freqs,
    cols,
    spectra_ref,
    source_ref,
    before_ref,
    after_ref,
    above_ref,
    below_ref,
    kappa_ref,
    out_ref,
    held,
    sems,
    wide,
    gain,
    one,
    two,
    sums,
):
    _, _, cells_x, cells_y, all_sensors = spectra_ref.shape
    cells = cells_x * cells_y
    stride = source_ref.shape[2] // cells_x
    slabs = one.shape[0]
    lanes = slabs * LANES
    start = (DEPTH + 1) * stride
    rows = cells_x * stride
    span = DEPTH * stride

    def fetch(f):
        return pltpu.make_async_copy(spectra_ref.at[f], held.at[f], sems.at[f])

    @pl.when(pl.program_id(0) == 0)
    def _():
        for f in range(freqs):
            fetch(f).start()

    total = wide.shape[1]
    lo, hi = start - span - 8, start + rows + span
    for k in range(slabs + 1):
        at = slice(k * LANES, (k + 1) * LANES)
        wide[k, 0:start] = jnp.zeros((start, LANES), F32)
        wide[k, start + rows : total] = jnp.zeros((total - start - rows, LANES), F32)
        wide[k, start : start + rows] = source_ref[0, k]
        before = before_ref[0, :, at].astype(F32)
        after = after_ref[0, :, at].astype(F32)
        for j in range(DEPTH):
            part = slice(j * cells_x, (j + 1) * cells_x)
            wide[k, pl.ds(start + cells_y + j, cells_x, stride=stride), :] = after[part]
            wide[k, pl.ds(start - DEPTH + j, cells_x, stride=stride), :] = before[part]
        wide[k, start - span - DEPTH : start - DEPTH] = above_ref[0, :, at].astype(F32)
        wide[k, start + rows - DEPTH : start + rows + span - DEPTH] = below_ref[0, :, at].astype(F32)

    classes = wide[slabs, lo:hi]
    kappa = jnp.zeros_like(classes)
    for n in range(kappa_ref.shape[0]):
        kappa = jnp.where(classes == n + 1.0, kappa_ref[n], kappa)
    scale = jnp.where(classes > 0.0, 1.0 / (1.0 + 4.0 * kappa), 0.0)
    gain[lo:hi] = kappa * scale

    def sweep(k, old, new, margin):
        first = start - margin * stride - 8
        last = start + rows + margin * stride
        near = (
            old[k, first - stride : last - stride]
            + old[k, first + stride : last + stride]
            + old[k, first - 1 : last - 1]
            + old[k, first + 1 : last + 1]
        )
        new[k, first:last] = wide[k, first:last] + gain[first:last] * near

    turned = []
    for k in range(slabs):
        wide[k, lo:hi] = wide[k, lo:hi] * scale
        one[k] = wide[k]
        old, new = one, two
        for margin in range(DEPTH - 1, -1, -1):
            sweep(k, old, new, margin)
            old, new = new, old
        field = old[k, start : start + rows].reshape(cells_x, stride, LANES)[:, 0:cells_y]
        turned.append(field.reshape(cells, LANES).T)
    turned = jnp.concatenate(turned, axis=0)
    blocks = lanes // (2 * cols)
    pair = turned.reshape(blocks, 2, cols, cells)
    plain = pair.astype(BF16).reshape(blocks, 2 * cols, cells)
    crossed = jnp.stack([-pair[:, 1], pair[:, 0]], axis=1)
    crossed = crossed.astype(BF16).reshape(blocks, 2 * cols, cells)
    groups = blocks // freqs
    for f in range(freqs):

        @pl.when(pl.program_id(0) == 0)
        def _():
            fetch(f).wait()

        ours = [
            jnp.concatenate([plain[g * freqs + f], crossed[g * freqs + f]], axis=1)
            for g in range(groups)
        ]
        left = jnp.concatenate(ours, axis=0)
        got = jnp.dot(
            left, held[f].reshape(2 * cells, all_sensors), preferred_element_type=F32
        )
        for g in range(groups):
            at = (g * freqs + f) * 2 * cols
            sums[at : at + 2 * cols] = got[g * 2 * cols : (g + 1) * 2 * cols]
    back = sums[...].T.astype(BF16)
    tiles, _, sensors, block = out_ref.shape
    for g in range(groups):
        out_ref[:, g] = back[:, g * block : (g + 1) * block].reshape(tiles, sensors, block)


def residual_kernel(
    terms_ref,
    table_ref,
    noise_ref,
    solution_ref,
    residual_ref,
    direction_ref,
    step_ref,
    new_solution_ref,
    new_residual_ref,
    norm_ref,
):
    cols, sensors, steps = direction_ref.shape
    parts = []
    for b in range(terms_ref.shape[1]):
        parts.append(jnp.sum(terms_ref[:, b].astype(F32), axis=0))
    spectrum = jnp.concatenate(parts, axis=1)
    col_of = lane_ids(spectrum.shape[1]) % cols
    left = jnp.concatenate([jnp.where(col_of == c, spectrum, 0.0) for c in range(cols)], axis=0)
    returned = jnp.dot(left, table_ref[...], precision=HIGHEST, preferred_element_type=F32)
    for c in range(cols):
        direction = direction_ref[c]
        product = direction + noise_ref[...] * returned[c * sensors : (c + 1) * sensors]
        new_solution_ref[c] = solution_ref[c] + step_ref[c] * direction
        new_residual = residual_ref[c] - step_ref[c] * product
        new_residual_ref[c] = new_residual
        norm_ref[c : c + 1] = jnp.sum(
            jnp.sum(new_residual * new_residual, axis=0, keepdims=True), axis=1, keepdims=True
        ) + jnp.zeros((1, norm_ref.shape[1]), F32)


def direction_kernel(norms_ref, residual_ref, direction_ref, old_ref, out_ref, norm_ref):
    cols, sensors, steps = direction_ref.shape
    norm = jnp.sum(norms_ref[...], axis=0)
    for c in range(cols):
        out_ref[c] = residual_ref[c] + (norm[c : c + 1, 0:1] / old_ref[c]) * direction_ref[c]
        norm_ref[c] = jnp.max(norm[c : c + 1])


def swap(axis, toward_partner, toward_other):
    count = lax.axis_size(axis)
    near = [(i, i ^ 1) for i in range(count) if (i ^ 1) < count]
    far = [(i, i + 1 if i % 2 else i - 1) for i in range(1, count - 1 + count % 2)]
    second = lax.ppermute(toward_other, axis, far)
    first = lax.ppermute(toward_partner, axis, near)
    return first, second


def exchange(axis, low, high):
    even = lax.axis_index(axis) % 2 == 0
    first, second = swap(axis, jnp.where(even, high, low), jnp.where(even, low, high))
    return jnp.where(even, second, first), jnp.where(even, first, second)


def on_device(
    spectra,
    noise_weight,
    class_map,
    class_kappa,
    solution,
    residual,
    direction,
    step_length,
    old_norm,
):
    local_freqs, _, cells_x, cells_y, all_sensors = spectra.shape
    cols, sensors, steps = direction.shape
    fq_blocks = lax.axis_size("fq")
    tiles = lax.axis_size("sx") * lax.axis_size("sy")
    block = 2 * local_freqs * cols
    lanes = block * fq_blocks
    forward, inverse = tables(local_freqs * fq_blocks, local_freqs, cols, steps)
    group = 2 if fq_blocks % 2 == 0 else 1
    chunks = fq_blocks // group
    width = group * block
    stride = cells_y + 8
    wide = width + LANES
    cells = cells_x * cells_y

    spec = pl.pallas_call(
        functools.partial(spectrum_kernel, tiles, fq_blocks),
        out_shape=jax.ShapeDtypeStruct((tiles, fq_blocks, sensors, block), BF16),
        in_specs=[VMEM] * 3,
        out_specs=VMEM,
        compiler_params=params(),
        name="spectrum",
    )(direction, noise_weight, forward)
    spec = lax.all_to_all(
        spec.reshape(tiles * fq_blocks, sensors, block), ALL_AXES, 0, 0, tiled=True
    ).reshape(tiles, fq_blocks, sensors, block)

    def chunked(*shape):
        return pl.BlockSpec((1,) + shape, lambda i: (i,) + (0,) * len(shape))

    by_block = pl.BlockSpec((tiles, group, sensors, block), lambda i: (0, i, 0, 0))
    held = [
        pltpu.VMEM((local_freqs, 2, cells_x, cells_y, all_sensors), BF16),
        pltpu.SemaphoreType.DMA((local_freqs,)),
    ]
    source, low, high, ends = pl.pallas_call(
        functools.partial(adjoint_kernel, local_freqs, cols),
        grid=(chunks,),
        out_shape=(
            jax.ShapeDtypeStruct((chunks, wide // LANES, cells_x * stride, LANES), F32),
            jax.ShapeDtypeStruct((chunks, DEPTH * cells_x, wide), BF16),
            jax.ShapeDtypeStruct((chunks, DEPTH * cells_x, wide), BF16),
            jax.ShapeDtypeStruct((chunks, 2, DEPTH * stride, wide), F32),
        ),
        in_specs=[ANY, by_block, pl.BlockSpec((cells_x, cells_y), lambda i: (0, 0))],
        out_specs=(
            chunked(wide // LANES, cells_x * stride, LANES),
            chunked(DEPTH * cells_x, wide),
            chunked(DEPTH * cells_x, wide),
            chunked(2, DEPTH * stride, wide),
        ),
        scratch_shapes=held,
        compiler_params=params(),
        name="adjoint",
    )(spectra, spec, class_map)
    before, after = exchange("sy", low, high)
    top, bottom = pl.pallas_call(
        ends_kernel,
        grid=(chunks,),
        out_shape=(jax.ShapeDtypeStruct((chunks, DEPTH * stride, wide), BF16),) * 2,
        in_specs=[
            chunked(2, DEPTH * stride, wide),
            chunked(DEPTH * cells_x, wide),
            chunked(DEPTH * cells_x, wide),
        ],
        out_specs=(chunked(DEPTH * stride, wide),) * 2,
        scratch_shapes=[pltpu.VMEM((DEPTH * stride + 16, wide), F32)],
        compiler_params=params(),
        name="ends",
    )(ends, before, after)
    above, below = exchange("sx", top, bottom)
    total = (cells_x + 2 * DEPTH + 2) * stride
    terms = pl.pallas_call(
        functools.partial(field_kernel, local_freqs, cols),
        grid=(chunks,),
        out_shape=jax.ShapeDtypeStruct((tiles, fq_blocks, sensors, block), BF16),
        in_specs=[
            ANY,
            chunked(wide // LANES, cells_x * stride, LANES),
            chunked(DEPTH * cells_x, wide),
            chunked(DEPTH * cells_x, wide),
            chunked(DEPTH * stride, wide),
            chunked(DEPTH * stride, wide),
            SMEM,
        ],
        out_specs=by_block,
        scratch_shapes=held
        + [
            pltpu.VMEM((wide // LANES, total, LANES), F32),
            pltpu.VMEM((total, LANES), F32),
            pltpu.VMEM((width // LANES, total, LANES), F32),
            pltpu.VMEM((width // LANES, total, LANES), F32),
            pltpu.VMEM((width, all_sensors), F32),
        ],
        compiler_params=params(),
        name="field",
    )(spectra, source, before, after, above, below, class_kappa)
    terms = lax.all_to_all(
        terms.reshape(tiles * fq_blocks, sensors, block), ALL_AXES, 0, 0, tiled=True
    ).reshape(tiles, fq_blocks, sensors, block)
    held_shape = jax.ShapeDtypeStruct(direction.shape, F32)
    new_solution, new_residual, norm = pl.pallas_call(
        residual_kernel,
        out_shape=(held_shape, held_shape, jax.ShapeDtypeStruct((cols, 128), F32)),
        in_specs=[VMEM] * 6 + [SMEM],
        out_specs=(VMEM,) * 3,
        compiler_params=params(),
        name="residual",
    )(terms, inverse, noise_weight, solution, residual, direction, step_length)
    norms = lax.all_to_all(
        jnp.broadcast_to(norm[None], (tiles, cols, 128)), GRID_AXES, 0, 0, tiled=True
    )
    new_direction, new_norm = pl.pallas_call(
        direction_kernel,
        out_shape=(held_shape, jax.ShapeDtypeStruct((cols,), F32)),
        in_specs=[VMEM] * 3 + [SMEM],
        out_specs=(VMEM, SMEM),
        compiler_params=params(),
        name="direction",
    )(norms, new_residual, direction, old_norm)
    return (new_solution, new_residual, new_direction, new_norm)


def solution(mesh):
    return jax.shard_map(
        on_device,
        mesh=mesh,
        in_specs=(
            P("fq", None, "sx", "sy", None),
            P(("sx", "sy"), None),
            P("sx", "sy"),
            P(),
            P("fq", ("sx", "sy"), None),
            P("fq", ("sx", "sy"), None),
            P("fq", ("sx", "sy"), None),
            P("fq"),
            P("fq"),
        ),
        out_specs=(
            P("fq", ("sx", "sy"), None),
            P("fq", ("sx", "sy"), None),
            P("fq", ("sx", "sy"), None),
            P("fq"),
        ),
        check_vma=False,
    )
```

profile of v0, /device:TPU:0, one launch (start us, length us, event | category | flops | bytes accessed | tf_op | source)
XLA Modules:
  0.0 73.8 jit_solution(4463559772708059571)
XLA Ops:
  0.6 0.0 copy-start
  0.6 0.9 %copy-done = f32[8,32,32]{2,1,0:T(8,128)S(1)} copy-done((f32[8,32,32]{2,1,0:T(8,128)S(1)}, f32[8,32,32]{2,1,0:T(8,128)}, u32[]{:S(2)}) %copy-start) | copy-done | bytes 32792
  1.5 0.0 copy-start.6
  1.5 0.7 copy-done.6
  2.3 0.0 copy-start.8
  2.3 0.8 %copy-done.8 = f32[32,256]{1,0:T(8,128)S(1)} copy-done((f32[32,256]{1,0:T(8,128)S(1)}, f32[32,256]{1,0:T(8,128)}, u32[]{:S(2)}) %copy-start.8) | copy-done | bytes 32792
  3.0 0.0 copy-start.9
  3.0 1.1 %spectrum.1 = bf16[16,2,32,128]{3,2,1,0:T(8,128)(2,1)} custom-call(f32[8,32,32]{2,1,0:T(8,128)S(1)} %copy-done, f32[32,32]{1,0:T(8,128)S(1)} %copy-done.6, f32[32,256]{1,0:T(8,128)S(1)} %copy-done.8), custom_call_target="tpu_custom_call" | custom-call | tf_op jit(solution)/shard_map/spectrum/pallas_call | solution.py:335
  4.1 7.3 %all-to-all-start = ((bf16[32,32,128]{2,1,0:T(8,128)(2,1)}), bf16[32,32,128]{2,1,0:T(8,128)(2,1)S(1)}, u32[]{:S(2)}, u32[]{:S(2)}) async-start(bf16[32,32,128]{2,1,0:T(8,128)(2,1)} %bitcast), calls=%async_computation | async-start | bytes 524288 | tf_op jit(solution)/shard_map/all_to_all | solution.py:343
  11.4 0.8 %copy.15.class_ref = s32[32,16]{1,0:T(8,128)S(1)} copy(s32[32,16]{0,1:T(8,128)} %param.13) | data formatting | bytes 4096 | tf_op args[2]
  12.2 9.9 %all-to-all-done = bf16[32,32,128]{2,1,0:T(8,128)(2,1)S(1)} async-done(((bf16[32,32,128]{2,1,0:T(8,128)(2,1)}), bf16[32,32,128]{2,1,0:T(8,128)(2,1)S(1)}, u32[]{:S(2)}, u32[]{:S(2)}) %all-to-all-start) | async-done | bytes 262176 | tf_op jit(solution)/shard_map/all_to_all | solution.py:343
  22.1 0.0 copy-start.1
  22.1 0.0 copy-start.3
  22.1 0.0 copy-start.4
  22.1 0.0 copy-start.5
  22.1 0.0 copy-start.7
  22.1 0.0 copy-start.11
  22.1 7.1 %adjoint.1 = (f32[1,3,768,128]{3,2,1,0:T(8,128)S(1)}, bf16[1,96,384]{2,1,0:T(8,128)(2,1)S(1)}, bf16[1,96,384]{2,1,0:T(8,128)(2,1)S(1)}, f32[1,2,72,384]{3,2,1,0:T(8,128)S(1)}) custom-call(bf16[8,2,32,16,512]{4,3,2,1,0:T(8,128)(2,1)} %spectra_ref.3, bf16[16,2,32,128]{3,2,1,0:T(8,128)(2,1)S(1)} %bitcast.4, s32[32,16]{1,0:T(8,128)S(1)} %copy.15.class_ref), custom_call_target="tpu_custom_call" | custom-call | tf_op jit(solution)/shard_map/adjoint/pallas_call | solution.py:355
  29.3 0.0 copy-start.10
  29.3 0.2 collective-permute-start.1
  29.5 0.7 collective-permute-start
  30.2 0.5 collective-permute-done.1
  30.6 0.0 collective-permute-done
  30.7 0.1 ends.1
  30.8 0.5 collective-permute-start.3
  31.3 0.7 collective-permute-start.2
  32.0 3.0 %collective-permute-done.3 = bf16[1,72,384]{2,1,0:T(8,128)(2,1)S(1)} collective-permute-done((bf16[1,72,384]{2,1,0:T(8,128)(2,1)S(1)}, bf16[1,72,384]{2,1,0:T(8,128)(2,1)S(1)}, u32[]{:S(2)}, u32[]{:S(2)}) %collective-permute-start.3) | collective-permute-done | bytes 55328 | tf_op jit(solution)/shard_map/ppermute | solution.py:300
  35.0 0.0 collective-permute-done.2
  35.0 0.0 copy-done.9
  35.0 5.6 %field.1 = bf16[16,2,32,128]{3,2,1,0:T(8,128)(2,1)S(1)} custom-call(bf16[8,2,32,16,512]{4,3,2,1,0:T(8,128)(2,1)} %spectra_ref.3, f32[1,3,768,128]{3,2,1,0:T(8,128)S(1)} %get-tuple-element.15.source_ref, bf16[1,96,384]{2,1,0:T(8,128)(2,1)S(1)} %get-tuple-element.27.before_ref, bf16[1,96,384]{2,1,0:T(8,128)(2,1)S(1)} %get-tuple-element.26.after_ref, ...), custom_call_target="tpu_custom_call" | custom-call | tf_op jit(solution)/shard_map/field/pallas_call | solution.py:392
  40.7 19.7 %all_to_all.15 = bf16[32,32,128]{2,1,0:T(8,128)(2,1)S(1)} all-to-all(bf16[32,32,128]{2,1,0:T(8,128)(2,1)S(1)} %bitcast.5), channel_id=1, replica_groups=mesh['sx'=4,'sy'=4,'fq'=2] {'sx','sy','fq'}, dimensions={0} | all-to-all | bytes 524288 | tf_op jit(solution)/shard_map/all_to_all | solution.py:417
  60.4 0.0 copy-done.1
  60.4 0.0 copy-done.3
  60.4 0.0 copy-done.4
  60.4 0.0 copy-done.5
  60.4 0.0 copy-done.7
  60.4 0.0 copy-done.11
  60.4 1.6 %residual.1 = (f32[8,32,32]{2,1,0:T(8,128)}, f32[8,32,32]{2,1,0:T(8,128)}, f32[8,128]{1,0:T(8,128)S(1)}) custom-call(bf16[16,2,32,128]{3,2,1,0:T(8,128)(2,1)S(1)} %bitcast.6, f32[256,32]{1,0:T(8,128)S(1)} %copy-done.5, f32[32,32]{1,0:T(8,128)S(1)} %copy-done.7, f32[8,32,32]{2,1,0:T(8,128)S(1)} %copy-done.3, f32[8,32,32]{2,1,0:T(8,128)S(1)} %copy-done.4, ...), custom_call_target="tpu_custom_call" | custom-call | tf_op jit(solution)/shard_map/residual/pallas_call | solution.py:421
  62.0 9.5 %all_to_all.16.norms_ref = f32[16,8,128]{2,1,0:T(8,128)S(1)} all-to-all(f32[16,8,128]{2,1,0:T(8,128)S(1)} %broadcast_in_dim.2), channel_id=1, replica_groups=mesh['sx'=4,'sy'=4,'fq'=2] {'sx','sy'}, dimensions={0} | all-to-all | bytes 131072 | tf_op jit(solution)/shard_map/all_to_all | solution.py:429
  71.5 0.0 copy-done.10
  71.5 0.0 copy-start.2
  71.5 0.9 %copy-done.2 = f32[8,32,32]{2,1,0:T(8,128)S(1)} copy-done((f32[8,32,32]{2,1,0:T(8,128)S(1)}, f32[8,32,32]{2,1,0:T(8,128)}, u32[]{:S(2)}) %copy-start.2) | copy-done | bytes 32792
  72.4 1.3 %direction.1 = (f32[8,32,32]{2,1,0:T(8,128)}, f32[8]{0:T(128)}) custom-call(f32[16,8,128]{2,1,0:T(8,128)S(1)} %all_to_all.16.norms_ref, f32[8,32,32]{2,1,0:T(8,128)S(1)} %copy-done.2, f32[8,32,32]{2,1,0:T(8,128)S(1)} %copy-done.1, f32[8]{0:T(128)S(1)} %copy-done.10), custom_call_target="tpu_custom_call" | custom-call | tf_op jit(solution)/shard_map/direction/pallas_call | solution.py:432
  (5 shorter events, 0.1 us)
Async XLA Ops:
  0.6 0.9 %copy-start = (f32[8,32,32]{2,1,0:T(8,128)S(1)}, f32[8,32,32]{2,1,0:T(8,128)}, u32[]{:S(2)}) copy-start(f32[8,32,32]{2,1,0:T(8,128)} %direction_ref.5) | copy-start | bytes 98308
  1.5 0.7 copy-start.6
  2.3 0.8 %copy-start.8 = (f32[32,256]{1,0:T(8,128)S(1)}, f32[32,256]{1,0:T(8,128)}, u32[]{:S(2)}) copy-start(f32[32,256]{1,0:T(8,128)} %constant.31.clone.table_ref) | copy-start | bytes 98308
  3.0 32.0 %copy-start.9 = (f32[8]{0:T(128)S(1)}, f32[8]{0:T(128)}, u32[]{:S(2)}) copy-start(f32[8]{0:T(128)} %kappa_ref.1) | copy-start | bytes 100
  4.1 18.0 %all-to-all-start = ((bf16[32,32,128]{2,1,0:T(8,128)(2,1)}), bf16[32,32,128]{2,1,0:T(8,128)(2,1)S(1)}, u32[]{:S(2)}, u32[]{:S(2)}) async-start(bf16[32,32,128]{2,1,0:T(8,128)(2,1)} %bitcast), calls=%async_computation | async-start | bytes 524288 | tf_op jit(solution)/shard_map/all_to_all | solution.py:343
  22.1 38.3 %copy-start.1 = (f32[8,32,32]{2,1,0:T(8,128)S(1)}, f32[8,32,32]{2,1,0:T(8,128)}, u32[]{:S(2)}) copy-start(f32[8,32,32]{2,1,0:T(8,128)} %direction_ref.5) | copy-start | bytes 98308
  22.1 38.3 %copy-start.3 = (f32[8,32,32]{2,1,0:T(8,128)S(1)}, f32[8,32,32]{2,1,0:T(8,128)}, u32[]{:S(2)}) copy-start(f32[8,32,32]{2,1,0:T(8,128)} %solution_ref.1) | copy-start | bytes 98308
  22.1 38.3 %copy-start.4 = (f32[8,32,32]{2,1,0:T(8,128)S(1)}, f32[8,32,32]{2,1,0:T(8,128)}, u32[]{:S(2)}) copy-start(f32[8,32,32]{2,1,0:T(8,128)} %residual_ref.1) | copy-start | bytes 98308
  22.1 38.3 %copy-start.5 = (f32[256,32]{1,0:T(8,128)S(1)}, f32[256,32]{1,0:T(8,128)}, u32[]{:S(2)}) copy-start(f32[256,32]{1,0:T(8,128)} %constant.32.clone.table_ref) | copy-start | bytes 98308
  22.1 38.3 %copy-start.7 = (f32[32,32]{1,0:T(8,128)S(1)}, f32[32,32]{1,0:T(8,128)}, u32[]{:S(2)}) copy-start(f32[32,32]{1,0:T(8,128)} %noise_ref.3) | copy-start | bytes 12292
  22.1 38.3 %copy-start.11 = (f32[8]{0:T(128)S(1)}, f32[8]{0:T(128)}, u32[]{:S(2)}) copy-start(f32[8]{0:T(128)} %step_ref.1) | copy-start | bytes 100
  29.3 42.2 %copy-start.10 = (f32[8]{0:T(128)S(1)}, f32[8]{0:T(128)}, u32[]{:S(2)}) copy-start(f32[8]{0:T(128)} %old_ref.1) | copy-start | bytes 100
  29.3 1.3 %collective-permute-start.1 = (bf16[1,96,384]{2,1,0:T(8,128)(2,1)S(1)}, bf16[1,96,384]{2,1,0:T(8,128)(2,1)S(1)}, u32[]{:S(2)}, u32[]{:S(2)}) collective-permute-start(bf16[1,96,384]{2,1,0:T(8,128)(2,1)S(1)} %get-tuple-element.28), channel_id=1, source_target_pairs={{0,2},{2,0},{4,6},{6,4},{1,3},{3,1},{5,7},{7,5},{8,10},{10,8},{12,... | collective-permute-start | bytes 221192 | tf_op jit(solution)/shard_map/ppermute | solution.py:300
  29.5 1.2 %collective-permute-start = (bf16[1,96,384]{2,1,0:T(8,128)(2,1)S(1)}, bf16[1,96,384]{2,1,0:T(8,128)(2,1)S(1)}, u32[]{:S(2)}, u32[]{:S(2)}) collective-permute-start(bf16[1,96,384]{2,1,0:T(8,128)(2,1)S(1)} %get-tuple-element.29), channel_id=1, source_target_pairs={{2,4},{4,2},{3,5},{5,3},{10,12},{12,10},{11,13},{13,11},{18,20},{2... | collective-permute-start | bytes 221192 | tf_op jit(solution)/shard_map/ppermute | solution.py:299
  30.8 4.2 %collective-permute-start.3 = (bf16[1,72,384]{2,1,0:T(8,128)(2,1)S(1)}, bf16[1,72,384]{2,1,0:T(8,128)(2,1)S(1)}, u32[]{:S(2)}, u32[]{:S(2)}) collective-permute-start(bf16[1,72,384]{2,1,0:T(8,128)(2,1)S(1)} %get-tuple-element.32), channel_id=1, source_target_pairs={{0,8},{8,0},{16,24},{24,16},{1,9},{9,1},{17,25},{25,17},{2,10},{10... | collective-permute-start | bytes 165896 | tf_op jit(solution)/shard_map/ppermute | solution.py:300
  31.3 3.7 %collective-permute-start.2 = (bf16[1,72,384]{2,1,0:T(8,128)(2,1)S(1)}, bf16[1,72,384]{2,1,0:T(8,128)(2,1)S(1)}, u32[]{:S(2)}, u32[]{:S(2)}) collective-permute-start(bf16[1,72,384]{2,1,0:T(8,128)(2,1)S(1)} %get-tuple-element.33), channel_id=1, source_target_pairs={{8,16},{16,8},{9,17},{17,9},{10,18},{18,10},{11,19},{19,11},{12,20... | collective-permute-start | bytes 165896 | tf_op jit(solution)/shard_map/ppermute | solution.py:299
  71.5 0.9 %copy-start.2 = (f32[8,32,32]{2,1,0:T(8,128)S(1)}, f32[8,32,32]{2,1,0:T(8,128)}, u32[]{:S(2)}) copy-start(f32[8,32,32]{2,1,0:T(8,128)} %get-tuple-element.12.residual_ref) | copy-start | bytes 98308
where the time goes:
time: 74.2 us; the launch traced here: 73.8 us
  blocking collectives  29.2 us (39%)
  Pallas kernels  16.9 us (23%)
  waiting for transfers between devices  13.4 us (18%)
  starting transfers between devices  9.31 us (13%)
  local copies, waits for them, and re-layouts  4.09 us (6%)
  between operations  0.8 us (1%)
    all_to_all x1, blocking collectives, on_device(): lax.all_to_all(terms.reshape(tiles * fq_blocks, sensors, block), ALL_AXES...  19.7 us
    all_to_all x1, waiting for transfers between devices, on_device(): lax.all_to_all(spec.reshape(tiles * fq_blocks, sensors, block), ALL_AXES,...  9.91 us
    all_to_all x1, blocking collectives, on_device(): lax.all_to_all(jnp.broadcast_to(norm[None], (tiles, cols, 128)), GRID_AXE...  9.47 us
    all_to_all x1, starting transfers between devices, on_device(): lax.all_to_all(spec.reshape(tiles * fq_blocks, sensors, block), ALL_AXES,...  7.3 us
    pallas_call x1, Pallas kernels, on_device(): pl.pallas_call(functools.partial(adjoint_kernel, local_freqs, cols), grid...  7.13 us
    pallas_call x1, Pallas kernels, on_device(): pl.pallas_call(functools.partial(field_kernel, local_freqs, cols), grid=(...  5.62 us
    unnamed x25, local copies, waits for them, and re-layouts  4.09 us
    ppermute x2, waiting for transfers between devices, swap(): first = lax.ppermute(toward_partner, axis, near)  3.51 us
  transfers between devices with their start and end apart: 5, of which 3 were waited for; matrix products, arithmetic and copies ran while one was open for 1% of the time, Pallas kernels for 0%

commit v1 on v0

v1 whole, which is shorter than its diff:
```python
import functools
import math

import jax
import jax.numpy as jnp
from jax import lax
from jax.experimental import pallas as pl
from jax.experimental.pallas import tpu as pltpu
from jax.sharding import PartitionSpec as P
import numpy as np

SWEEPS = 4
DEPTH = SWEEPS - 1
HIGHEST = lax.Precision.HIGHEST
F32 = jnp.float32
BF16 = jnp.bfloat16
GRID_AXES = ("sx", "sy")
ALL_AXES = ("sx", "sy", "fq")
LANES = 128
MIB = 1024 * 1024
VMEM = pl.BlockSpec(memory_space=pltpu.VMEM)
SMEM = pl.BlockSpec(memory_space=pltpu.SMEM)
HBM = pl.BlockSpec(memory_space=pltpu.HBM)


def params(mib=24):
    return pltpu.CompilerParams(vmem_limit_bytes=mib * MIB)


def tables(freq_count, local_freqs, local_cols, time_steps):
    freq = np.arange(freq_count)[:, None]
    step = np.arange(time_steps)[None, :]
    phases = (freq * step % time_steps) * (2.0 * math.pi / time_steps)
    factor = 1.0 / math.sqrt(time_steps)
    pair = np.stack([np.cos(phases) * factor, -np.sin(phases) * factor], 1)
    forward = np.repeat(pair.reshape(2 * freq_count, time_steps), local_cols, 0)
    doubling = np.where(np.arange(freq_count) == 0, 1.0, 2.0)[:, None, None]
    inverse = np.repeat((pair * doubling).reshape(2 * freq_count, time_steps), local_cols, 0)
    return forward.T.astype(np.float32), inverse.astype(np.float32)


def by_side(axis, low, high):
    even = lax.axis_index(axis) % 2 == 0
    return jnp.where(even, high, low), jnp.where(even, low, high)


def lane_ids(lanes):
    return lax.broadcasted_iota(jnp.int32, (1, lanes), 1)


def fetch_all(pairs, sems):
    copies = [pltpu.make_async_copy(a, b, sems.at[i]) for i, (a, b) in enumerate(pairs)]
    for copy in copies:
        copy.start()
    for copy in copies:
        copy.wait()


def spectrum_kernel(
    tiles, fq_blocks, direction_in, noise_in, table_in, out_ref, direction_ref, noise_ref, table_ref, sems
):
    fetch_all(
        ((direction_in, direction_ref), (noise_in, noise_ref), (table_in, table_ref)), sems
    )
    cols, sensors, steps = direction_ref.shape
    lanes = table_ref.shape[1]
    weighted = (noise_ref[...][None] * direction_ref[...]).reshape(cols * sensors, steps)
    full = jnp.dot(weighted, table_ref[...], precision=HIGHEST, preferred_element_type=F32)
    col_of = lane_ids(lanes) % cols
    spec = full[0:sensors]
    for col in range(1, cols):
        spec = jnp.where(col_of == col, full[col * sensors : (col + 1) * sensors], spec)
    spec = spec.astype(BF16)
    block = lanes // fq_blocks
    for b in range(fq_blocks):
        part = spec[:, b * block : (b + 1) * block]
        out_ref[:, b] = jnp.broadcast_to(part[None], (tiles, sensors, block))


def class_rows(class_ref):
    cells_y, cells_x = class_ref.shape
    cells = cells_x * cells_y
    row = lax.broadcasted_iota(jnp.int32, (cells, cells_x), 0)
    pick = (row // cells_y == lax.broadcasted_iota(jnp.int32, (cells, cells_x), 1)).astype(F32)
    by_row = lax.dot_general(
        pick,
        class_ref[...].astype(F32) + 1.0,
        (((1,), (1,)), ((), ())),
        preferred_element_type=F32,
    )
    at = lax.broadcasted_iota(jnp.int32, (cells, cells_y), 0) % cells_y
    own = (at == lax.broadcasted_iota(jnp.int32, (cells, cells_y), 1)).astype(F32)
    return jnp.dot(by_row * own, jnp.ones((cells_y, LANES), F32), preferred_element_type=F32)


def adjoint_kernel(
    freqs, cols, spectra_ref, spec_ref, class_ref, out_ref, near_ref, far_ref, ends_ref
):
    _, _, cells_x, cells_y, all_sensors = spectra_ref.shape
    cells = cells_x * cells_y
    stride = out_ref.shape[1] // cells_x
    lanes = spec_ref.shape[1] * spec_ref.shape[3]

    parts = [
        spec_ref[:, b].reshape(all_sensors, spec_ref.shape[3]) for b in range(spec_ref.shape[1])
    ]
    direct = jnp.concatenate(parts, axis=1)
    wide = direct.astype(F32)
    is_real = (lane_ids(lanes) // cols) % 2 == 0
    turned = jnp.where(
        is_real, pltpu.roll(wide, lanes - cols, 1), -pltpu.roll(wide, cols, 1)
    ).astype(BF16)
    stacked = jnp.concatenate([direct, turned], axis=0)
    freq_of = (lane_ids(lanes) // (2 * cols)) % freqs

    classes = class_rows(class_ref)
    acc = None
    for f in range(freqs):
        both = spectra_ref[f].reshape(2, cells, all_sensors)
        both = jnp.concatenate([both[0], both[1]], axis=1)
        got = jnp.dot(both, stacked, preferred_element_type=F32)
        acc = got if acc is None else jnp.where(freq_of == f, got, acc)
    for k in range(out_ref.shape[0]):
        part = classes if k * LANES == lanes else acc[:, k * LANES : (k + 1) * LANES]
        for x in range(cells_x):
            base = x * stride
            out_ref[k, base : base + cells_y] = part[x * cells_y : (x + 1) * cells_y]
            out_ref[k, base + cells_y : base + stride] = jnp.zeros((stride - cells_y, LANES), F32)
        at = slice(k * LANES, (k + 1) * LANES)
        for j in range(DEPTH):
            low = out_ref[k, pl.ds(j, cells_x, stride=stride), :]
            high = out_ref[k, pl.ds(cells_y - DEPTH + j, cells_x, stride=stride), :]
            near, far = by_side("sy", low, high)
            near_ref[j * cells_x : (j + 1) * cells_x, at] = near.astype(BF16)
            far_ref[j * cells_x : (j + 1) * cells_x, at] = far.astype(BF16)
        ends_ref[0, :, at] = out_ref[k, 0 : DEPTH * stride]
        ends_ref[1, :, at] = out_ref[k, (cells_x - DEPTH) * stride : cells_x * stride]


def ends_kernel(ends_ref, near_ref, far_ref, near_out, far_out, held):
    span = ends_ref.shape[1]
    stride = span // DEPTH
    cells_x = near_ref.shape[0] // DEPTH
    cells_y = stride - 8
    after, before = by_side("sy", far_ref[...].astype(F32), near_ref[...].astype(F32))
    built = []
    for side in range(2):
        held[...] = jnp.zeros_like(held)
        held[8 : 8 + span] = ends_ref[side]
        first = 0 if side == 0 else cells_x - DEPTH
        for x in range(DEPTH):
            for j in range(DEPTH):
                take = j * cells_x + first + x
                to = 8 + x * stride
                held[to + cells_y + j : to + cells_y + j + 1] = after[take : take + 1]
                held[to - DEPTH + j : to - DEPTH + j + 1] = before[take : take + 1]
        built.append(held[8 - DEPTH : 8 - DEPTH + span])
    near, far = by_side("sx", built[0], built[1])
    near_out[...] = near.astype(BF16)
    far_out[...] = far.astype(BF16)


def field_kernel(
    freqs,
    cols,
    spectra_ref,
    source_ref,
    near_y_ref,
    far_y_ref,
    near_x_ref,
    far_x_ref,
    kappa_ref,
    out_ref,
    wide,
    gain,
    one,
    two,
    sums,
):
    _, _, cells_x, cells_y, all_sensors = spectra_ref.shape
    cells = cells_x * cells_y
    stride = source_ref.shape[1] // cells_x
    slabs = one.shape[0]
    lanes = slabs * LANES
    start = (DEPTH + 1) * stride
    rows = cells_x * stride
    span = DEPTH * stride

    total = wide.shape[1]
    lo, hi = start - span - 8, start + rows + span
    for k in range(slabs + 1):
        at = slice(k * LANES, (k + 1) * LANES)
        wide[k, 0:start] = jnp.zeros((start, LANES), F32)
        wide[k, start + rows : total] = jnp.zeros((total - start - rows, LANES), F32)
        wide[k, start : start + rows] = source_ref[k]
        after, before = by_side("sy", far_y_ref[:, at].astype(F32), near_y_ref[:, at].astype(F32))
        below, above = by_side("sx", far_x_ref[:, at].astype(F32), near_x_ref[:, at].astype(F32))
        for j in range(DEPTH):
            part = slice(j * cells_x, (j + 1) * cells_x)
            wide[k, pl.ds(start + cells_y + j, cells_x, stride=stride), :] = after[part]
            wide[k, pl.ds(start - DEPTH + j, cells_x, stride=stride), :] = before[part]
        wide[k, start - span - DEPTH : start - DEPTH] = above
        wide[k, start + rows - DEPTH : start + rows + span - DEPTH] = below

    classes = wide[slabs, lo:hi]
    kappa = jnp.zeros_like(classes)
    for n in range(kappa_ref.shape[0]):
        kappa = jnp.where(classes == n + 1.0, kappa_ref[n], kappa)
    scale = jnp.where(classes > 0.0, 1.0 / (1.0 + 4.0 * kappa), 0.0)
    gain[lo:hi] = kappa * scale

    def sweep(k, old, new, margin):
        first = start - margin * stride - 8
        last = start + rows + margin * stride
        near = (
            old[k, first - stride : last - stride]
            + old[k, first + stride : last + stride]
            + old[k, first - 1 : last - 1]
            + old[k, first + 1 : last + 1]
        )
        new[k, first:last] = wide[k, first:last] + gain[first:last] * near

    turned = []
    for k in range(slabs):
        wide[k, lo:hi] = wide[k, lo:hi] * scale
        one[k] = wide[k]
        old, new = one, two
        for margin in range(DEPTH - 1, -1, -1):
            sweep(k, old, new, margin)
            old, new = new, old
        field = old[k, start : start + rows].reshape(cells_x, stride, LANES)[:, 0:cells_y]
        turned.append(field.reshape(cells, LANES).T)
    turned = jnp.concatenate(turned, axis=0)
    blocks = lanes // (2 * cols)
    pair = turned.reshape(blocks, 2, cols, cells)
    plain = pair.astype(BF16).reshape(blocks, 2 * cols, cells)
    crossed = jnp.stack([-pair[:, 1], pair[:, 0]], axis=1)
    crossed = crossed.astype(BF16).reshape(blocks, 2 * cols, cells)
    groups = blocks // freqs
    for f in range(freqs):
        ours = [
            jnp.concatenate([plain[g * freqs + f], crossed[g * freqs + f]], axis=1)
            for g in range(groups)
        ]
        left = jnp.concatenate(ours, axis=0)
        got = jnp.dot(
            left, spectra_ref[f].reshape(2 * cells, all_sensors), preferred_element_type=F32
        )
        for g in range(groups):
            at = (g * freqs + f) * 2 * cols
            sums[at : at + 2 * cols] = got[g * 2 * cols : (g + 1) * 2 * cols]
    back = sums[...].T.astype(BF16)
    tiles, _, sensors, block = out_ref.shape
    for g in range(groups):
        out_ref[:, g] = back[:, g * block : (g + 1) * block].reshape(tiles, sensors, block)


def solution_kernel(solution_in, direction_in, step_ref, out_ref, solution_ref, direction_ref, sems):
    fetch_all(((solution_in, solution_ref), (direction_in, direction_ref)), sems)
    for c in range(solution_ref.shape[0]):
        out_ref[c] = solution_ref[c] + step_ref[c] * direction_ref[c]


def residual_kernel(
    terms_ref, table_ref, noise_ref, residual_ref, direction_ref, step_ref, new_residual_ref, norm_ref
):
    cols, sensors, steps = direction_ref.shape
    parts = []
    for b in range(terms_ref.shape[1]):
        parts.append(jnp.sum(terms_ref[:, b].astype(F32), axis=0))
    spectrum = jnp.concatenate(parts, axis=1)
    col_of = lane_ids(spectrum.shape[1]) % cols
    left = jnp.concatenate([jnp.where(col_of == c, spectrum, 0.0) for c in range(cols)], axis=0)
    returned = jnp.dot(left, table_ref[...], precision=HIGHEST, preferred_element_type=F32)
    for c in range(cols):
        product = direction_ref[c] + noise_ref[...] * returned[c * sensors : (c + 1) * sensors]
        new_residual = residual_ref[c] - step_ref[c] * product
        new_residual_ref[c] = new_residual
        norm = jnp.sum(
            jnp.sum(new_residual * new_residual, axis=0, keepdims=True), axis=1, keepdims=True
        )
        norm_ref[:, c : c + 1] = jnp.broadcast_to(norm[None], (norm_ref.shape[0], 1, LANES))


def direction_kernel(
    norms_ref, residual_ref, direction_ref, old_ref, residual_out, direction_out, norm_ref, held, sems
):
    cols, sensors, steps = direction_ref.shape
    first = pltpu.make_async_copy(residual_ref, residual_out, sems.at[0])
    first.start()
    norm = jnp.sum(norms_ref[...], axis=0)
    for c in range(cols):
        held[c] = residual_ref[c] + (norm[c : c + 1, 0:1] / old_ref[c]) * direction_ref[c]
    second = pltpu.make_async_copy(held, direction_out, sems.at[1])
    second.start()
    for c in range(cols):
        norm_ref[c] = jnp.max(norm[c : c + 1])
    first.wait()
    second.wait()


def swap(axis, toward_partner, toward_other):
    count = lax.axis_size(axis)
    near = [(i, i ^ 1) for i in range(count) if (i ^ 1) < count]
    far = [(i, i + 1 if i % 2 else i - 1) for i in range(1, count - 1 + count % 2)]
    second = lax.ppermute(toward_other, axis, far)
    first = lax.ppermute(toward_partner, axis, near)
    return first, second


def on_device(
    spectra,
    noise_weight,
    class_map,
    class_kappa,
    solution,
    residual,
    direction,
    step_length,
    old_norm,
):
    local_freqs, _, cells_x, cells_y, all_sensors = spectra.shape
    cols, sensors, steps = direction.shape
    fq_blocks = lax.axis_size("fq")
    tiles = lax.axis_size("sx") * lax.axis_size("sy")
    block = 2 * local_freqs * cols
    lanes = block * fq_blocks
    forward, inverse = tables(local_freqs * fq_blocks, local_freqs, cols, steps)
    group = 2 if fq_blocks % 2 == 0 else 1
    chunks = fq_blocks // group
    width = group * block
    stride = cells_y + 8
    wide = width + LANES
    cells = cells_x * cells_y

    like = jax.ShapeDtypeStruct(direction.shape, F32)
    held = pltpu.VMEM(direction.shape, F32)
    spec = pl.pallas_call(
        functools.partial(spectrum_kernel, tiles, fq_blocks),
        out_shape=jax.ShapeDtypeStruct((tiles, fq_blocks, sensors, block), BF16),
        in_specs=[HBM] * 3,
        out_specs=VMEM,
        scratch_shapes=[
            held,
            pltpu.VMEM(noise_weight.shape, F32),
            pltpu.VMEM(forward.shape, F32),
            pltpu.SemaphoreType.DMA((3,)),
        ],
        compiler_params=params(62),
        cost_estimate=pl.CostEstimate(
            flops=2 * spectra.size, bytes_accessed=4 * spectra.size, transcendentals=0
        ),
        name="spectrum",
    )(direction, noise_weight, forward)
    spec = lax.all_to_all(
        spec.reshape(tiles * fq_blocks, sensors, block), ALL_AXES, 0, 0, tiled=True
    ).reshape(tiles, fq_blocks, sensors, block)
    new_solution = pl.pallas_call(
        solution_kernel,
        out_shape=like,
        in_specs=[HBM, HBM, SMEM],
        out_specs=VMEM,
        scratch_shapes=[held, held, pltpu.SemaphoreType.DMA((2,))],
        compiler_params=params(),
        name="solution",
    )(solution, direction, step_length)

    edge = jax.ShapeDtypeStruct((DEPTH * cells_x, wide), BF16)
    end = jax.ShapeDtypeStruct((DEPTH * stride, wide), BF16)
    total = (cells_x + 2 * DEPTH + 2) * stride
    slabs = width // LANES
    pieces = []
    for i in range(chunks):
        source, near_y, far_y, ends = pl.pallas_call(
            functools.partial(adjoint_kernel, local_freqs, cols),
            out_shape=(
                jax.ShapeDtypeStruct((slabs + 1, cells_x * stride, LANES), F32),
                edge,
                edge,
                jax.ShapeDtypeStruct((2, DEPTH * stride, wide), F32),
            ),
            in_specs=[VMEM] * 3,
            out_specs=(VMEM,) * 4,
            compiler_params=params(),
            name="adjoint",
        )(spectra, spec[:, i * group : (i + 1) * group], class_map.T)
        near_y, far_y = swap("sy", near_y, far_y)
        near_x, far_x = pl.pallas_call(
            ends_kernel,
            out_shape=(end, end),
            in_specs=[VMEM] * 3,
            out_specs=(VMEM,) * 2,
            scratch_shapes=[pltpu.VMEM((DEPTH * stride + 16, wide), F32)],
            compiler_params=params(),
            name="ends",
        )(ends, near_y, far_y)
        near_x, far_x = swap("sx", near_x, far_x)
        pieces.append(
            pl.pallas_call(
                functools.partial(field_kernel, local_freqs, cols),
                out_shape=jax.ShapeDtypeStruct((tiles, group, sensors, block), BF16),
                in_specs=[VMEM] * 6 + [SMEM],
                out_specs=VMEM,
                scratch_shapes=[
                    pltpu.VMEM((slabs + 1, total, LANES), F32),
                    pltpu.VMEM((total, LANES), F32),
                    pltpu.VMEM((slabs, total, LANES), F32),
                    pltpu.VMEM((slabs, total, LANES), F32),
                    pltpu.VMEM((width, all_sensors), F32),
                ],
                compiler_params=params(),
                name="field",
            )(spectra, source, near_y, far_y, near_x, far_x, class_kappa)
        )
    terms = jnp.concatenate(pieces, axis=1)
    terms = lax.all_to_all(
        terms.reshape(tiles * fq_blocks, sensors, block), ALL_AXES, 0, 0, tiled=True
    ).reshape(tiles, fq_blocks, sensors, block)
    new_residual, norms = pl.pallas_call(
        residual_kernel,
        out_shape=(like, jax.ShapeDtypeStruct((tiles, cols, LANES), F32)),
        in_specs=[VMEM] * 5 + [SMEM],
        out_specs=(VMEM,) * 2,
        compiler_params=params(),
        name="residual",
    )(terms, inverse, noise_weight, residual, direction, step_length)
    norms = lax.all_to_all(norms, GRID_AXES, 0, 0, tiled=True)
    new_residual, new_direction, new_norm = pl.pallas_call(
        direction_kernel,
        out_shape=(like, like, jax.ShapeDtypeStruct((cols,), F32)),
        in_specs=[VMEM] * 3 + [SMEM],
        out_specs=(HBM, HBM, SMEM),
        scratch_shapes=[held, pltpu.SemaphoreType.DMA((2,))],
        compiler_params=params(),
        name="direction",
    )(norms, new_residual, direction, old_norm)
    return (new_solution, new_residual, new_direction, new_norm)


def solution(mesh):
    return jax.shard_map(
        on_device,
        mesh=mesh,
        in_specs=(
            P("fq", None, "sx", "sy", None),
            P(("sx", "sy"), None),
            P("sx", "sy"),
            P(),
            P("fq", ("sx", "sy"), None),
            P("fq", ("sx", "sy"), None),
            P("fq", ("sx", "sy"), None),
            P("fq"),
            P("fq"),
        ),
        out_specs=(
            P("fq", ("sx", "sy"), None),
            P("fq", ("sx", "sy"), None),
            P("fq", ("sx", "sy"), None),
            P("fq"),
        ),
        check_vma=False,
    )
```

time: 74.2 us -> 70.6 us (0.951)
  blocking collectives: 29.2 us -> 37.7 us
  waiting for transfers between devices: 13.4 us -> 8.8 us
  starting transfers between devices: 9.31 us -> 5.51 us
  Pallas kernels: 16.9 us -> 13.3 us
    all_to_all x1, blocking collectives: 9.47 us -> 18 us  [on_device(): lax.all_to_all(spec.reshape(tiles * fq_blocks, sensors, block), ALL_AXES,...]
    all_to_all x1, waiting for transfers between devices: 9.91 us -> 5.27 us  [on_device(): norms = lax.all_to_all(norms, GRID_AXES, 0, 0, tiled=True)]
    pallas_call x5 -> x6, Pallas kernels: 15.8 us -> 11.3 us  [the longest x1 3.63 us: on_device(): pl.pallas_call(functools.partial(field_kernel, local_freqs, cols), out_sh...]
    all_to_all x1, starting transfers between devices: 7.3 us -> 3.5 us  [on_device(): norms = lax.all_to_all(norms, GRID_AXES, 0, 0, tiled=True)]
    pallas_call x1, Pallas kernels: 1.08 us -> 2.02 us  [on_device(): pl.pallas_call(functools.partial(spectrum_kernel, tiles, fq_blocks), out_...]
    unnamed x25 -> x22, local copies, waits for them, and re-layouts: 4.09 us -> 4.12 us
  transfers between devices with their start and end apart: 5 -> 5, of which waited for: 3 -> 3; matrix products, arithmetic and copies ran while one was open for 1% -> 0% of each run, Pallas kernels for 0% -> 2%
where the time goes in v1:
time: 70.6 us; the launch traced here: 70.2 us
  blocking collectives  37.7 us (53%)
  Pallas kernels  13.3 us (19%)
  waiting for transfers between devices  8.8 us (12%)
  starting transfers between devices  5.51 us (8%)
  local copies, waits for them, and re-layouts  4.12 us (6%)
  between operations  0.77 us (1%)
    all_to_all x1, blocking collectives, on_device(): lax.all_to_all(terms.reshape(tiles * fq_blocks, sensors, block), ALL_AXES...  19.7 us
    all_to_all x1, blocking collectives, on_device(): lax.all_to_all(spec.reshape(tiles * fq_blocks, sensors, block), ALL_AXES,...  18 us
    all_to_all x1, waiting for transfers between devices, on_device(): norms = lax.all_to_all(norms, GRID_AXES, 0, 0, tiled=True)  5.27 us
    unnamed x22, local copies, waits for them, and re-layouts  4.12 us
    pallas_call x1, Pallas kernels, on_device(): pl.pallas_call(functools.partial(field_kernel, local_freqs, cols), out_sh...  3.63 us
    ppermute x2, waiting for transfers between devices, swap(): first = lax.ppermute(toward_partner, axis, near)  3.53 us
    all_to_all x1, starting transfers between devices, on_device(): norms = lax.all_to_all(norms, GRID_AXES, 0, 0, tiled=True)  3.5 us
    pallas_call x1, Pallas kernels, on_device(): pl.pallas_call(functools.partial(adjoint_kernel, local_freqs, cols), out_...  2.5 us
  transfers between devices with their start and end apart: 5, of which 3 were waited for; matrix products, arithmetic and copies ran while one was open for 0% of the time, Pallas kernels for 2%

profile of v1, /device:TPU:0, one launch (start us, length us, event | category | flops | bytes accessed | tf_op | source)
XLA Modules:
  0.0 70.2 jit_solution(2820736355105729842)
XLA Ops:
  0.6 0.0 copy-start.9
  0.6 2.0 %spectrum.1 = bf16[16,2,32,128]{3,2,1,0:T(8,128)(2,1)} custom-call(f32[8,32,32]{2,1,0:T(8,128)} %direction_ref.3, f32[32,32]{1,0:T(8,128)} %noise_ref.1, f32[32,256]{1,0:T(8,128)} %constant.4.clone.table_in), custom_call_target="tpu_custom_call" | custom-call | flops 8388608 | bytes 16777216 | tf_op jit(solution)/shard_map/spectrum/pallas_call | solution.py:338
  2.7 18.0 %all_to_all.15 = bf16[32,32,128]{2,1,0:T(8,128)(2,1)S(1)} all-to-all(bf16[32,32,128]{2,1,0:T(8,128)(2,1)} %bitcast.9), channel_id=1, replica_groups=mesh['sx'=4,'sy'=4,'fq'=2] {'sx','sy','fq'}, dimensions={0} | all-to-all | bytes 524288 | tf_op jit(solution)/shard_map/all_to_all | solution.py:355
  20.7 0.0 copy-start
  20.7 3.4 %copy-done = bf16[8,2,32,16,512]{4,3,2,1,0:T(8,128)(2,1)S(1)} copy-done((bf16[8,2,32,16,512]{4,3,2,1,0:T(8,128)(2,1)S(1)}, bf16[8,2,32,16,512]{4,3,2,1,0:T(8,128)(2,1)}, u32[]{:S(2)}) %copy-start) | copy-done | bytes 8388632
  24.1 0.0 copy-start.7
  24.1 0.7 copy-done.7
  24.8 0.0 copy-start.1
  24.8 0.0 copy-start.2
  24.8 0.0 copy-start.4
  24.8 0.0 copy-start.5
  24.8 0.0 copy-start.6
  24.8 0.0 copy-start.8
  24.8 0.0 copy-start.3
  24.8 0.0 copy-start.10
  24.8 2.5 %adjoint.1 = (f32[3,768,128]{2,1,0:T(8,128)S(1)}, bf16[96,384]{1,0:T(8,128)(2,1)S(1)}, bf16[96,384]{1,0:T(8,128)(2,1)S(1)}, f32[2,72,384]{2,1,0:T(8,128)S(1)}) custom-call(bf16[8,2,32,16,512]{4,3,2,1,0:T(8,128)(2,1)S(1)} %copy-done, bf16[16,2,32,128]{3,2,1,0:T(8,128)(2,1)S(1)} %bitcast.5, s32[16,32]{1,0:T(8,128)S(1)} %bitcast.8), custom_call_target="tpu_custom_call" | custom-call | tf_op jit(solution)/shard_map/adjoint/pallas_call | solution.py:374
  27.3 0.2 collective-permute-start
  27.5 0.7 collective-permute-start.1
  28.2 0.5 collective-permute-done.near_ref.near_y_ref
  28.6 0.0 collective-permute-done.1.far_ref.far_y_ref
  28.6 0.1 ends.1
  28.8 0.5 collective-permute-start.2
  29.3 0.7 collective-permute-start.3
  29.9 3.0 %collective-permute-done.2.near_x_ref = bf16[72,384]{1,0:T(8,128)(2,1)S(1)} collective-permute-done((bf16[72,384]{1,0:T(8,128)(2,1)S(1)}, bf16[72,384]{1,0:T(8,128)(2,1)S(1)}, u32[]{:S(2)}, u32[]{:S(2)}) %collective-permute-start.2) | collective-permute-done | bytes 55328 | tf_op jit(solution)/shard_map/ppermute | solution.py:307
  33.0 0.0 collective-permute-done.3.far_x_ref
  33.0 0.0 copy-done.9
  33.0 0.0 copy-done.1
  33.0 3.6 %field.1 = bf16[16,2,32,128]{3,2,1,0:T(8,128)(2,1)S(1)} custom-call(bf16[8,2,32,16,512]{4,3,2,1,0:T(8,128)(2,1)S(1)} %copy-done.1, f32[3,768,128]{2,1,0:T(8,128)S(1)} %get-tuple-element.15.source_ref, bf16[96,384]{1,0:T(8,128)(2,1)S(1)} %collective-permute-done.near_ref.near_y_ref, bf16[96,384]{1,0:T(8,128)(2,1)S(1)} %collective-permute-done.1.far_ref.far_y_ref, ...), custom_call_target="tpu_custom_call" | custom-call | tf_op jit(solution)/shard_map/field/pallas_call | solution.py:399
  36.6 19.7 %all_to_all.16 = bf16[32,32,128]{2,1,0:T(8,128)(2,1)S(1)} all-to-all(bf16[32,32,128]{2,1,0:T(8,128)(2,1)S(1)} %bitcast.6), channel_id=1, replica_groups=mesh['sx'=4,'sy'=4,'fq'=2] {'sx','sy','fq'}, dimensions={0} | all-to-all | bytes 524288 | tf_op jit(solution)/shard_map/all_to_all | solution.py:416
  56.3 0.0 copy-done.2
  56.3 0.0 copy-done.4
  56.3 0.0 copy-done.5
  56.3 0.0 copy-done.6
  56.4 0.0 copy-done.8
  56.4 1.7 %residual.1 = (f32[8,32,32]{2,1,0:T(8,128)S(1)}, f32[16,8,128]{2,1,0:T(8,128)}) custom-call(bf16[16,2,32,128]{3,2,1,0:T(8,128)(2,1)S(1)} %bitcast.7, f32[256,32]{1,0:T(8,128)S(1)} %copy-done.5, f32[32,32]{1,0:T(8,128)S(1)} %copy-done.6, f32[8,32,32]{2,1,0:T(8,128)S(1)} %copy-done.4, f32[8,32,32]{2,1,0:T(8,128)S(1)} %copy-done.2, f32[8]{0:T(128)S(1)} %copy-done.8), custom_call_target="tpu_custom_call" | custom-call | tf_op jit(solution)/shard_map/residual/pallas_call | solution.py:419
  58.0 3.5 %all-to-all-start.2 = ((f32[16,8,128]{2,1,0:T(8,128)}), f32[16,8,128]{2,1,0:T(8,128)S(1)}, u32[]{:S(2)}, u32[]{:S(2)}) async-start(f32[16,8,128]{2,1,0:T(8,128)} %get-tuple-element.21), calls=%async_computation.2 | async-start | bytes 131072 | tf_op jit(solution)/shard_map/all_to_all | solution.py:427
  61.5 0.0 copy-done.3
  61.5 1.6 %solution.1 = f32[8,32,32]{2,1,0:T(8,128)} custom-call(f32[8,32,32]{2,1,0:T(8,128)S(1)} %copy-done.3, f32[8,32,32]{2,1,0:T(8,128)S(1)} %copy-done.2, f32[8]{0:T(128)S(1)} %copy-done.8), custom_call_target="tpu_custom_call" | custom-call | tf_op jit(solution)/shard_map/solution/pallas_call | solution.py:358
  63.1 5.3 %all-to-all-done.2.norms_ref = f32[16,8,128]{2,1,0:T(8,128)S(1)} async-done(((f32[16,8,128]{2,1,0:T(8,128)}), f32[16,8,128]{2,1,0:T(8,128)S(1)}, u32[]{:S(2)}, u32[]{:S(2)}) %all-to-all-start.2) | async-done | bytes 65568 | tf_op jit(solution)/shard_map/all_to_all | solution.py:427
  68.4 0.0 copy-done.10
  68.4 1.8 %direction.1 = (f32[8,32,32]{2,1,0:T(8,128)}, f32[8,32,32]{2,1,0:T(8,128)}, f32[8]{0:T(128)}) custom-call(f32[16,8,128]{2,1,0:T(8,128)S(1)} %all-to-all-done.2.norms_ref, f32[8,32,32]{2,1,0:T(8,128)S(1)} %get-tuple-element.22.residual_ref, f32[8,32,32]{2,1,0:T(8,128)S(1)} %copy-done.2, f32[8]{0:T(128)S(1)} %copy-done.10), custom_call_target="tpu_custom_call" | custom-call | tf_op jit(solution)/shard_map/direction/pallas_call | solution.py:428
Async XLA Ops:
  0.6 32.4 %copy-start.9 = (f32[8]{0:T(128)S(1)}, f32[8]{0:T(128)}, u32[]{:S(2)}) copy-start(f32[8]{0:T(128)} %kappa_ref.1) | copy-start | bytes 100
  20.7 3.4 %copy-start = (bf16[8,2,32,16,512]{4,3,2,1,0:T(8,128)(2,1)S(1)}, bf16[8,2,32,16,512]{4,3,2,1,0:T(8,128)(2,1)}, u32[]{:S(2)}) copy-start(bf16[8,2,32,16,512]{4,3,2,1,0:T(8,128)(2,1)} %spectra_ref.3) | copy-start | bytes 25165828
  24.1 0.7 copy-start.7
  24.8 8.2 %copy-start.1 = (bf16[8,2,32,16,512]{4,3,2,1,0:T(8,128)(2,1)S(1)}, bf16[8,2,32,16,512]{4,3,2,1,0:T(8,128)(2,1)}, u32[]{:S(2)}) copy-start(bf16[8,2,32,16,512]{4,3,2,1,0:T(8,128)(2,1)} %spectra_ref.3) | copy-start | bytes 25165828
  24.8 31.6 %copy-start.2 = (f32[8,32,32]{2,1,0:T(8,128)S(1)}, f32[8,32,32]{2,1,0:T(8,128)}, u32[]{:S(2)}) copy-start(f32[8,32,32]{2,1,0:T(8,128)} %direction_ref.3) | copy-start | bytes 98308
  24.8 31.6 %copy-start.4 = (f32[8,32,32]{2,1,0:T(8,128)S(1)}, f32[8,32,32]{2,1,0:T(8,128)}, u32[]{:S(2)}) copy-start(f32[8,32,32]{2,1,0:T(8,128)} %residual_ref.1) | copy-start | bytes 98308
  24.8 31.6 %copy-start.5 = (f32[256,32]{1,0:T(8,128)S(1)}, f32[256,32]{1,0:T(8,128)}, u32[]{:S(2)}) copy-start(f32[256,32]{1,0:T(8,128)} %constant.5.clone.table_ref) | copy-start | bytes 98308
  24.8 31.6 %copy-start.6 = (f32[32,32]{1,0:T(8,128)S(1)}, f32[32,32]{1,0:T(8,128)}, u32[]{:S(2)}) copy-start(f32[32,32]{1,0:T(8,128)} %noise_ref.1) | copy-start | bytes 12292
  24.8 31.6 %copy-start.8 = (f32[8]{0:T(128)S(1)}, f32[8]{0:T(128)}, u32[]{:S(2)}) copy-start(f32[8]{0:T(128)} %step_ref.3) | copy-start | bytes 100
  24.8 36.7 %copy-start.3 = (f32[8,32,32]{2,1,0:T(8,128)S(1)}, f32[8,32,32]{2,1,0:T(8,128)}, u32[]{:S(2)}) copy-start(f32[8,32,32]{2,1,0:T(8,128)} %solution_in.1) | copy-start | bytes 98308
  24.8 43.6 %copy-start.10 = (f32[8]{0:T(128)S(1)}, f32[8]{0:T(128)}, u32[]{:S(2)}) copy-start(f32[8]{0:T(128)} %old_ref.1) | copy-start | bytes 100
  27.3 1.3 %collective-permute-start = (bf16[96,384]{1,0:T(8,128)(2,1)S(1)}, bf16[96,384]{1,0:T(8,128)(2,1)S(1)}, u32[]{:S(2)}, u32[]{:S(2)}) collective-permute-start(bf16[96,384]{1,0:T(8,128)(2,1)S(1)} %get-tuple-element.16), channel_id=1, source_target_pairs={{0,2},{2,0},{4,6},{6,4},{1,3},{3,1},{5,7},{7,5},{8,10},{10,8},{12,... | collective-permute-start | bytes 221192 | tf_op jit(solution)/shard_map/ppermute | solution.py:307
  27.5 1.2 %collective-permute-start.1 = (bf16[96,384]{1,0:T(8,128)(2,1)S(1)}, bf16[96,384]{1,0:T(8,128)(2,1)S(1)}, u32[]{:S(2)}, u32[]{:S(2)}) collective-permute-start(bf16[96,384]{1,0:T(8,128)(2,1)S(1)} %get-tuple-element.17), channel_id=1, source_target_pairs={{2,4},{4,2},{3,5},{5,3},{10,12},{12,10},{11,13},{13,11},{18,20},{2... | collective-permute-start | bytes 221192 | tf_op jit(solution)/shard_map/ppermute | solution.py:306
  28.8 4.2 %collective-permute-start.2 = (bf16[72,384]{1,0:T(8,128)(2,1)S(1)}, bf16[72,384]{1,0:T(8,128)(2,1)S(1)}, u32[]{:S(2)}, u32[]{:S(2)}) collective-permute-start(bf16[72,384]{1,0:T(8,128)(2,1)S(1)} %get-tuple-element.19), channel_id=1, source_target_pairs={{0,8},{8,0},{16,24},{24,16},{1,9},{9,1},{17,25},{25,17},{2,10},{10... | collective-permute-start | bytes 165896 | tf_op jit(solution)/shard_map/ppermute | solution.py:307
  29.3 3.7 %collective-permute-start.3 = (bf16[72,384]{1,0:T(8,128)(2,1)S(1)}, bf16[72,384]{1,0:T(8,128)(2,1)S(1)}, u32[]{:S(2)}, u32[]{:S(2)}) collective-permute-start(bf16[72,384]{1,0:T(8,128)(2,1)S(1)} %get-tuple-element.20), channel_id=1, source_target_pairs={{8,16},{16,8},{9,17},{17,9},{10,18},{18,10},{11,19},{19,11},{12,20... | collective-permute-start | bytes 165896 | tf_op jit(solution)/shard_map/ppermute | solution.py:306
  58.0 10.4 %all-to-all-start.2 = ((f32[16,8,128]{2,1,0:T(8,128)}), f32[16,8,128]{2,1,0:T(8,128)S(1)}, u32[]{:S(2)}, u32[]{:S(2)}) async-start(f32[16,8,128]{2,1,0:T(8,128)} %get-tuple-element.21), calls=%async_computation.2 | async-start | bytes 131072 | tf_op jit(solution)/shard_map/all_to_all | solution.py:427

commit v2 on v1

--- a/solution.py
+++ b/solution.py
@@ -42,6 +42,11 @@
 def by_side(axis, low, high):
     even = lax.axis_index(axis) % 2 == 0
     return jnp.where(even, high, low), jnp.where(even, low, high)
+
+
+def by_parity(axis, mine, other):
+    even = lax.axis_index(axis) % 2 == 0
+    return jnp.where(even, mine, other), jnp.where(even, other, mine)
 
 
 def lane_ids(lanes):
@@ -93,33 +98,45 @@
     return jnp.dot(by_row * own, jnp.ones((cells_y, LANES), F32), preferred_element_type=F32)
 
 
-def adjoint_kernel(
-    freqs, cols, spectra_ref, spec_ref, class_ref, out_ref, near_ref, far_ref, ends_ref
-):
-    _, _, cells_x, cells_y, all_sensors = spectra_ref.shape
-    cells = cells_x * cells_y
-    stride = out_ref.shape[1] // cells_x
-    lanes = spec_ref.shape[1] * spec_ref.shape[3]
-
-    parts = [
-        spec_ref[:, b].reshape(all_sensors, spec_ref.shape[3]) for b in range(spec_ref.shape[1])
-    ]
+def adjoint_of(part, stacked):
+    _, cells_x, cells_y, all_sensors = part.shape
+    both = part.reshape(2, cells_x * cells_y, all_sensors)
+    both = jnp.concatenate([both[0], both[1]], axis=1)
+    return jnp.dot(both, stacked, preferred_element_type=F32)
+
+
+def freq_lanes(lanes, cols, freqs):
+    return (lane_ids(lanes) // (2 * cols)) % freqs
+
+
+def order_kernel(cols, spectra_in, mine_ref, other_ref, stacked_ref):
+    halves, group, sensors, block = mine_ref.shape
+    lanes = group * block
+    parts = []
+    for b in range(group):
+        pair = by_parity("sy", mine_ref[:, b], other_ref[:, b])
+        parts.append(jnp.stack(pair, axis=1).reshape(2 * halves * sensors, block))
     direct = jnp.concatenate(parts, axis=1)
     wide = direct.astype(F32)
     is_real = (lane_ids(lanes) // cols) % 2 == 0
     turned = jnp.where(
         is_real, pltpu.roll(wide, lanes - cols, 1), -pltpu.roll(wide, cols, 1)
     ).astype(BF16)
-    stacked = jnp.concatenate([direct, turned], axis=0)
-    freq_of = (lane_ids(lanes) // (2 * cols)) % freqs
-
+    stacked_ref[...] = jnp.concatenate([direct, turned], axis=0)
+
+
+def adjoint_kernel(
+    freqs, cols, spectra_ref, stacked_ref, class_ref, out_ref, near_ref, far_ref, ends_ref
+):
+    _, _, cells_x, cells_y, all_sensors = spectra_ref.shape
+    stride = out_ref.shape[1] // cells_x
+    lanes = stacked_ref.shape[1]
+    freq_of = freq_lanes(lanes, cols, freqs)
     classes = class_rows(class_ref)
-    acc = None
-    for f in range(freqs):
-        both = spectra_ref[f].reshape(2, cells, all_sensors)
-        both = jnp.concatenate([both[0], both[1]], axis=1)
-        got = jnp.dot(both, stacked, preferred_element_type=F32)
-        acc = got if acc is None else jnp.where(freq_of == f, got, acc)
+    stacked = stacked_ref[...]
+    acc = adjoint_of(spectra_ref[0], stacked)
+    for f in range(1, freqs):
+        acc = jnp.where(freq_of == f, adjoint_of(spectra_ref[f], stacked), acc)
     for k in range(out_ref.shape[0]):
         part = classes if k * LANES == lanes else acc[:, k * LANES : (k + 1) * LANES]
         for x in range(cells_x):
@@ -170,7 +187,8 @@
     near_x_ref,
     far_x_ref,
     kappa_ref,
-    out_ref,
+    keep_ref,
+    send_ref,
     wide,
     gain,
     one,
@@ -249,20 +267,26 @@
         for g in range(groups):
             at = (g * freqs + f) * 2 * cols
             sums[at : at + 2 * cols] = got[g * 2 * cols : (g + 1) * 2 * cols]
-    back = sums[...].T.astype(BF16)
-    tiles, _, sensors, block = out_ref.shape
+    back = sums[...].T
+    halves, _, sensors, block = keep_ref.shape
     for g in range(groups):
-        out_ref[:, g] = back[:, g * block : (g + 1) * block].reshape(tiles, sensors, block)
-
-
-def solution_kernel(solution_in, direction_in, step_ref, out_ref, solution_ref, direction_ref, sems):
-    fetch_all(((solution_in, solution_ref), (direction_in, direction_ref)), sems)
-    for c in range(solution_ref.shape[0]):
-        out_ref[c] = solution_ref[c] + step_ref[c] * direction_ref[c]
+        pair = back[:, g * block : (g + 1) * block].reshape(halves, 2, sensors, block)
+        keep, send = by_parity("sy", pair[:, 0], pair[:, 1])
+        keep_ref[:, g] = keep
+        send_ref[:, g] = send.astype(BF16)
 
 
 def residual_kernel(
-    terms_ref, table_ref, noise_ref, residual_ref, direction_ref, step_ref, new_residual_ref, norm_ref
+    terms_ref,
+    table_ref,
+    noise_ref,
+    solution_ref,
+    residual_ref,
+    direction_ref,
+    step_ref,
+    new_solution_ref,
+    new_residual_ref,
+    norm_ref,
 ):
     cols, sensors, steps = direction_ref.shape
     parts = []
@@ -276,6 +300,7 @@
         product = direction_ref[c] + noise_ref[...] * returned[c * sensors : (c + 1) * sensors]
         new_residual = residual_ref[c] - step_ref[c] * product
         new_residual_ref[c] = new_residual
+        new_solution_ref[c] = solution_ref[c] + step_ref[c] * direction_ref[c]
         norm = jnp.sum(
             jnp.sum(new_residual * new_residual, axis=0, keepdims=True), axis=1, keepdims=True
         )
@@ -283,20 +308,34 @@
 
 
 def direction_kernel(
-    norms_ref, residual_ref, direction_ref, old_ref, residual_out, direction_out, norm_ref, held, sems
+    norms_ref,
+    solution_ref,
+    residual_ref,
+    direction_ref,
+    old_ref,
+    solution_out,
+    residual_out,
+    direction_out,
+    norm_ref,
+    held,
+    sems,
 ):
     cols, sensors, steps = direction_ref.shape
-    first = pltpu.make_async_copy(residual_ref, residual_out, sems.at[0])
-    first.start()
+    early = [
+        pltpu.make_async_copy(solution_ref, solution_out, sems.at[0]),
+        pltpu.make_async_copy(residual_ref, residual_out, sems.at[1]),
+    ]
+    for copy in early:
+        copy.start()
     norm = jnp.sum(norms_ref[...], axis=0)
     for c in range(cols):
         held[c] = residual_ref[c] + (norm[c : c + 1, 0:1] / old_ref[c]) * direction_ref[c]
-    second = pltpu.make_async_copy(held, direction_out, sems.at[1])
-    second.start()
+    last = pltpu.make_async_copy(held, direction_out, sems.at[2])
+    last.start()
     for c in range(cols):
         norm_ref[c] = jnp.max(norm[c : c + 1])
-    first.wait()
-    second.wait()
+    for copy in (*early, last):
+        copy.wait()
 
 
 def swap(axis, toward_partner, toward_other):
@@ -306,6 +345,22 @@
     second = lax.ppermute(toward_other, axis, far)
     first = lax.ppermute(toward_partner, axis, near)
     return first, second
+
+
+def partners(axis):
+    return [(i, i ^ 1) for i in range(lax.axis_size(axis))]
+
+
+def exchange_half(blocks):
+    sx, sy, fq = (lax.axis_size(axis) for axis in ALL_AXES)
+    groups = [
+        [(x * sy + y) * fq + f for x in range(sx) for y in range(parity, sy, 2) for f in range(fq)]
+        for parity in range(2)
+    ]
+    flat = blocks.reshape((-1,) + blocks.shape[2:])
+    return lax.all_to_all(flat, ALL_AXES, 0, 0, axis_index_groups=groups, tiled=True).reshape(
+        blocks.shape
+    )
 
 
 def on_device(
@@ -323,6 +378,7 @@
     cols, sensors, steps = direction.shape
     fq_blocks = lax.axis_size("fq")
     tiles = lax.axis_size("sx") * lax.axis_size("sy")
+    halves = tiles // 2
     block = 2 * local_freqs * cols
     lanes = block * fq_blocks
     forward, inverse = tables(local_freqs * fq_blocks, local_freqs, cols, steps)
@@ -336,8 +392,8 @@
     like = jax.ShapeDtypeStruct(direction.shape, F32)
     held = pltpu.VMEM(direction.shape, F32)
     spec = pl.pallas_call(
-        functools.partial(spectrum_kernel, tiles, fq_blocks),
-        out_shape=jax.ShapeDtypeStruct((tiles, fq_blocks, sensors, block), BF16),
+        functools.partial(spectrum_kernel, halves, fq_blocks),
+        out_shape=jax.ShapeDtypeStruct((halves, fq_blocks, sensors, block), BF16),
         in_specs=[HBM] * 3,
         out_specs=VMEM,
         scratch_shapes=[
@@ -352,18 +408,8 @@
         ),
         name="spectrum",
     )(direction, noise_weight, forward)
-    spec = lax.all_to_all(
-        spec.reshape(tiles * fq_blocks, sensors, block), ALL_AXES, 0, 0, tiled=True
-    ).reshape(tiles, fq_blocks, sensors, block)
-    new_solution = pl.pallas_call(
-        solution_kernel,
-        out_shape=like,
-        in_specs=[HBM, HBM, SMEM],
-        out_specs=VMEM,
-        scratch_shapes=[held, held, pltpu.SemaphoreType.DMA((2,))],
-        compiler_params=params(),
-        name="solution",
-    )(solution, direction, step_length)
+    mine = exchange_half(spec)
+    other = lax.ppermute(mine, "sy", partners("sy"))
 
     edge = jax.ShapeDtypeStruct((DEPTH * cells_x, wide), BF16)
     end = jax.ShapeDtypeStruct((DEPTH * stride, wide), BF16)
@@ -371,6 +417,18 @@
     slabs = width // LANES
     pieces = []
     for i in range(chunks):
+        at = slice(i * group, (i + 1) * group)
+        stacked = pl.pallas_call(
+            functools.partial(order_kernel, cols),
+            out_shape=jax.ShapeDtypeStruct((2 * all_sensors, width), BF16),
+            in_specs=[HBM, VMEM, VMEM],
+            out_specs=VMEM,
+            compiler_params=params(48),
+            cost_estimate=pl.CostEstimate(
+                flops=2 * spectra.size, bytes_accessed=4 * spectra.size, transcendentals=0
+            ),
+            name="order",
+        )(spectra, mine[:, at], other[:, at])
         source, near_y, far_y, ends = pl.pallas_call(
             functools.partial(adjoint_kernel, local_freqs, cols),
             out_shape=(
@@ -383,7 +441,7 @@
             out_specs=(VMEM,) * 4,
             compiler_params=params(),
             name="adjoint",
-        )(spectra, spec[:, i * group : (i + 1) * group], class_map.T)
+        )(spectra, stacked, class_map.T)
         near_y, far_y = swap("sy", near_y, far_y)
         near_x, far_x = pl.pallas_call(
             ends_kernel,
@@ -398,9 +456,12 @@
         pieces.append(
             pl.pallas_call(
                 functools.partial(field_kernel, local_freqs, cols),
-                out_shape=jax.ShapeDtypeStruct((tiles, group, sensors, block), BF16),
+                out_shape=(
+                    jax.ShapeDtypeStruct((halves, group, sensors, block), F32),
+                    jax.ShapeDtypeStruct((halves, group, sensors, block), BF16),
+                ),
                 in_specs=[VMEM] * 6 + [SMEM],
-                out_specs=VMEM,
+                out_specs=(VMEM,) * 2,
                 scratch_shapes=[
                     pltpu.VMEM((slabs + 1, total, LANES), F32),
                     pltpu.VMEM((total, LANES), F32),
@@ -412,28 +473,28 @@
                 name="field",
             )(spectra, source, near_y, far_y, near_x, far_x, class_kappa)
         )
-    terms = jnp.concatenate(pieces, axis=1)
-    terms = lax.all_to_all(
-        terms.reshape(tiles * fq_blocks, sensors, block), ALL_AXES, 0, 0, tiled=True
-    ).reshape(tiles, fq_blocks, sensors, block)
-    new_residual, norms = pl.pallas_call(
+    keep = jnp.concatenate([piece[0] for piece in pieces], axis=1)
+    send = jnp.concatenate([piece[1] for piece in pieces], axis=1)
+    taken = lax.ppermute(send, "sy", partners("sy"))
+    terms = exchange_half((keep + taken.astype(F32)).astype(BF16))
+    new_solution, new_residual, norms = pl.pallas_call(
         residual_kernel,
-        out_shape=(like, jax.ShapeDtypeStruct((tiles, cols, LANES), F32)),
-        in_specs=[VMEM] * 5 + [SMEM],
-        out_specs=(VMEM,) * 2,
+        out_shape=(like, like, jax.ShapeDtypeStruct((tiles, cols, LANES), F32)),
+        in_specs=[VMEM] * 6 + [SMEM],
+        out_specs=(VMEM,) * 3,
         compiler_params=params(),
         name="residual",
-    )(terms, inverse, noise_weight, residual, direction, step_length)
+    )(terms, inverse, noise_weight, solution, residual, direction, step_length)
     norms = lax.all_to_all(norms, GRID_AXES, 0, 0, tiled=True)
-    new_residual, new_direction, new_norm = pl.pallas_call(
+    new_solution, new_residual, new_direction, new_norm = pl.pallas_call(
         direction_kernel,
-        out_shape=(like, like, jax.ShapeDtypeStruct((cols,), F32)),
-        in_specs=[VMEM] * 3 + [SMEM],
-        out_specs=(HBM, HBM, SMEM),
-        scratch_shapes=[held, pltpu.SemaphoreType.DMA((2,))],
+        out_shape=(like, like, like, jax.ShapeDtypeStruct((cols,), F32)),
+        in_specs=[VMEM] * 4 + [SMEM],
+        out_specs=(HBM, HBM, HBM, SMEM),
+        scratch_shapes=[held, pltpu.SemaphoreType.DMA((3,))],
         compiler_params=params(),
         name="direction",
-    )(norms, new_residual, direction, old_norm)
+    )(norms, new_solution, new_residual, direction, old_norm)
     return (new_solution, new_residual, new_direction, new_norm)
 
 

time: 70.6 us -> 64.8 us (0.918)
  local copies, waits for them, and re-layouts: 4.12 us -> 0.06 us
  waiting for transfers between devices: 8.8 us -> 5.55 us
  blocking collectives: 37.7 us -> 40.5 us
  Pallas kernels: 13.3 us -> 11.4 us
    all_to_all x1 -> x0, waiting for transfers between devices: 5.27 us -> none  [on_device(): norms = lax.all_to_all(norms, GRID_AXES, 0, 0, tiled=True)]
    unnamed x22 -> x20, local copies, waits for them, and re-layouts: 4.12 us -> 0.06 us
    ppermute x0 -> x2, starting transfers between devices: none -> 3.82 us  [the longest x1 3.82 us: on_device(): taken = lax.ppermute(send, 'sy', partners('sy'))]
    all_to_all x1 -> x0, starting transfers between devices: 3.5 us -> none  [on_device(): norms = lax.all_to_all(norms, GRID_AXES, 0, 0, tiled=True)]
    all_to_all x2 -> x3, blocking collectives: 37.7 us -> 40.5 us  [the longest x2 30.6 us: exchange_half(): lax.all_to_all(flat, ALL_AXES, 0, 0, axis_index_groups=groups, tiled=True)]
    ppermute x0 -> x2, waiting for transfers between devices: none -> 2.33 us  [the longest x1 1.35 us: on_device(): other = lax.ppermute(mine, 'sy', partners('sy'))]
    pallas_call x4, Pallas kernels: 7.06 us -> 5.1 us  [the longest x1 1.96 us: on_device(): pl.pallas_call(functools.partial(spectrum_kernel, halves, fq_blocks), out...]
  transfers between devices with their start and end apart: 5 -> 6, of which waited for: 3 -> 4; matrix products, arithmetic and copies ran while one was open for 0% -> 0% of each run, Pallas kernels for 2% -> 0%
where the time goes in v2:
time: 64.8 us; the launch traced here: 64.5 us
  blocking collectives  40.5 us (62%)
  Pallas kernels  11.4 us (18%)
  starting transfers between devices  6.14 us (9%)
  waiting for transfers between devices  5.55 us (9%)
  between operations  0.81 us (1%)
    all_to_all x2, blocking collectives, exchange_half(): lax.all_to_all(flat, ALL_AXES, 0, 0, axis_index_groups=groups, tiled=True)  30.6 us
    all_to_all x1, blocking collectives, on_device(): norms = lax.all_to_all(norms, GRID_AXES, 0, 0, tiled=True)  9.82 us
    ppermute x1, starting transfers between devices, on_device(): taken = lax.ppermute(send, 'sy', partners('sy'))  3.82 us
    pallas_call x1, Pallas kernels, on_device(): pl.pallas_call(functools.partial(field_kernel, local_freqs, cols), out_sh...  3.71 us
    ppermute x2, waiting for transfers between devices, swap(): first = lax.ppermute(toward_partner, axis, near)  3.21 us
    pallas_call x1, Pallas kernels, on_device(): pl.pallas_call(functools.partial(adjoint_kernel, local_freqs, cols), out_...  2.5 us
    pallas_call x1, Pallas kernels, on_device(): pl.pallas_call(functools.partial(spectrum_kernel, halves, fq_blocks), out...  1.96 us
    pallas_call x1, Pallas kernels, on_device(): pl.pallas_call(direction_kernel, out_shape=(like, like, like, jax.ShapeDt...  1.88 us
  transfers between devices with their start and end apart: 6, of which 4 were waited for; matrix products, arithmetic and copies ran while one was open for 0% of the time, Pallas kernels for 0%

profile of v2, /device:TPU:0, one launch (start us, length us, event | category | flops | bytes accessed | tf_op | source)
XLA Modules:
  0.0 64.5 jit_solution(16541255933491623981)
XLA Ops:
  0.6 0.0 copy-start.6
  0.6 2.0 %spectrum.1 = bf16[8,2,32,128]{3,2,1,0:T(8,128)(2,1)} custom-call(f32[8,32,32]{2,1,0:T(8,128)} %direction_ref.3, f32[32,32]{1,0:T(8,128)} %noise_ref.1, f32[32,256]{1,0:T(8,128)} %constant.4.clone.table_in), custom_call_target="tpu_custom_call" | custom-call | flops 8388608 | bytes 16777216 | tf_op jit(solution)/shard_map/spectrum/pallas_call | solution.py:394
  2.6 0.0 copy-start
  2.6 16.4 %all_to_all.15 = bf16[16,32,128]{2,1,0:T(8,128)(2,1)S(1)} all-to-all(bf16[16,32,128]{2,1,0:T(8,128)(2,1)} %bitcast.9), channel_id=1, replica_groups={{0,1,4,5,8,9,12,13,16,17,20,21,24,25,28,29},{2,3,6,7,10,11,14,15,18,19,..., dimensions={0} | all-to-all | bytes 262144 | tf_op jit(solution)/shard_map/all_to_all | solution.py:361
  19.0 0.0 copy-start.9
  19.0 0.0 collective-permute-start
  19.0 1.3 %collective-permute-done.other_ref = bf16[8,2,32,128]{3,2,1,0:T(8,128)(2,1)S(1)} collective-permute-done((bf16[8,2,32,128]{3,2,1,0:T(8,128)(2,1)S(1)}, bf16[8,2,32,128]{3,2,1,0:T(8,128)(2,1)S(1)}, u32[]{:S(2)}, u32[]{:S(2)}) %collective-permute-start) | collective-permute-done | bytes 131104 | tf_op jit(solution)/shard_map/ppermute | solution.py:412
  20.3 0.3 order.1.stacked_ref
  20.6 0.0 copy-done.6
  20.6 0.0 copy-done
  20.6 0.0 copy-start.1
  20.7 0.0 copy-start.2
  20.7 0.0 copy-start.3
  20.7 0.0 copy-start.4
  20.7 0.0 copy-start.5
  20.7 0.0 copy-start.7
  20.7 0.0 copy-start.8
  20.7 2.5 %adjoint.1 = (f32[3,768,128]{2,1,0:T(8,128)S(1)}, bf16[96,384]{1,0:T(8,128)(2,1)S(1)}, bf16[96,384]{1,0:T(8,128)(2,1)S(1)}, f32[2,72,384]{2,1,0:T(8,128)S(1)}) custom-call(bf16[8,2,32,16,512]{4,3,2,1,0:T(8,128)(2,1)S(1)} %copy-done, bf16[1024,256]{1,0:T(8,128)(2,1)S(1)} %order.1.stacked_ref, s32[16,32]{1,0:T(8,128)S(1)} %bitcast.8), custom_call_target="tpu_custom_call" | custom-call | tf_op jit(solution)/shard_map/adjoint/pallas_call | solution.py:432
  23.2 0.2 collective-permute-start.1
  23.4 0.7 %collective-permute-start.2 = (bf16[96,384]{1,0:T(8,128)(2,1)S(1)}, bf16[96,384]{1,0:T(8,128)(2,1)S(1)}, u32[]{:S(2)}, u32[]{:S(2)}) collective-permute-start(bf16[96,384]{1,0:T(8,128)(2,1)S(1)} %get-tuple-element.17), channel_id=1, source_target_pairs={{2,4},{4,2},{3,5},{5,3},{10,12},{12,10},{11,13},{13,11},{18,20},{2... | collective-permute-start | bytes 221192 | tf_op jit(solution)/shard_map/ppermute | solution.py:345
  24.1 0.5 collective-permute-done.1.near_ref.near_y_ref
  24.6 0.0 collective-permute-done.2.far_ref.far_y_ref
  24.6 0.1 ends.1
  24.7 0.8 %collective-permute-start.3 = (bf16[72,384]{1,0:T(8,128)(2,1)S(1)}, bf16[72,384]{1,0:T(8,128)(2,1)S(1)}, u32[]{:S(2)}, u32[]{:S(2)}) collective-permute-start(bf16[72,384]{1,0:T(8,128)(2,1)S(1)} %get-tuple-element.19), channel_id=1, source_target_pairs={{0,8},{8,0},{16,24},{24,16},{1,9},{9,1},{17,25},{25,17},{2,10},{10... | collective-permute-start | bytes 165896 | tf_op jit(solution)/shard_map/ppermute | solution.py:346
  25.5 0.7 %collective-permute-start.4 = (bf16[72,384]{1,0:T(8,128)(2,1)S(1)}, bf16[72,384]{1,0:T(8,128)(2,1)S(1)}, u32[]{:S(2)}, u32[]{:S(2)}) collective-permute-start(bf16[72,384]{1,0:T(8,128)(2,1)S(1)} %get-tuple-element.20), channel_id=1, source_target_pairs={{8,16},{16,8},{9,17},{17,9},{10,18},{18,10},{11,19},{19,11},{12,20... | collective-permute-start | bytes 165896 | tf_op jit(solution)/shard_map/ppermute | solution.py:345
  26.1 2.8 %collective-permute-done.3.near_x_ref = bf16[72,384]{1,0:T(8,128)(2,1)S(1)} collective-permute-done((bf16[72,384]{1,0:T(8,128)(2,1)S(1)}, bf16[72,384]{1,0:T(8,128)(2,1)S(1)}, u32[]{:S(2)}, u32[]{:S(2)}) %collective-permute-start.3) | collective-permute-done | bytes 55328 | tf_op jit(solution)/shard_map/ppermute | solution.py:346
  28.9 0.0 collective-permute-done.4.far_x_ref
  28.9 0.0 copy-done.9
  28.9 3.7 %field.1 = (f32[8,2,32,128]{3,2,1,0:T(8,128)S(1)}, bf16[8,2,32,128]{3,2,1,0:T(8,128)(2,1)S(1)}) custom-call(bf16[8,2,32,16,512]{4,3,2,1,0:T(8,128)(2,1)S(1)} %copy-done, f32[3,768,128]{2,1,0:T(8,128)S(1)} %get-tuple-element.15.source_ref, bf16[96,384]{1,0:T(8,128)(2,1)S(1)} %collective-permute-done.1.near_ref.near_y_ref, ...), custom_call_target="tpu_custom_call" | custom-call | tf_op jit(solution)/shard_map/field/pallas_call | solution.py:457
  32.6 3.8 %collective-permute-start.5 = (bf16[8,2,32,128]{3,2,1,0:T(8,128)(2,1)S(1)}, bf16[8,2,32,128]{3,2,1,0:T(8,128)(2,1)S(1)}, u32[]{:S(2)}, u32[]{:S(2)}) collective-permute-start(bf16[8,2,32,128]{3,2,1,0:T(8,128)(2,1)S(1)} %get-tuple-element.22), channel_id=1, source_target_pairs={{0,2},{2,0},{4,6},{6,4},{1,3},{3,1},{5,7},{7,5},{8,10},{10,8},{12,... | collective-permute-start | bytes 393224 | tf_op jit(solution)/shard_map/ppermute | solution.py:478
  36.4 1.0 %collective-permute-done.5 = bf16[8,2,32,128]{3,2,1,0:T(8,128)(2,1)S(1)} collective-permute-done((bf16[8,2,32,128]{3,2,1,0:T(8,128)(2,1)S(1)}, bf16[8,2,32,128]{3,2,1,0:T(8,128)(2,1)S(1)}, u32[]{:S(2)}, u32[]{:S(2)}) %collective-permute-start.5) | collective-permute-done | bytes 131104 | tf_op jit(solution)/shard_map/ppermute | solution.py:478
  37.5 14.3 %all_to_all.16 = bf16[16,32,128]{2,1,0:T(8,128)(2,1)S(1)} all-to-all(bf16[16,32,128]{2,1,0:T(8,128)(2,1)S(1)} %bitcast.10), channel_id=1, replica_groups={{0,1,4,5,8,9,12,13,16,17,20,21,24,25,28,29},{2,3,6,7,10,11,14,15,18,19,..., dimensions={0} | all-to-all | bytes 262144 | tf_op jit(solution)/shard_map/all_to_all | solution.py:361
  51.7 0.0 copy-done.1
  51.7 0.0 copy-done.2
  51.7 0.0 copy-done.3
  51.7 0.0 copy-done.4
  51.7 0.0 copy-done.5
  51.7 0.0 copy-done.7
  51.8 1.0 %residual.1 = (f32[8,32,32]{2,1,0:T(8,128)S(1)}, f32[8,32,32]{2,1,0:T(8,128)S(1)}, f32[16,8,128]{2,1,0:T(8,128)S(1)}) custom-call(bf16[8,2,32,128]{3,2,1,0:T(8,128)(2,1)S(1)} %bitcast.7, f32[256,32]{1,0:T(8,128)S(1)} %copy-done.4, f32[32,32]{1,0:T(8,128)S(1)} %copy-done.5, f32[8,32,32]{2,1,0:T(8,128)S(1)} %copy-done.2, f32[8,32,32]{2,1,0:T(8,128)S(1)} %copy-done.3, ...), custom_call_target="tpu_custom_call" | custom-call | tf_op jit(solution)/shard_map/residual/pallas_call | solution.py:480
  52.8 9.8 %all_to_all.17.norms_ref = f32[16,8,128]{2,1,0:T(8,128)S(1)} all-to-all(f32[16,8,128]{2,1,0:T(8,128)S(1)} %get-tuple-element.23), channel_id=1, replica_groups=mesh['sx'=4,'sy'=4,'fq'=2] {'sx','sy'}, dimensions={0} | all-to-all | bytes 131072 | tf_op jit(solution)/shard_map/all_to_all | solution.py:488
  62.6 0.0 copy-done.8
  62.6 1.9 %direction.1 = (f32[8,32,32]{2,1,0:T(8,128)}, f32[8,32,32]{2,1,0:T(8,128)}, f32[8,32,32]{2,1,0:T(8,128)}, f32[8]{0:T(128)}) custom-call(f32[16,8,128]{2,1,0:T(8,128)S(1)} %all_to_all.17.norms_ref, f32[8,32,32]{2,1,0:T(8,128)S(1)} %get-tuple-element.24.solution_ref, f32[8,32,32]{2,1,0:T(8,128)S(1)} %get-tuple-element.25.residual_ref, ...), custom_call_target="tpu_custom_call" | custom-call | tf_op jit(solution)/shard_map/direction/pallas_call | solution.py:489
  (1 shorter events, 0.0 us)
Async XLA Ops:
  0.6 20.0 %copy-start.6 = (s32[32,16]{0,1:T(8,128)S(1)}, s32[32,16]{0,1:T(8,128)}, u32[]{:S(2)}) copy-start(s32[32,16]{0,1:T(8,128)} %param.13) | copy-start | bytes 6148
  2.6 18.0 %copy-start = (bf16[8,2,32,16,512]{4,3,2,1,0:T(8,128)(2,1)S(1)}, bf16[8,2,32,16,512]{4,3,2,1,0:T(8,128)(2,1)}, u32[]{:S(2)}) copy-start(bf16[8,2,32,16,512]{4,3,2,1,0:T(8,128)(2,1)} %spectra_ref.3) | copy-start | bytes 25165828
  19.0 9.9 %copy-start.9 = (f32[8]{0:T(128)S(1)}, f32[8]{0:T(128)}, u32[]{:S(2)}) copy-start(f32[8]{0:T(128)} %kappa_ref.1) | copy-start | bytes 100
  19.0 1.3 %collective-permute-start = (bf16[8,2,32,128]{3,2,1,0:T(8,128)(2,1)S(1)}, bf16[8,2,32,128]{3,2,1,0:T(8,128)(2,1)S(1)}, u32[]{:S(2)}, u32[]{:S(2)}) collective-permute-start(bf16[8,2,32,128]{3,2,1,0:T(8,128)(2,1)S(1)} %bitcast.5), channel_id=1, source_target_pairs={{0,2},{2,0},{4,6},{6,4},{1,3},{3,1},{5,7},{7,5},{8,10},{10,8},{12,... | collective-permute-start | bytes 393224 | tf_op jit(solution)/shard_map/ppermute | solution.py:412
  20.6 31.1 %copy-start.1 = (f32[8,32,32]{2,1,0:T(8,128)S(1)}, f32[8,32,32]{2,1,0:T(8,128)}, u32[]{:S(2)}) copy-start(f32[8,32,32]{2,1,0:T(8,128)} %direction_ref.3) | copy-start | bytes 98308
  20.7 31.1 %copy-start.2 = (f32[8,32,32]{2,1,0:T(8,128)S(1)}, f32[8,32,32]{2,1,0:T(8,128)}, u32[]{:S(2)}) copy-start(f32[8,32,32]{2,1,0:T(8,128)} %solution_ref.1) | copy-start | bytes 98308
  20.7 31.1 %copy-start.3 = (f32[8,32,32]{2,1,0:T(8,128)S(1)}, f32[8,32,32]{2,1,0:T(8,128)}, u32[]{:S(2)}) copy-start(f32[8,32,32]{2,1,0:T(8,128)} %residual_ref.1) | copy-start | bytes 98308
  20.7 31.1 %copy-start.4 = (f32[256,32]{1,0:T(8,128)S(1)}, f32[256,32]{1,0:T(8,128)}, u32[]{:S(2)}) copy-start(f32[256,32]{1,0:T(8,128)} %constant.5.clone.table_ref) | copy-start | bytes 98308
  20.7 31.1 %copy-start.5 = (f32[32,32]{1,0:T(8,128)S(1)}, f32[32,32]{1,0:T(8,128)}, u32[]{:S(2)}) copy-start(f32[32,32]{1,0:T(8,128)} %noise_ref.1) | copy-start | bytes 12292
  20.7 31.0 %copy-start.7 = (f32[8]{0:T(128)S(1)}, f32[8]{0:T(128)}, u32[]{:S(2)}) copy-start(f32[8]{0:T(128)} %step_ref.1) | copy-start | bytes 100
  20.7 41.9 %copy-start.8 = (f32[8]{0:T(128)S(1)}, f32[8]{0:T(128)}, u32[]{:S(2)}) copy-start(f32[8]{0:T(128)} %old_ref.1) | copy-start | bytes 100
  23.2 1.3 %collective-permute-start.1 = (bf16[96,384]{1,0:T(8,128)(2,1)S(1)}, bf16[96,384]{1,0:T(8,128)(2,1)S(1)}, u32[]{:S(2)}, u32[]{:S(2)}) collective-permute-start(bf16[96,384]{1,0:T(8,128)(2,1)S(1)} %get-tuple-element.16), channel_id=1, source_target_pairs={{0,2},{2,0},{4,6},{6,4},{1,3},{3,1},{5,7},{7,5},{8,10},{10,8},{12,... | collective-permute-start | bytes 221192 | tf_op jit(solution)/shard_map/ppermute | solution.py:346
  23.4 1.1 %collective-permute-start.2 = (bf16[96,384]{1,0:T(8,128)(2,1)S(1)}, bf16[96,384]{1,0:T(8,128)(2,1)S(1)}, u32[]{:S(2)}, u32[]{:S(2)}) collective-permute-start(bf16[96,384]{1,0:T(8,128)(2,1)S(1)} %get-tuple-element.17), channel_id=1, source_target_pairs={{2,4},{4,2},{3,5},{5,3},{10,12},{12,10},{11,13},{13,11},{18,20},{2... | collective-permute-start | bytes 221192 | tf_op jit(solution)/shard_map/ppermute | solution.py:345
  24.7 4.2 %collective-permute-start.3 = (bf16[72,384]{1,0:T(8,128)(2,1)S(1)}, bf16[72,384]{1,0:T(8,128)(2,1)S(1)}, u32[]{:S(2)}, u32[]{:S(2)}) collective-permute-start(bf16[72,384]{1,0:T(8,128)(2,1)S(1)} %get-tuple-element.19), channel_id=1, source_target_pairs={{0,8},{8,0},{16,24},{24,16},{1,9},{9,1},{17,25},{25,17},{2,10},{10... | collective-permute-start | bytes 165896 | tf_op jit(solution)/shard_map/ppermute | solution.py:346
  25.5 3.4 %collective-permute-start.4 = (bf16[72,384]{1,0:T(8,128)(2,1)S(1)}, bf16[72,384]{1,0:T(8,128)(2,1)S(1)}, u32[]{:S(2)}, u32[]{:S(2)}) collective-permute-start(bf16[72,384]{1,0:T(8,128)(2,1)S(1)} %get-tuple-element.20), channel_id=1, source_target_pairs={{8,16},{16,8},{9,17},{17,9},{10,18},{18,10},{11,19},{19,11},{12,20... | collective-permute-start | bytes 165896 | tf_op jit(solution)/shard_map/ppermute | solution.py:345
  32.6 4.8 %collective-permute-start.5 = (bf16[8,2,32,128]{3,2,1,0:T(8,128)(2,1)S(1)}, bf16[8,2,32,128]{3,2,1,0:T(8,128)(2,1)S(1)}, u32[]{:S(2)}, u32[]{:S(2)}) collective-permute-start(bf16[8,2,32,128]{3,2,1,0:T(8,128)(2,1)S(1)} %get-tuple-element.22), channel_id=1, source_target_pairs={{0,2},{2,0},{4,6},{6,4},{1,3},{3,1},{5,7},{7,5},{8,10},{10,8},{12,... | collective-permute-start | bytes 393224 | tf_op jit(solution)/shard_map/ppermute | solution.py:478

commit v3 on v2

--- a/solution.py
+++ b/solution.py
@@ -126,7 +126,7 @@
 
 
 def adjoint_kernel(
-    freqs, cols, spectra_ref, stacked_ref, class_ref, out_ref, near_ref, far_ref, ends_ref
+    freqs, cols, spectra_ref, stacked_ref, class_ref, out_ref, far_ref, near_ref, ends_ref
 ):
     _, _, cells_x, cells_y, all_sensors = spectra_ref.shape
     stride = out_ref.shape[1] // cells_x
@@ -154,7 +154,7 @@
         ends_ref[1, :, at] = out_ref[k, (cells_x - DEPTH) * stride : cells_x * stride]
 
 
-def ends_kernel(ends_ref, near_ref, far_ref, near_out, far_out, held):
+def ends_kernel(ends_ref, far_ref, near_ref, far_out, near_out, held):
     span = ends_ref.shape[1]
     stride = span // DEPTH
     cells_x = near_ref.shape[0] // DEPTH
@@ -177,15 +177,93 @@
     far_out[...] = far.astype(BF16)
 
 
+def coefficients(classes, kappa_ref):
+    kappa = jnp.zeros_like(classes)
+    for n in range(kappa_ref.shape[0]):
+        kappa = jnp.where(classes == n + 1.0, kappa_ref[n], kappa)
+    scale = jnp.where(classes > 0.0, 1.0 / (1.0 + 4.0 * kappa), 0.0)
+    return scale, kappa * scale
+
+
+def sweep(source, gain, old, new, first, last, stride):
+    near = (
+        old[first - stride : last - stride]
+        + old[first + stride : last + stride]
+        + old[first - 1 : last - 1]
+        + old[first + 1 : last + 1]
+    )
+    new[first:last] = source[first:last] + gain[first:last] * near
+
+
+def both_forms(turned, cols):
+    blocks, cells = turned.shape[0] // (2 * cols), turned.shape[1]
+    pair = turned.reshape(blocks, 2, cols, cells)
+    plain = pair.astype(BF16).reshape(blocks, 2 * cols, cells)
+    crossed = jnp.stack([-pair[:, 1], pair[:, 0]], axis=1)
+    crossed = crossed.astype(BF16).reshape(blocks, 2 * cols, cells)
+    return jnp.concatenate([plain, crossed], axis=2)
+
+
+def rows_of(forms, f, freqs):
+    return jnp.concatenate([forms[b] for b in range(f, forms.shape[0], freqs)], axis=0)
+
+
+def inner_kernel(
+    freqs, cols, spectra_ref, source_ref, far_y_ref, near_y_ref, kappa_ref, sums_ref, wide, gain, one, two
+):
+    _, _, cells_x, cells_y, all_sensors = spectra_ref.shape
+    cells = cells_x * cells_y
+    stride = source_ref.shape[1] // cells_x
+    slabs = one.shape[0]
+    start = 2 * stride
+    rows = cells_x * stride
+    total = wide.shape[1]
+    for k in range(slabs + 1):
+        at = slice(k * LANES, (k + 1) * LANES)
+        wide[k, 0:start] = jnp.zeros((start, LANES), F32)
+        wide[k, start + rows : total] = jnp.zeros((total - start - rows, LANES), F32)
+        wide[k, start : start + rows] = source_ref[k]
+        after, before = by_side("sy", far_y_ref[:, at].astype(F32), near_y_ref[:, at].astype(F32))
+        for j in range(DEPTH):
+            part = slice(j * cells_x, (j + 1) * cells_x)
+            wide[k, pl.ds(start + cells_y + j, cells_x, stride=stride), :] = after[part]
+            wide[k, pl.ds(start - DEPTH + j, cells_x, stride=stride), :] = before[part]
+    lo, hi = start - 8, start + rows
+    scale, gain[lo:hi] = coefficients(wide[slabs, lo:hi], kappa_ref)
+    turned = []
+    for k in range(slabs):
+        wide[k, lo:hi] = wide[k, lo:hi] * scale
+        old, new = wide.at[k], one.at[k]
+        for x in range(1, DEPTH + 1):
+            first, last = start + x * stride - 8, start + rows - x * stride
+            sweep(wide.at[k], gain, old, new, first, last, stride)
+            old, new = new, (two.at[k] if x % 2 else one.at[k])
+        inner = old[start + DEPTH * stride : start + rows - DEPTH * stride]
+        inner = inner.reshape(cells_x - 2 * DEPTH, stride, LANES)[:, 0:cells_y]
+        edge = jnp.zeros((DEPTH * cells_y, LANES), F32)
+        turned.append(
+            jnp.concatenate([edge, inner.reshape(cells - 2 * DEPTH * cells_y, LANES), edge], axis=0).T
+        )
+    forms = both_forms(jnp.concatenate(turned, axis=0), cols)
+    groups = forms.shape[0] // freqs
+    for f in range(freqs):
+        right = spectra_ref[f].reshape(2 * cells, all_sensors)
+        got = jnp.dot(rows_of(forms, f, freqs), right, preferred_element_type=F32)
+        for g in range(groups):
+            at = (g * freqs + f) * 2 * cols
+            sums_ref[at : at + 2 * cols] = got[g * 2 * cols : (g + 1) * 2 * cols]
+
+
 def field_kernel(
     freqs,
     cols,
     spectra_ref,
     source_ref,
+    sums_ref,
+    far_y_ref,
     near_y_ref,
-    far_y_ref,
+    far_x_ref,
     near_x_ref,
-    far_x_ref,
     kappa_ref,
     keep_ref,
     send_ref,
@@ -196,77 +274,67 @@
     sums,
 ):
     _, _, cells_x, cells_y, all_sensors = spectra_ref.shape
-    cells = cells_x * cells_y
     stride = source_ref.shape[1] // cells_x
-    slabs = one.shape[0]
-    lanes = slabs * LANES
-    start = (DEPTH + 1) * stride
     rows = cells_x * stride
-    span = DEPTH * stride
-
-    total = wide.shape[1]
-    lo, hi = start - span - 8, start + rows + span
+    slabs = one.shape[1]
+    start = stride + 8
+    deep = 2 * DEPTH
+    total = wide.shape[2]
+
+    def base(x):
+        return start + x * stride
+
     for k in range(slabs + 1):
         at = slice(k * LANES, (k + 1) * LANES)
-        wide[k, 0:start] = jnp.zeros((start, LANES), F32)
-        wide[k, start + rows : total] = jnp.zeros((total - start - rows, LANES), F32)
-        wide[k, start : start + rows] = source_ref[k]
         after, before = by_side("sy", far_y_ref[:, at].astype(F32), near_y_ref[:, at].astype(F32))
         below, above = by_side("sx", far_x_ref[:, at].astype(F32), near_x_ref[:, at].astype(F32))
-        for j in range(DEPTH):
-            part = slice(j * cells_x, (j + 1) * cells_x)
-            wide[k, pl.ds(start + cells_y + j, cells_x, stride=stride), :] = after[part]
-            wide[k, pl.ds(start - DEPTH + j, cells_x, stride=stride), :] = before[part]
-        wide[k, start - span - DEPTH : start - DEPTH] = above
-        wide[k, start + rows - DEPTH : start + rows + span - DEPTH] = below
-
-    classes = wide[slabs, lo:hi]
-    kappa = jnp.zeros_like(classes)
-    for n in range(kappa_ref.shape[0]):
-        kappa = jnp.where(classes == n + 1.0, kappa_ref[n], kappa)
-    scale = jnp.where(classes > 0.0, 1.0 / (1.0 + 4.0 * kappa), 0.0)
-    gain[lo:hi] = kappa * scale
-
-    def sweep(k, old, new, margin):
-        first = start - margin * stride - 8
-        last = start + rows + margin * stride
-        near = (
-            old[k, first - stride : last - stride]
-            + old[k, first + stride : last + stride]
-            + old[k, first - 1 : last - 1]
-            + old[k, first + 1 : last + 1]
-        )
-        new[k, first:last] = wide[k, first:last] + gain[first:last] * near
-
+        for end in range(2):
+            own, outer = (DEPTH, 0) if end == 0 else (0, deep)
+            inside = 0 if end == 0 else cells_x - deep
+            wide[end, k] = jnp.zeros((total, LANES), F32)
+            wide[end, k, base(own) : base(own + deep)] = source_ref[
+                k, inside * stride : (inside + deep) * stride
+            ]
+            for j in range(DEPTH):
+                part = slice(j * cells_x + inside, j * cells_x + inside + deep)
+                wide[end, k, pl.ds(base(own) + cells_y + j, deep, stride=stride), :] = after[part]
+                wide[end, k, pl.ds(base(own) - DEPTH + j, deep, stride=stride), :] = before[part]
+            wide[end, k, base(outer) - DEPTH : base(outer + DEPTH) - DEPTH] = above if end == 0 else below
+    lo, hi = base(0) - 8, base(3 * DEPTH)
     turned = []
+    filler = -(deep * cells_y) % LANES
+    for end in range(2):
+        scale, gain[end, lo:hi] = coefficients(wide[end, slabs, lo:hi], kappa_ref)
+        for k in range(slabs):
+            wide[end, k, lo:hi] = wide[end, k, lo:hi] * scale
     for k in range(slabs):
-        wide[k, lo:hi] = wide[k, lo:hi] * scale
-        one[k] = wide[k]
-        old, new = one, two
-        for margin in range(DEPTH - 1, -1, -1):
-            sweep(k, old, new, margin)
-            old, new = new, old
-        field = old[k, start : start + rows].reshape(cells_x, stride, LANES)[:, 0:cells_y]
-        turned.append(field.reshape(cells, LANES).T)
-    turned = jnp.concatenate(turned, axis=0)
-    blocks = lanes // (2 * cols)
-    pair = turned.reshape(blocks, 2, cols, cells)
-    plain = pair.astype(BF16).reshape(blocks, 2 * cols, cells)
-    crossed = jnp.stack([-pair[:, 1], pair[:, 0]], axis=1)
-    crossed = crossed.astype(BF16).reshape(blocks, 2 * cols, cells)
-    groups = blocks // freqs
+        fields = []
+        for end in range(2):
+            source = wide.at[end, k]
+            old, new = source, one.at[end, k]
+            for x in range(1, DEPTH + 1):
+                sweep(source, gain.at[end], old, new, base(x) - 8, base(3 * DEPTH - x), stride)
+                old, new = new, (two.at[end, k] if x % 2 else one.at[end, k])
+            field = old[base(DEPTH) : base(deep)].reshape(DEPTH, stride, LANES)[:, 0:cells_y]
+            fields.append(field.reshape(DEPTH * cells_y, LANES))
+        fields.append(jnp.zeros((filler, LANES), F32))
+        turned.append(jnp.concatenate(fields, axis=0).T)
+    forms = both_forms(jnp.concatenate(turned, axis=0), cols)
+    groups = forms.shape[0] // freqs
+    blank = jnp.zeros((filler, all_sensors), BF16)
     for f in range(freqs):
-        ours = [
-            jnp.concatenate([plain[g * freqs + f], crossed[g * freqs + f]], axis=1)
-            for g in range(groups)
-        ]
-        left = jnp.concatenate(ours, axis=0)
+        right = []
+        for part in range(2):
+            for x in (0, cells_x - DEPTH):
+                rows_here = spectra_ref[f, part, x : x + DEPTH]
+                right.append(rows_here.reshape(DEPTH * cells_y, all_sensors))
+            right.append(blank)
         got = jnp.dot(
-            left, spectra_ref[f].reshape(2 * cells, all_sensors), preferred_element_type=F32
+            rows_of(forms, f, freqs), jnp.concatenate(right, axis=0), preferred_element_type=F32
         )
         for g in range(groups):
             at = (g * freqs + f) * 2 * cols
-            sums[at : at + 2 * cols] = got[g * 2 * cols : (g + 1) * 2 * cols]
+            sums[at : at + 2 * cols] = sums_ref[at : at + 2 * cols] + got[g * 2 * cols : (g + 1) * 2 * cols]
     back = sums[...].T
     halves, _, sensors, block = keep_ref.shape
     for g in range(groups):
@@ -296,6 +364,8 @@
     col_of = lane_ids(spectrum.shape[1]) % cols
     left = jnp.concatenate([jnp.where(col_of == c, spectrum, 0.0) for c in range(cols)], axis=0)
     returned = jnp.dot(left, table_ref[...], precision=HIGHEST, preferred_element_type=F32)
+    lane = lane_ids(LANES)
+    norms = jnp.zeros((1, LANES), F32)
     for c in range(cols):
         product = direction_ref[c] + noise_ref[...] * returned[c * sensors : (c + 1) * sensors]
         new_residual = residual_ref[c] - step_ref[c] * product
@@ -304,7 +374,8 @@
         norm = jnp.sum(
             jnp.sum(new_residual * new_residual, axis=0, keepdims=True), axis=1, keepdims=True
         )
-        norm_ref[:, c : c + 1] = jnp.broadcast_to(norm[None], (norm_ref.shape[0], 1, LANES))
+        norms = jnp.where(lane == c, norm, norms)
+    norm_ref[...] = jnp.broadcast_to(norms[None], norm_ref.shape)
 
 
 def direction_kernel(
@@ -316,8 +387,9 @@
     solution_out,
     residual_out,
     direction_out,
+    norm_out,
+    held,
     norm_ref,
-    held,
     sems,
 ):
     cols, sensors, steps = direction_ref.shape
@@ -328,13 +400,14 @@
     for copy in early:
         copy.start()
     norm = jnp.sum(norms_ref[...], axis=0)
+    norm_ref[...] = norm[0, 0:cols]
+    final = pltpu.make_async_copy(norm_ref, norm_out, sems.at[3])
+    final.start()
     for c in range(cols):
-        held[c] = residual_ref[c] + (norm[c : c + 1, 0:1] / old_ref[c]) * direction_ref[c]
+        held[c] = residual_ref[c] + (norm[:, c : c + 1] / old_ref[c]) * direction_ref[c]
     last = pltpu.make_async_copy(held, direction_out, sems.at[2])
     last.start()
-    for c in range(cols):
-        norm_ref[c] = jnp.max(norm[c : c + 1])
-    for copy in (*early, last):
+    for copy in (*early, last, final):
         copy.wait()
 
 
@@ -413,7 +486,8 @@
 
     edge = jax.ShapeDtypeStruct((DEPTH * cells_x, wide), BF16)
     end = jax.ShapeDtypeStruct((DEPTH * stride, wide), BF16)
-    total = (cells_x + 2 * DEPTH + 2) * stride
+    total = (cells_x + 4) * stride
+    strip = (3 * DEPTH + 2) * stride + 16
     slabs = width // LANES
     pieces = []
     for i in range(chunks):
@@ -429,7 +503,7 @@
             ),
             name="order",
         )(spectra, mine[:, at], other[:, at])
-        source, near_y, far_y, ends = pl.pallas_call(
+        source, far_y, near_y, ends = pl.pallas_call(
             functools.partial(adjoint_kernel, local_freqs, cols),
             out_shape=(
                 jax.ShapeDtypeStruct((slabs + 1, cells_x * stride, LANES), F32),
@@ -443,7 +517,7 @@
             name="adjoint",
         )(spectra, stacked, class_map.T)
         near_y, far_y = swap("sy", near_y, far_y)
-        near_x, far_x = pl.pallas_call(
+        far_x, near_x = pl.pallas_call(
             ends_kernel,
             out_shape=(end, end),
             in_specs=[VMEM] * 3,
@@ -451,8 +525,25 @@
             scratch_shapes=[pltpu.VMEM((DEPTH * stride + 16, wide), F32)],
             compiler_params=params(),
             name="ends",
-        )(ends, near_y, far_y)
+        )(ends, far_y, near_y)
         near_x, far_x = swap("sx", near_x, far_x)
+        sums = pl.pallas_call(
+            functools.partial(inner_kernel, local_freqs, cols),
+            out_shape=jax.ShapeDtypeStruct((width, all_sensors), F32),
+            in_specs=[VMEM] * 4 + [SMEM],
+            out_specs=VMEM,
+            scratch_shapes=[
+                pltpu.VMEM((slabs + 1, total, LANES), F32),
+                pltpu.VMEM((total, LANES), F32),
+                pltpu.VMEM((slabs, total, LANES), F32),
+                pltpu.VMEM((slabs, total, LANES), F32),
+            ],
+            compiler_params=params(),
+            cost_estimate=pl.CostEstimate(
+                flops=4 * spectra.size * width, bytes_accessed=2 * spectra.size, transcendentals=0
+            ),
+            name="inner",
+        )(spectra, source, far_y, near_y, class_kappa)
         pieces.append(
             pl.pallas_call(
                 functools.partial(field_kernel, local_freqs, cols),
@@ -460,18 +551,18 @@
                     jax.ShapeDtypeStruct((halves, group, sensors, block), F32),
                     jax.ShapeDtypeStruct((halves, group, sensors, block), BF16),
                 ),
-                in_specs=[VMEM] * 6 + [SMEM],
+                in_specs=[VMEM] * 7 + [SMEM],
                 out_specs=(VMEM,) * 2,
                 scratch_shapes=[
-                    pltpu.VMEM((slabs + 1, total, LANES), F32),
-                    pltpu.VMEM((total, LANES), F32),
-                    pltpu.VMEM((slabs, total, LANES), F32),
-                    pltpu.VMEM((slabs, total, LANES), F32),
+                    pltpu.VMEM((2, slabs + 1, strip, LANES), F32),
+                    pltpu.VMEM((2, strip, LANES), F32),
+                    pltpu.VMEM((2, slabs, strip, LANES), F32),
+                    pltpu.VMEM((2, slabs, strip, LANES), F32),
                     pltpu.VMEM((width, all_sensors), F32),
                 ],
                 compiler_params=params(),
                 name="field",
-            )(spectra, source, near_y, far_y, near_x, far_x, class_kappa)
+            )(spectra, source, sums, far_y, near_y, far_x, near_x, class_kappa)
         )
     keep = jnp.concatenate([piece[0] for piece in pieces], axis=1)
     send = jnp.concatenate([piece[1] for piece in pieces], axis=1)
@@ -479,7 +570,7 @@
     terms = exchange_half((keep + taken.astype(F32)).astype(BF16))
     new_solution, new_residual, norms = pl.pallas_call(
         residual_kernel,
-        out_shape=(like, like, jax.ShapeDtypeStruct((tiles, cols, LANES), F32)),
+        out_shape=(like, like, jax.ShapeDtypeStruct((tiles, 1, LANES), F32)),
         in_specs=[VMEM] * 6 + [SMEM],
         out_specs=(VMEM,) * 3,
         compiler_params=params(),
@@ -490,8 +581,8 @@
         direction_kernel,
         out_shape=(like, like, like, jax.ShapeDtypeStruct((cols,), F32)),
         in_specs=[VMEM] * 4 + [SMEM],
-        out_specs=(HBM, HBM, HBM, SMEM),
-        scratch_shapes=[held, pltpu.SemaphoreType.DMA((3,))],
+        out_specs=(HBM,) * 4,
+        scratch_shapes=[held, pltpu.VMEM((cols,), F32), pltpu.SemaphoreType.DMA((4,))],
         compiler_params=params(),
         name="direction",
     )(norms, new_solution, new_residual, direction, old_norm)

time: 64.8 us -> 62.2 us (0.960)
  blocking collectives: 40.5 us -> 37.8 us
  waiting for transfers between devices: 5.55 us -> 3.25 us
  starting transfers between devices: 6.14 us -> 7.86 us
  Pallas kernels: 11.4 us -> 12.1 us
    ppermute x2, starting transfers between devices: 1.02 us -> 4.95 us  [swap(): first = lax.ppermute(toward_partner, axis, near)]
    pallas_call x0 -> x1, Pallas kernels: none -> 3.24 us  [on_device(): pl.pallas_call(functools.partial(inner_kernel, local_freqs, cols), out_sh...]
    ppermute x2, waiting for transfers between devices: 3.21 us -> 0.91 us  [swap(): first = lax.ppermute(toward_partner, axis, near)]
    ppermute x1, starting transfers between devices: 3.82 us -> 1.58 us  [on_device(): taken = lax.ppermute(send, 'sy', partners('sy'))]
    all_to_all x2, blocking collectives: 30.6 us -> 28.5 us  [exchange_half(): lax.all_to_all(flat, ALL_AXES, 0, 0, axis_index_groups=groups, tiled=True)]
    pallas_call x1, Pallas kernels: 3.71 us -> 1.64 us  [on_device(): pl.pallas_call(functools.partial(field_kernel, local_freqs, cols), out_sh...]
  transfers between devices with their start and end apart: 6 -> 6, of which waited for: 4 -> 3; matrix products, arithmetic and copies ran while one was open for 0% -> 0% of each run, Pallas kernels for 0% -> 5%
where the time goes in v3:
time: 62.2 us; the launch traced here: 61.9 us
  blocking collectives  37.8 us (61%)
  Pallas kernels  12.1 us (19%)
  starting transfers between devices  7.86 us (13%)
  waiting for transfers between devices  3.25 us (5%)
  between operations  0.81 us (1%)
    all_to_all x2, blocking collectives, exchange_half(): lax.all_to_all(flat, ALL_AXES, 0, 0, axis_index_groups=groups, tiled=True)  28.5 us
    all_to_all x1, blocking collectives, on_device(): norms = lax.all_to_all(norms, GRID_AXES, 0, 0, tiled=True)  9.32 us
    ppermute x2, starting transfers between devices, swap(): first = lax.ppermute(toward_partner, axis, near)  4.95 us
    pallas_call x1, Pallas kernels, on_device(): pl.pallas_call(functools.partial(inner_kernel, local_freqs, cols), out_sh...  3.24 us
    pallas_call x1, Pallas kernels, on_device(): pl.pallas_call(functools.partial(adjoint_kernel, local_freqs, cols), out_...  2.5 us
    pallas_call x1, Pallas kernels, on_device(): pl.pallas_call(functools.partial(spectrum_kernel, halves, fq_blocks), out...  1.96 us
    pallas_call x1, Pallas kernels, on_device(): pl.pallas_call(functools.partial(field_kernel, local_freqs, cols), out_sh...  1.64 us
    ppermute x1, starting transfers between devices, on_device(): taken = lax.ppermute(send, 'sy', partners('sy'))  1.58 us
  transfers between devices with their start and end apart: 6, of which 3 were waited for; matrix products, arithmetic and copies ran while one was open for 0% of the time, Pallas kernels for 5%

profile of v3, /device:TPU:0, one launch (start us, length us, event | category | flops | bytes accessed | tf_op | source)
XLA Modules:
  0.0 61.9 jit_solution(5791250272892287393)
XLA Ops:
  0.6 0.0 copy-start.6
  0.6 2.0 %spectrum.1 = bf16[8,2,32,128]{3,2,1,0:T(8,128)(2,1)} custom-call(f32[8,32,32]{2,1,0:T(8,128)} %direction_ref.3, f32[32,32]{1,0:T(8,128)} %noise_ref.1, f32[32,256]{1,0:T(8,128)} %constant.4.clone.table_in), custom_call_target="tpu_custom_call" | custom-call | flops 8388608 | bytes 16777216 | tf_op jit(solution)/shard_map/spectrum/pallas_call | solution.py:467
  2.6 0.0 copy-start
  2.6 16.4 %all_to_all.15 = bf16[16,32,128]{2,1,0:T(8,128)(2,1)S(1)} all-to-all(bf16[16,32,128]{2,1,0:T(8,128)(2,1)} %bitcast.9), channel_id=1, replica_groups={{0,1,4,5,8,9,12,13,16,17,20,21,24,25,28,29},{2,3,6,7,10,11,14,15,18,19,..., dimensions={0} | all-to-all | bytes 262144 | tf_op jit(solution)/shard_map/all_to_all | solution.py:434
  19.0 0.0 copy-start.7
  19.0 0.0 collective-permute-start
  19.0 1.3 %collective-permute-done.other_ref = bf16[8,2,32,128]{3,2,1,0:T(8,128)(2,1)S(1)} collective-permute-done((bf16[8,2,32,128]{3,2,1,0:T(8,128)(2,1)S(1)}, bf16[8,2,32,128]{3,2,1,0:T(8,128)(2,1)S(1)}, u32[]{:S(2)}, u32[]{:S(2)}) %collective-permute-start) | collective-permute-done | bytes 131104 | tf_op jit(solution)/shard_map/ppermute | solution.py:485
  20.3 0.3 order.1.stacked_ref
  20.6 0.0 copy-done.6
  20.6 0.0 copy-done
  20.6 2.5 %adjoint.1 = (f32[3,768,128]{2,1,0:T(8,128)S(1)}, bf16[96,384]{1,0:T(8,128)(2,1)S(1)}, bf16[96,384]{1,0:T(8,128)(2,1)S(1)}, f32[2,72,384]{2,1,0:T(8,128)S(1)}) custom-call(bf16[8,2,32,16,512]{4,3,2,1,0:T(8,128)(2,1)S(1)} %copy-done, bf16[1024,256]{1,0:T(8,128)(2,1)S(1)} %order.1.stacked_ref, s32[16,32]{1,0:T(8,128)S(1)} %bitcast.8), custom_call_target="tpu_custom_call" | custom-call | tf_op jit(solution)/shard_map/adjoint/pallas_call | solution.py:506
  23.1 0.7 %collective-permute-start.1 = (bf16[96,384]{1,0:T(8,128)(2,1)S(1)}, bf16[96,384]{1,0:T(8,128)(2,1)S(1)}, u32[]{:S(2)}, u32[]{:S(2)}) collective-permute-start(bf16[96,384]{1,0:T(8,128)(2,1)S(1)} %get-tuple-element.16), channel_id=1, source_target_pairs={{2,4},{4,2},{3,5},{5,3},{10,12},{12,10},{11,13},{13,11},{18,20},{2... | collective-permute-start | bytes 221192 | tf_op jit(solution)/shard_map/ppermute | solution.py:418
  23.8 2.2 %collective-permute-start.2 = (bf16[96,384]{1,0:T(8,128)(2,1)S(1)}, bf16[96,384]{1,0:T(8,128)(2,1)S(1)}, u32[]{:S(2)}, u32[]{:S(2)}) collective-permute-start(bf16[96,384]{1,0:T(8,128)(2,1)S(1)} %get-tuple-element.17), channel_id=1, source_target_pairs={{0,2},{2,0},{4,6},{6,4},{1,3},{3,1},{5,7},{7,5},{8,10},{10,8},{12,... | collective-permute-start | bytes 221192 | tf_op jit(solution)/shard_map/ppermute | solution.py:419
  26.0 0.0 collective-permute-done.1.far_y_ref.far_ref
  26.0 0.9 %collective-permute-done.2.near_y_ref.near_ref = bf16[96,384]{1,0:T(8,128)(2,1)S(1)} collective-permute-done((bf16[96,384]{1,0:T(8,128)(2,1)S(1)}, bf16[96,384]{1,0:T(8,128)(2,1)S(1)}, u32[]{:S(2)}, u32[]{:S(2)}) %collective-permute-start.2) | collective-permute-done | bytes 73760 | tf_op jit(solution)/shard_map/ppermute | solution.py:419
  26.9 0.1 ends.1
  27.0 0.7 %collective-permute-start.3 = (bf16[72,384]{1,0:T(8,128)(2,1)S(1)}, bf16[72,384]{1,0:T(8,128)(2,1)S(1)}, u32[]{:S(2)}, u32[]{:S(2)}) collective-permute-start(bf16[72,384]{1,0:T(8,128)(2,1)S(1)} %get-tuple-element.19), channel_id=1, source_target_pairs={{8,16},{16,8},{9,17},{17,9},{10,18},{18,10},{11,19},{19,11},{12,20... | collective-permute-start | bytes 165896 | tf_op jit(solution)/shard_map/ppermute | solution.py:418
  27.7 2.8 %collective-permute-start.4 = (bf16[72,384]{1,0:T(8,128)(2,1)S(1)}, bf16[72,384]{1,0:T(8,128)(2,1)S(1)}, u32[]{:S(2)}, u32[]{:S(2)}) collective-permute-start(bf16[72,384]{1,0:T(8,128)(2,1)S(1)} %get-tuple-element.20), channel_id=1, source_target_pairs={{0,8},{8,0},{16,24},{24,16},{1,9},{9,1},{17,25},{25,17},{2,10},{10... | collective-permute-start | bytes 165896 | tf_op jit(solution)/shard_map/ppermute | solution.py:419
  30.5 0.0 copy-done.7
  30.5 3.2 %inner.1.sums_ref = f32[256,512]{1,0:T(8,128)S(1)} custom-call(bf16[8,2,32,16,512]{4,3,2,1,0:T(8,128)(2,1)S(1)} %copy-done, f32[3,768,128]{2,1,0:T(8,128)S(1)} %get-tuple-element.15.source_ref, bf16[96,384]{1,0:T(8,128)(2,1)S(1)} %collective-permute-done.1.far_y_ref.far_ref, bf16[96,384]{1,0:T(8,128)(2,1)S(1)} %collective-permute-done.2.near_y_ref.near_ref, ...), custom_call_target="tpu_custom_call" | custom-call | flops 4294967296 | bytes 8388608 | tf_op jit(solution)/shard_map/inner/pallas_call | solution.py:530
  33.7 0.0 copy-start.1
  33.7 0.0 copy-start.2
  33.7 0.0 copy-start.3
  33.7 0.0 copy-start.4
  33.7 0.0 copy-start.5
  33.8 0.0 copy-start.8
  33.8 0.0 copy-start.9
  33.8 0.0 collective-permute-done.3.far_x_ref
  33.8 0.0 collective-permute-done.4.near_x_ref
  33.8 1.6 %field.1 = (f32[8,2,32,128]{3,2,1,0:T(8,128)S(1)}, bf16[8,2,32,128]{3,2,1,0:T(8,128)(2,1)S(1)}) custom-call(bf16[8,2,32,16,512]{4,3,2,1,0:T(8,128)(2,1)S(1)} %copy-done, f32[3,768,128]{2,1,0:T(8,128)S(1)} %get-tuple-element.15.source_ref, f32[256,512]{1,0:T(8,128)S(1)} %inner.1.sums_ref, bf16[96,384]{1,0:T(8,128)(2,1)S(1)} %collective-permute-done.1.far_y_ref.far_ref, ...), custom_call_target="tpu_custom_call" | custom-call | tf_op jit(solution)/shard_map/field/pallas_call | solution.py:548
  35.4 1.6 %collective-permute-start.5 = (bf16[8,2,32,128]{3,2,1,0:T(8,128)(2,1)S(1)}, bf16[8,2,32,128]{3,2,1,0:T(8,128)(2,1)S(1)}, u32[]{:S(2)}, u32[]{:S(2)}) collective-permute-start(bf16[8,2,32,128]{3,2,1,0:T(8,128)(2,1)S(1)} %get-tuple-element.22), channel_id=1, source_target_pairs={{0,2},{2,0},{4,6},{6,4},{1,3},{3,1},{5,7},{7,5},{8,10},{10,8},{12,... | collective-permute-start | bytes 393224 | tf_op jit(solution)/shard_map/ppermute | solution.py:569
  37.0 1.0 %collective-permute-done.5 = bf16[8,2,32,128]{3,2,1,0:T(8,128)(2,1)S(1)} collective-permute-done((bf16[8,2,32,128]{3,2,1,0:T(8,128)(2,1)S(1)}, bf16[8,2,32,128]{3,2,1,0:T(8,128)(2,1)S(1)}, u32[]{:S(2)}, u32[]{:S(2)}) %collective-permute-start.5) | collective-permute-done | bytes 131104 | tf_op jit(solution)/shard_map/ppermute | solution.py:569
  38.1 12.1 %all_to_all.16 = bf16[16,32,128]{2,1,0:T(8,128)(2,1)S(1)} all-to-all(bf16[16,32,128]{2,1,0:T(8,128)(2,1)S(1)} %bitcast.10), channel_id=1, replica_groups={{0,1,4,5,8,9,12,13,16,17,20,21,24,25,28,29},{2,3,6,7,10,11,14,15,18,19,..., dimensions={0} | all-to-all | bytes 262144 | tf_op jit(solution)/shard_map/all_to_all | solution.py:434
  50.2 0.0 copy-done.1
  50.2 0.0 copy-done.2
  50.2 0.0 copy-done.3
  50.2 0.0 copy-done.4
  50.2 0.0 copy-done.5
  50.2 0.0 copy-done.8
  50.2 1.0 %residual.1 = (f32[8,32,32]{2,1,0:T(8,128)S(1)}, f32[8,32,32]{2,1,0:T(8,128)S(1)}, f32[16,1,128]{2,1,0:T(1,128)S(1)}) custom-call(bf16[8,2,32,128]{3,2,1,0:T(8,128)(2,1)S(1)} %bitcast.7, f32[256,32]{1,0:T(8,128)S(1)} %copy-done.4, f32[32,32]{1,0:T(8,128)S(1)} %copy-done.5, f32[8,32,32]{2,1,0:T(8,128)S(1)} %copy-done.2, f32[8,32,32]{2,1,0:T(8,128)S(1)} %copy-done.3, ...), custom_call_target="tpu_custom_call" | custom-call | tf_op jit(solution)/shard_map/residual/pallas_call | solution.py:571
  51.2 9.3 %all_to_all.17.norms_ref = f32[16,1,128]{2,1,0:T(1,128)S(1)} all-to-all(f32[16,1,128]{2,1,0:T(1,128)S(1)} %get-tuple-element.23), channel_id=1, replica_groups=mesh['sx'=4,'sy'=4,'fq'=2] {'sx','sy'}, dimensions={0} | all-to-all | bytes 16384 | tf_op jit(solution)/shard_map/all_to_all | solution.py:579
  60.5 0.0 copy-done.9
  60.5 1.4 %direction.1 = (f32[8,32,32]{2,1,0:T(8,128)}, f32[8,32,32]{2,1,0:T(8,128)}, f32[8,32,32]{2,1,0:T(8,128)}, f32[8]{0:T(128)}) custom-call(f32[16,1,128]{2,1,0:T(1,128)S(1)} %all_to_all.17.norms_ref, f32[8,32,32]{2,1,0:T(8,128)S(1)} %get-tuple-element.24.solution_ref, f32[8,32,32]{2,1,0:T(8,128)S(1)} %get-tuple-element.25.residual_ref, ...), custom_call_target="tpu_custom_call" | custom-call | tf_op jit(solution)/shard_map/direction/pallas_call | solution.py:580
  (1 shorter events, 0.0 us)
Async XLA Ops:
  0.6 20.0 %copy-start.6 = (s32[32,16]{0,1:T(8,128)S(1)}, s32[32,16]{0,1:T(8,128)}, u32[]{:S(2)}) copy-start(s32[32,16]{0,1:T(8,128)} %param.13) | copy-start | bytes 6148
  2.6 18.0 %copy-start = (bf16[8,2,32,16,512]{4,3,2,1,0:T(8,128)(2,1)S(1)}, bf16[8,2,32,16,512]{4,3,2,1,0:T(8,128)(2,1)}, u32[]{:S(2)}) copy-start(bf16[8,2,32,16,512]{4,3,2,1,0:T(8,128)(2,1)} %spectra_ref.5) | copy-start | bytes 25165828
  19.0 11.5 %copy-start.7 = (f32[8]{0:T(128)S(1)}, f32[8]{0:T(128)}, u32[]{:S(2)}) copy-start(f32[8]{0:T(128)} %kappa_ref.3) | copy-start | bytes 100
  19.0 1.3 %collective-permute-start = (bf16[8,2,32,128]{3,2,1,0:T(8,128)(2,1)S(1)}, bf16[8,2,32,128]{3,2,1,0:T(8,128)(2,1)S(1)}, u32[]{:S(2)}, u32[]{:S(2)}) collective-permute-start(bf16[8,2,32,128]{3,2,1,0:T(8,128)(2,1)S(1)} %bitcast.5), channel_id=1, source_target_pairs={{0,2},{2,0},{4,6},{6,4},{1,3},{3,1},{5,7},{7,5},{8,10},{10,8},{12,... | collective-permute-start | bytes 393224 | tf_op jit(solution)/shard_map/ppermute | solution.py:485
  23.1 2.8 %collective-permute-start.1 = (bf16[96,384]{1,0:T(8,128)(2,1)S(1)}, bf16[96,384]{1,0:T(8,128)(2,1)S(1)}, u32[]{:S(2)}, u32[]{:S(2)}) collective-permute-start(bf16[96,384]{1,0:T(8,128)(2,1)S(1)} %get-tuple-element.16), channel_id=1, source_target_pairs={{2,4},{4,2},{3,5},{5,3},{10,12},{12,10},{11,13},{13,11},{18,20},{2... | collective-permute-start | bytes 221192 | tf_op jit(solution)/shard_map/ppermute | solution.py:418
  23.8 3.1 %collective-permute-start.2 = (bf16[96,384]{1,0:T(8,128)(2,1)S(1)}, bf16[96,384]{1,0:T(8,128)(2,1)S(1)}, u32[]{:S(2)}, u32[]{:S(2)}) collective-permute-start(bf16[96,384]{1,0:T(8,128)(2,1)S(1)} %get-tuple-element.17), channel_id=1, source_target_pairs={{0,2},{2,0},{4,6},{6,4},{1,3},{3,1},{5,7},{7,5},{8,10},{10,8},{12,... | collective-permute-start | bytes 221192 | tf_op jit(solution)/shard_map/ppermute | solution.py:419
  27.0 6.8 %collective-permute-start.3 = (bf16[72,384]{1,0:T(8,128)(2,1)S(1)}, bf16[72,384]{1,0:T(8,128)(2,1)S(1)}, u32[]{:S(2)}, u32[]{:S(2)}) collective-permute-start(bf16[72,384]{1,0:T(8,128)(2,1)S(1)} %get-tuple-element.19), channel_id=1, source_target_pairs={{8,16},{16,8},{9,17},{17,9},{10,18},{18,10},{11,19},{19,11},{12,20... | collective-permute-start | bytes 165896 | tf_op jit(solution)/shard_map/ppermute | solution.py:418
  27.7 6.1 %collective-permute-start.4 = (bf16[72,384]{1,0:T(8,128)(2,1)S(1)}, bf16[72,384]{1,0:T(8,128)(2,1)S(1)}, u32[]{:S(2)}, u32[]{:S(2)}) collective-permute-start(bf16[72,384]{1,0:T(8,128)(2,1)S(1)} %get-tuple-element.20), channel_id=1, source_target_pairs={{0,8},{8,0},{16,24},{24,16},{1,9},{9,1},{17,25},{25,17},{2,10},{10... | collective-permute-start | bytes 165896 | tf_op jit(solution)/shard_map/ppermute | solution.py:419
  33.7 16.5 %copy-start.1 = (f32[8,32,32]{2,1,0:T(8,128)S(1)}, f32[8,32,32]{2,1,0:T(8,128)}, u32[]{:S(2)}) copy-start(f32[8,32,32]{2,1,0:T(8,128)} %direction_ref.3) | copy-start | bytes 98308
  33.7 16.5 %copy-start.2 = (f32[8,32,32]{2,1,0:T(8,128)S(1)}, f32[8,32,32]{2,1,0:T(8,128)}, u32[]{:S(2)}) copy-start(f32[8,32,32]{2,1,0:T(8,128)} %solution_ref.1) | copy-start | bytes 98308
  33.7 16.5 %copy-start.3 = (f32[8,32,32]{2,1,0:T(8,128)S(1)}, f32[8,32,32]{2,1,0:T(8,128)}, u32[]{:S(2)}) copy-start(f32[8,32,32]{2,1,0:T(8,128)} %residual_ref.1) | copy-start | bytes 98308
  33.7 16.4 %copy-start.4 = (f32[256,32]{1,0:T(8,128)S(1)}, f32[256,32]{1,0:T(8,128)}, u32[]{:S(2)}) copy-start(f32[256,32]{1,0:T(8,128)} %constant.5.clone.table_ref) | copy-start | bytes 98308
  33.7 16.4 %copy-start.5 = (f32[32,32]{1,0:T(8,128)S(1)}, f32[32,32]{1,0:T(8,128)}, u32[]{:S(2)}) copy-start(f32[32,32]{1,0:T(8,128)} %noise_ref.1) | copy-start | bytes 12292
  33.8 16.4 %copy-start.8 = (f32[8]{0:T(128)S(1)}, f32[8]{0:T(128)}, u32[]{:S(2)}) copy-start(f32[8]{0:T(128)} %step_ref.1) | copy-start | bytes 100
  33.8 26.8 %copy-start.9 = (f32[8]{0:T(128)S(1)}, f32[8]{0:T(128)}, u32[]{:S(2)}) copy-start(f32[8]{0:T(128)} %old_ref.1) | copy-start | bytes 100
  35.4 2.6 %collective-permute-start.5 = (bf16[8,2,32,128]{3,2,1,0:T(8,128)(2,1)S(1)}, bf16[8,2,32,128]{3,2,1,0:T(8,128)(2,1)S(1)}, u32[]{:S(2)}, u32[]{:S(2)}) collective-permute-start(bf16[8,2,32,128]{3,2,1,0:T(8,128)(2,1)S(1)} %get-tuple-element.22), channel_id=1, source_target_pairs={{0,2},{2,0},{4,6},{6,4},{1,3},{3,1},{5,7},{7,5},{8,10},{10,8},{12,... | collective-permute-start | bytes 393224 | tf_op jit(solution)/shard_map/ppermute | solution.py:569

commit v4 on v3

--- a/solution.py
+++ b/solution.py
@@ -208,31 +208,52 @@
     return jnp.concatenate([forms[b] for b in range(f, forms.shape[0], freqs)], axis=0)
 
 
+def own_kernel(source_ref, kappa_ref, scaled_ref, gain_ref):
+    slabs = scaled_ref.shape[0]
+    scale, gain_ref[...] = coefficients(source_ref[slabs], kappa_ref)
+    for k in range(slabs):
+        scaled_ref[k] = source_ref[k] * scale
+
+
 def inner_kernel(
-    freqs, cols, spectra_ref, source_ref, far_y_ref, near_y_ref, kappa_ref, sums_ref, wide, gain, one, two
+    freqs,
+    cols,
+    spectra_ref,
+    scaled_ref,
+    own_gain_ref,
+    far_y_ref,
+    near_y_ref,
+    kappa_ref,
+    sums_ref,
+    halo_ref,
+    wide,
+    gain,
+    one,
+    two,
 ):
     _, _, cells_x, cells_y, all_sensors = spectra_ref.shape
     cells = cells_x * cells_y
-    stride = source_ref.shape[1] // cells_x
-    slabs = one.shape[0]
+    slabs, rows, _ = scaled_ref.shape
+    stride = rows // cells_x
     start = 2 * stride
-    rows = cells_x * stride
-    total = wide.shape[1]
-    for k in range(slabs + 1):
-        at = slice(k * LANES, (k + 1) * LANES)
-        wide[k, 0:start] = jnp.zeros((start, LANES), F32)
-        wide[k, start + rows : total] = jnp.zeros((total - start - rows, LANES), F32)
-        wide[k, start : start + rows] = source_ref[k]
-        after, before = by_side("sy", far_y_ref[:, at].astype(F32), near_y_ref[:, at].astype(F32))
+    after, before = by_side("sy", far_y_ref[...].astype(F32), near_y_ref[...].astype(F32))
+    gain[start - 8 : start] = jnp.zeros((8, LANES), F32)
+    gain[start : start + rows] = own_gain_ref[...]
+    for k in range(slabs):
+        wide[k, start - 8 : start] = jnp.zeros((8, LANES), F32)
+        wide[k, start : start + rows] = scaled_ref[k]
+    for side, halo in ((0, before), (1, after)):
+        scale, halo_ref[side, slabs] = coefficients(halo[:, slabs * LANES :], kappa_ref)
+        for k in range(slabs):
+            halo_ref[side, k] = halo[:, k * LANES : (k + 1) * LANES] * scale
         for j in range(DEPTH):
             part = slice(j * cells_x, (j + 1) * cells_x)
-            wide[k, pl.ds(start + cells_y + j, cells_x, stride=stride), :] = after[part]
-            wide[k, pl.ds(start - DEPTH + j, cells_x, stride=stride), :] = before[part]
-    lo, hi = start - 8, start + rows
-    scale, gain[lo:hi] = coefficients(wide[slabs, lo:hi], kappa_ref)
+            to = pl.ds(start + j + (cells_y if side else -DEPTH), cells_x, stride=stride)
+            gain[to, :] = halo_ref[side, slabs, part]
+            for k in range(slabs):
+                wide[k, to, :] = halo_ref[side, k, part]
     turned = []
     for k in range(slabs):
-        wide[k, lo:hi] = wide[k, lo:hi] * scale
         old, new = wide.at[k], one.at[k]
         for x in range(1, DEPTH + 1):
             first, last = start + x * stride - 8, start + rows - x * stride
@@ -258,10 +279,10 @@
     freqs,
     cols,
     spectra_ref,
-    source_ref,
+    scaled_ref,
+    own_gain_ref,
+    halo_ref,
     sums_ref,
-    far_y_ref,
-    near_y_ref,
     far_x_ref,
     near_x_ref,
     kappa_ref,
@@ -274,39 +295,35 @@
     sums,
 ):
     _, _, cells_x, cells_y, all_sensors = spectra_ref.shape
-    stride = source_ref.shape[1] // cells_x
-    rows = cells_x * stride
-    slabs = one.shape[1]
+    slabs, rows, _ = scaled_ref.shape
+    stride = rows // cells_x
     start = stride + 8
     deep = 2 * DEPTH
-    total = wide.shape[2]
 
     def base(x):
         return start + x * stride
 
-    for k in range(slabs + 1):
-        at = slice(k * LANES, (k + 1) * LANES)
-        after, before = by_side("sy", far_y_ref[:, at].astype(F32), near_y_ref[:, at].astype(F32))
-        below, above = by_side("sx", far_x_ref[:, at].astype(F32), near_x_ref[:, at].astype(F32))
-        for end in range(2):
-            own, outer = (DEPTH, 0) if end == 0 else (0, deep)
-            inside = 0 if end == 0 else cells_x - deep
-            wide[end, k] = jnp.zeros((total, LANES), F32)
-            wide[end, k, base(own) : base(own + deep)] = source_ref[
-                k, inside * stride : (inside + deep) * stride
-            ]
+    below, above = by_side("sx", far_x_ref[...].astype(F32), near_x_ref[...].astype(F32))
+    for end in range(2):
+        own, outer = (DEPTH, 0) if end == 0 else (0, deep)
+        inside = 0 if end == 0 else cells_x - deep
+        beyond = above if end == 0 else below
+        scale, beyond_gain = coefficients(beyond[:, slabs * LANES :], kappa_ref)
+        for k in range(slabs + 1):
+            to = wide.at[end, k] if k < slabs else gain.at[end]
+            inner = scaled_ref.at[k] if k < slabs else own_gain_ref
+            to[base(0) - 8 : base(0)] = jnp.zeros((8, LANES), F32)
+            to[base(3 * DEPTH) - 8 : base(3 * DEPTH)] = jnp.zeros((8, LANES), F32)
+            to[base(own) : base(own + deep)] = inner[inside * stride : (inside + deep) * stride]
             for j in range(DEPTH):
                 part = slice(j * cells_x + inside, j * cells_x + inside + deep)
-                wide[end, k, pl.ds(base(own) + cells_y + j, deep, stride=stride), :] = after[part]
-                wide[end, k, pl.ds(base(own) - DEPTH + j, deep, stride=stride), :] = before[part]
-            wide[end, k, base(outer) - DEPTH : base(outer + DEPTH) - DEPTH] = above if end == 0 else below
-    lo, hi = base(0) - 8, base(3 * DEPTH)
+                to[pl.ds(base(own) - DEPTH + j, deep, stride=stride), :] = halo_ref[0, k, part]
+                to[pl.ds(base(own) + cells_y + j, deep, stride=stride), :] = halo_ref[1, k, part]
+            to[base(outer) - DEPTH : base(outer + DEPTH) - DEPTH] = (
+                beyond[:, k * LANES : (k + 1) * LANES] * scale if k < slabs else beyond_gain
+            )
     turned = []
     filler = -(deep * cells_y) % LANES
-    for end in range(2):
-        scale, gain[end, lo:hi] = coefficients(wide[end, slabs, lo:hi], kappa_ref)
-        for k in range(slabs):
-            wide[end, k, lo:hi] = wide[end, k, lo:hi] * scale
     for k in range(slabs):
         fields = []
         for end in range(2):
@@ -527,13 +544,27 @@
             name="ends",
         )(ends, far_y, near_y)
         near_x, far_x = swap("sx", near_x, far_x)
-        sums = pl.pallas_call(
+        scaled, own_gain = pl.pallas_call(
+            own_kernel,
+            out_shape=(
+                jax.ShapeDtypeStruct((slabs, cells_x * stride, LANES), F32),
+                jax.ShapeDtypeStruct((cells_x * stride, LANES), F32),
+            ),
+            in_specs=[VMEM, SMEM],
+            out_specs=(VMEM,) * 2,
+            compiler_params=params(),
+            name="own",
+        )(source, class_kappa)
+        sums, halo = pl.pallas_call(
             functools.partial(inner_kernel, local_freqs, cols),
-            out_shape=jax.ShapeDtypeStruct((width, all_sensors), F32),
-            in_specs=[VMEM] * 4 + [SMEM],
-            out_specs=VMEM,
+            out_shape=(
+                jax.ShapeDtypeStruct((width, all_sensors), F32),
+                jax.ShapeDtypeStruct((2, slabs + 1, DEPTH * cells_x, LANES), F32),
+            ),
+            in_specs=[VMEM] * 5 + [SMEM],
+            out_specs=(VMEM,) * 2,
             scratch_shapes=[
-                pltpu.VMEM((slabs + 1, total, LANES), F32),
+                pltpu.VMEM((slabs, total, LANES), F32),
                 pltpu.VMEM((total, LANES), F32),
                 pltpu.VMEM((slabs, total, LANES), F32),
                 pltpu.VMEM((slabs, total, LANES), F32),
@@ -543,7 +574,7 @@
                 flops=4 * spectra.size * width, bytes_accessed=2 * spectra.size, transcendentals=0
             ),
             name="inner",
-        )(spectra, source, far_y, near_y, class_kappa)
+        )(spectra, scaled, own_gain, far_y, near_y, class_kappa)
         pieces.append(
             pl.pallas_call(
                 functools.partial(field_kernel, local_freqs, cols),
@@ -554,7 +585,7 @@
                 in_specs=[VMEM] * 7 + [SMEM],
                 out_specs=(VMEM,) * 2,
                 scratch_shapes=[
-                    pltpu.VMEM((2, slabs + 1, strip, LANES), F32),
+                    pltpu.VMEM((2, slabs, strip, LANES), F32),
                     pltpu.VMEM((2, strip, LANES), F32),
                     pltpu.VMEM((2, slabs, strip, LANES), F32),
                     pltpu.VMEM((2, slabs, strip, LANES), F32),
@@ -562,7 +593,7 @@
                 ],
                 compiler_params=params(),
                 name="field",
-            )(spectra, source, sums, far_y, near_y, far_x, near_x, class_kappa)
+            )(spectra, scaled, own_gain, halo, sums, far_x, near_x, class_kappa)
         )
     keep = jnp.concatenate([piece[0] for piece in pieces], axis=1)
     send = jnp.concatenate([piece[1] for piece in pieces], axis=1)

time: 62.2 us -> 61.6 us (level)
  waiting for transfers between devices: 3.25 us -> 2.35 us
    ppermute x2, waiting for transfers between devices: 0.91 us -> 0.01 us  [swap(): first = lax.ppermute(toward_partner, axis, near)]
    pallas_call x0 -> x1, Pallas kernels: none -> 0.89 us  [on_device(): pl.pallas_call(own_kernel, out_shape=(jax.ShapeDtypeStruct((slabs, cells_...]
  transfers between devices with their start and end apart: 6 -> 6, of which waited for: 3 -> 2; matrix products, arithmetic and copies ran while one was open for 0% -> 0% of each run, Pallas kernels for 5% -> 6%
where the time goes in v4:
time: 61.6 us; the launch traced here: 61.3 us
  blocking collectives  37.8 us (61%)
  Pallas kernels  12.3 us (20%)
  starting transfers between devices  7.85 us (13%)
  waiting for transfers between devices  2.35 us (4%)
  between operations  0.83 us (1%)
    all_to_all x2, blocking collectives, exchange_half(): lax.all_to_all(flat, ALL_AXES, 0, 0, axis_index_groups=groups, tiled=True)  28.5 us
    all_to_all x1, blocking collectives, on_device(): norms = lax.all_to_all(norms, GRID_AXES, 0, 0, tiled=True)  9.32 us
    ppermute x2, starting transfers between devices, swap(): first = lax.ppermute(toward_partner, axis, near)  4.95 us
    pallas_call x1, Pallas kernels, on_device(): pl.pallas_call(functools.partial(inner_kernel, local_freqs, cols), out_sh...  2.79 us
    pallas_call x1, Pallas kernels, on_device(): pl.pallas_call(functools.partial(adjoint_kernel, local_freqs, cols), out_...  2.5 us
    pallas_call x1, Pallas kernels, on_device(): pl.pallas_call(functools.partial(spectrum_kernel, halves, fq_blocks), out...  1.96 us
    ppermute x1, starting transfers between devices, on_device(): taken = lax.ppermute(send, 'sy', partners('sy'))  1.57 us
    pallas_call x1, Pallas kernels, on_device(): pl.pallas_call(functools.partial(field_kernel, local_freqs, cols), out_sh...  1.45 us
  transfers between devices with their start and end apart: 6, of which 2 were waited for; matrix products, arithmetic and copies ran while one was open for 0% of the time, Pallas kernels for 6%

profile of v4, /device:TPU:0, one launch (start us, length us, event | category | flops | bytes accessed | tf_op | source)
XLA Modules:
  0.0 61.3 jit_solution(9833893183120318737)
XLA Ops:
  0.6 0.0 copy-start.6
  0.6 2.0 %spectrum.1 = bf16[8,2,32,128]{3,2,1,0:T(8,128)(2,1)} custom-call(f32[8,32,32]{2,1,0:T(8,128)} %direction_ref.3, f32[32,32]{1,0:T(8,128)} %noise_ref.1, f32[32,256]{1,0:T(8,128)} %constant.4.clone.table_in), custom_call_target="tpu_custom_call" | custom-call | flops 8388608 | bytes 16777216 | tf_op jit(solution)/shard_map/spectrum/pallas_call | solution.py:484
  2.6 0.0 copy-start
  2.6 16.4 %all_to_all.15 = bf16[16,32,128]{2,1,0:T(8,128)(2,1)S(1)} all-to-all(bf16[16,32,128]{2,1,0:T(8,128)(2,1)} %bitcast.9), channel_id=1, replica_groups={{0,1,4,5,8,9,12,13,16,17,20,21,24,25,28,29},{2,3,6,7,10,11,14,15,18,19,..., dimensions={0} | all-to-all | bytes 262144 | tf_op jit(solution)/shard_map/all_to_all | solution.py:451
  19.0 0.0 copy-start.7
  19.0 0.0 collective-permute-start
  19.0 1.3 %collective-permute-done.other_ref = bf16[8,2,32,128]{3,2,1,0:T(8,128)(2,1)S(1)} collective-permute-done((bf16[8,2,32,128]{3,2,1,0:T(8,128)(2,1)S(1)}, bf16[8,2,32,128]{3,2,1,0:T(8,128)(2,1)S(1)}, u32[]{:S(2)}, u32[]{:S(2)}) %collective-permute-start) | collective-permute-done | bytes 131104 | tf_op jit(solution)/shard_map/ppermute | solution.py:502
  20.3 0.3 order.1.stacked_ref
  20.6 0.0 copy-done.6
  20.6 0.0 copy-done
  20.6 2.5 %adjoint.1 = (f32[3,768,128]{2,1,0:T(8,128)S(1)}, bf16[96,384]{1,0:T(8,128)(2,1)S(1)}, bf16[96,384]{1,0:T(8,128)(2,1)S(1)}, f32[2,72,384]{2,1,0:T(8,128)S(1)}) custom-call(bf16[8,2,32,16,512]{4,3,2,1,0:T(8,128)(2,1)S(1)} %copy-done, bf16[1024,256]{1,0:T(8,128)(2,1)S(1)} %order.1.stacked_ref, s32[16,32]{1,0:T(8,128)S(1)} %bitcast.8), custom_call_target="tpu_custom_call" | custom-call | tf_op jit(solution)/shard_map/adjoint/pallas_call | solution.py:523
  23.1 0.7 %collective-permute-start.1 = (bf16[96,384]{1,0:T(8,128)(2,1)S(1)}, bf16[96,384]{1,0:T(8,128)(2,1)S(1)}, u32[]{:S(2)}, u32[]{:S(2)}) collective-permute-start(bf16[96,384]{1,0:T(8,128)(2,1)S(1)} %get-tuple-element.22), channel_id=1, source_target_pairs={{2,4},{4,2},{3,5},{5,3},{10,12},{12,10},{11,13},{13,11},{18,20},{2... | collective-permute-start | bytes 221192 | tf_op jit(solution)/shard_map/ppermute | solution.py:435
  23.8 2.2 %collective-permute-start.2 = (bf16[96,384]{1,0:T(8,128)(2,1)S(1)}, bf16[96,384]{1,0:T(8,128)(2,1)S(1)}, u32[]{:S(2)}, u32[]{:S(2)}) collective-permute-start(bf16[96,384]{1,0:T(8,128)(2,1)S(1)} %get-tuple-element.23), channel_id=1, source_target_pairs={{0,2},{2,0},{4,6},{6,4},{1,3},{3,1},{5,7},{7,5},{8,10},{10,8},{12,... | collective-permute-start | bytes 221192 | tf_op jit(solution)/shard_map/ppermute | solution.py:436
  26.0 0.0 copy-done.7
  26.0 0.9 %own.1 = (f32[2,768,128]{2,1,0:T(8,128)S(1)}, f32[768,128]{1,0:T(8,128)S(1)}) custom-call(f32[3,768,128]{2,1,0:T(8,128)S(1)} %get-tuple-element.19.source_ref, f32[8]{0:T(128)S(1)} %copy-done.7), custom_call_target="tpu_custom_call" | custom-call | tf_op jit(solution)/shard_map/own/pallas_call | solution.py:547
  26.9 0.0 collective-permute-done.1.far_y_ref.far_ref
  26.9 0.0 collective-permute-done.2.near_y_ref.near_ref
  26.9 0.1 ends.1
  27.0 0.7 %collective-permute-start.3 = (bf16[72,384]{1,0:T(8,128)(2,1)S(1)}, bf16[72,384]{1,0:T(8,128)(2,1)S(1)}, u32[]{:S(2)}, u32[]{:S(2)}) collective-permute-start(bf16[72,384]{1,0:T(8,128)(2,1)S(1)} %get-tuple-element.27), channel_id=1, source_target_pairs={{8,16},{16,8},{9,17},{17,9},{10,18},{18,10},{11,19},{19,11},{12,20... | collective-permute-start | bytes 165896 | tf_op jit(solution)/shard_map/ppermute | solution.py:435
  27.7 2.8 %collective-permute-start.4 = (bf16[72,384]{1,0:T(8,128)(2,1)S(1)}, bf16[72,384]{1,0:T(8,128)(2,1)S(1)}, u32[]{:S(2)}, u32[]{:S(2)}) collective-permute-start(bf16[72,384]{1,0:T(8,128)(2,1)S(1)} %get-tuple-element.28), channel_id=1, source_target_pairs={{0,8},{8,0},{16,24},{24,16},{1,9},{9,1},{17,25},{25,17},{2,10},{10... | collective-permute-start | bytes 165896 | tf_op jit(solution)/shard_map/ppermute | solution.py:436
  30.5 2.8 %inner.1 = (f32[256,512]{1,0:T(8,128)S(1)}, f32[2,3,96,128]{3,2,1,0:T(8,128)S(1)}) custom-call(bf16[8,2,32,16,512]{4,3,2,1,0:T(8,128)(2,1)S(1)} %copy-done, f32[2,768,128]{2,1,0:T(8,128)S(1)} %get-tuple-element.20.scaled_ref, f32[768,128]{1,0:T(8,128)S(1)} %get-tuple-element.21.own_gain_ref, bf16[96,384]{1,0:T(8,128)(2,1)S(1)} %collective-permute-done.1.far_y_ref.far_ref, ...), custom_call_target="tpu_custom_call" | custom-call | flops 4294967296 | bytes 8388608 | tf_op jit(solution)/shard_map/inner/pallas_call | solution.py:558
  33.3 0.0 copy-start.1
  33.3 0.0 copy-start.2
  33.3 0.0 copy-start.3
  33.3 0.0 copy-start.4
  33.3 0.0 copy-start.5
  33.3 0.0 copy-start.8
  33.3 0.0 copy-start.9
  33.3 0.0 collective-permute-done.3.far_x_ref
  33.4 0.0 collective-permute-done.4.near_x_ref
  33.4 1.4 %field.1 = (f32[8,2,32,128]{3,2,1,0:T(8,128)S(1)}, bf16[8,2,32,128]{3,2,1,0:T(8,128)(2,1)S(1)}) custom-call(bf16[8,2,32,16,512]{4,3,2,1,0:T(8,128)(2,1)S(1)} %copy-done, f32[2,768,128]{2,1,0:T(8,128)S(1)} %get-tuple-element.20.scaled_ref, f32[768,128]{1,0:T(8,128)S(1)} %get-tuple-element.21.own_gain_ref, f32[2,3,96,128]{3,2,1,0:T(8,128)S(1)} %get-tuple-element.24.halo_ref, ...), custom_call_target="tpu_custom_call" | custom-call | tf_op jit(solution)/shard_map/field/pallas_call | solution.py:579
  34.8 1.6 %collective-permute-start.5 = (bf16[8,2,32,128]{3,2,1,0:T(8,128)(2,1)S(1)}, bf16[8,2,32,128]{3,2,1,0:T(8,128)(2,1)S(1)}, u32[]{:S(2)}, u32[]{:S(2)}) collective-permute-start(bf16[8,2,32,128]{3,2,1,0:T(8,128)(2,1)S(1)} %get-tuple-element.30), channel_id=1, source_target_pairs={{0,2},{2,0},{4,6},{6,4},{1,3},{3,1},{5,7},{7,5},{8,10},{10,8},{12,... | collective-permute-start | bytes 393224 | tf_op jit(solution)/shard_map/ppermute | solution.py:600
  36.4 1.0 %collective-permute-done.5 = bf16[8,2,32,128]{3,2,1,0:T(8,128)(2,1)S(1)} collective-permute-done((bf16[8,2,32,128]{3,2,1,0:T(8,128)(2,1)S(1)}, bf16[8,2,32,128]{3,2,1,0:T(8,128)(2,1)S(1)}, u32[]{:S(2)}, u32[]{:S(2)}) %collective-permute-start.5) | collective-permute-done | bytes 131104 | tf_op jit(solution)/shard_map/ppermute | solution.py:600
  37.4 12.1 %all_to_all.16 = bf16[16,32,128]{2,1,0:T(8,128)(2,1)S(1)} all-to-all(bf16[16,32,128]{2,1,0:T(8,128)(2,1)S(1)} %bitcast.10), channel_id=1, replica_groups={{0,1,4,5,8,9,12,13,16,17,20,21,24,25,28,29},{2,3,6,7,10,11,14,15,18,19,..., dimensions={0} | all-to-all | bytes 262144 | tf_op jit(solution)/shard_map/all_to_all | solution.py:451
  49.5 0.0 copy-done.1
  49.5 0.0 copy-done.2
  49.5 0.0 copy-done.3
  49.5 0.0 copy-done.4
  49.5 0.0 copy-done.5
  49.6 0.0 copy-done.8
  49.6 1.0 %residual.1 = (f32[8,32,32]{2,1,0:T(8,128)S(1)}, f32[8,32,32]{2,1,0:T(8,128)S(1)}, f32[16,1,128]{2,1,0:T(1,128)S(1)}) custom-call(bf16[8,2,32,128]{3,2,1,0:T(8,128)(2,1)S(1)} %bitcast.7, f32[256,32]{1,0:T(8,128)S(1)} %copy-done.4, f32[32,32]{1,0:T(8,128)S(1)} %copy-done.5, f32[8,32,32]{2,1,0:T(8,128)S(1)} %copy-done.2, f32[8,32,32]{2,1,0:T(8,128)S(1)} %copy-done.3, ...), custom_call_target="tpu_custom_call" | custom-call | tf_op jit(solution)/shard_map/residual/pallas_call | solution.py:602
  50.6 9.3 %all_to_all.17.norms_ref = f32[16,1,128]{2,1,0:T(1,128)S(1)} all-to-all(f32[16,1,128]{2,1,0:T(1,128)S(1)} %get-tuple-element.31), channel_id=1, replica_groups=mesh['sx'=4,'sy'=4,'fq'=2] {'sx','sy'}, dimensions={0} | all-to-all | bytes 16384 | tf_op jit(solution)/shard_map/all_to_all | solution.py:610
  59.9 0.0 copy-done.9
  59.9 1.4 %direction.1 = (f32[8,32,32]{2,1,0:T(8,128)}, f32[8,32,32]{2,1,0:T(8,128)}, f32[8,32,32]{2,1,0:T(8,128)}, f32[8]{0:T(128)}) custom-call(f32[16,1,128]{2,1,0:T(1,128)S(1)} %all_to_all.17.norms_ref, f32[8,32,32]{2,1,0:T(8,128)S(1)} %get-tuple-element.32.solution_ref, f32[8,32,32]{2,1,0:T(8,128)S(1)} %get-tuple-element.33.residual_ref, ...), custom_call_target="tpu_custom_call" | custom-call | tf_op jit(solution)/shard_map/direction/pallas_call | solution.py:611
  (1 shorter events, 0.0 us)
Async XLA Ops:
  0.6 20.0 %copy-start.6 = (s32[32,16]{0,1:T(8,128)S(1)}, s32[32,16]{0,1:T(8,128)}, u32[]{:S(2)}) copy-start(s32[32,16]{0,1:T(8,128)} %param.13) | copy-start | bytes 6148
  2.6 18.0 %copy-start = (bf16[8,2,32,16,512]{4,3,2,1,0:T(8,128)(2,1)S(1)}, bf16[8,2,32,16,512]{4,3,2,1,0:T(8,128)(2,1)}, u32[]{:S(2)}) copy-start(bf16[8,2,32,16,512]{4,3,2,1,0:T(8,128)(2,1)} %spectra_ref.5) | copy-start | bytes 25165828
  19.0 7.0 %copy-start.7 = (f32[8]{0:T(128)S(1)}, f32[8]{0:T(128)}, u32[]{:S(2)}) copy-start(f32[8]{0:T(128)} %kappa_ref.5) | copy-start | bytes 100
  19.0 1.3 %collective-permute-start = (bf16[8,2,32,128]{3,2,1,0:T(8,128)(2,1)S(1)}, bf16[8,2,32,128]{3,2,1,0:T(8,128)(2,1)S(1)}, u32[]{:S(2)}, u32[]{:S(2)}) collective-permute-start(bf16[8,2,32,128]{3,2,1,0:T(8,128)(2,1)S(1)} %bitcast.5), channel_id=1, source_target_pairs={{0,2},{2,0},{4,6},{6,4},{1,3},{3,1},{5,7},{7,5},{8,10},{10,8},{12,... | collective-permute-start | bytes 393224 | tf_op jit(solution)/shard_map/ppermute | solution.py:502
  23.1 3.7 %collective-permute-start.1 = (bf16[96,384]{1,0:T(8,128)(2,1)S(1)}, bf16[96,384]{1,0:T(8,128)(2,1)S(1)}, u32[]{:S(2)}, u32[]{:S(2)}) collective-permute-start(bf16[96,384]{1,0:T(8,128)(2,1)S(1)} %get-tuple-element.22), channel_id=1, source_target_pairs={{2,4},{4,2},{3,5},{5,3},{10,12},{12,10},{11,13},{13,11},{18,20},{2... | collective-permute-start | bytes 221192 | tf_op jit(solution)/shard_map/ppermute | solution.py:435
  23.8 3.1 %collective-permute-start.2 = (bf16[96,384]{1,0:T(8,128)(2,1)S(1)}, bf16[96,384]{1,0:T(8,128)(2,1)S(1)}, u32[]{:S(2)}, u32[]{:S(2)}) collective-permute-start(bf16[96,384]{1,0:T(8,128)(2,1)S(1)} %get-tuple-element.23), channel_id=1, source_target_pairs={{0,2},{2,0},{4,6},{6,4},{1,3},{3,1},{5,7},{7,5},{8,10},{10,8},{12,... | collective-permute-start | bytes 221192 | tf_op jit(solution)/shard_map/ppermute | solution.py:436
  27.0 6.3 %collective-permute-start.3 = (bf16[72,384]{1,0:T(8,128)(2,1)S(1)}, bf16[72,384]{1,0:T(8,128)(2,1)S(1)}, u32[]{:S(2)}, u32[]{:S(2)}) collective-permute-start(bf16[72,384]{1,0:T(8,128)(2,1)S(1)} %get-tuple-element.27), channel_id=1, source_target_pairs={{8,16},{16,8},{9,17},{17,9},{10,18},{18,10},{11,19},{19,11},{12,20... | collective-permute-start | bytes 165896 | tf_op jit(solution)/shard_map/ppermute | solution.py:435
  27.7 5.7 %collective-permute-start.4 = (bf16[72,384]{1,0:T(8,128)(2,1)S(1)}, bf16[72,384]{1,0:T(8,128)(2,1)S(1)}, u32[]{:S(2)}, u32[]{:S(2)}) collective-permute-start(bf16[72,384]{1,0:T(8,128)(2,1)S(1)} %get-tuple-element.28), channel_id=1, source_target_pairs={{0,8},{8,0},{16,24},{24,16},{1,9},{9,1},{17,25},{25,17},{2,10},{10... | collective-permute-start | bytes 165896 | tf_op jit(solution)/shard_map/ppermute | solution.py:436
  33.3 16.3 %copy-start.1 = (f32[8,32,32]{2,1,0:T(8,128)S(1)}, f32[8,32,32]{2,1,0:T(8,128)}, u32[]{:S(2)}) copy-start(f32[8,32,32]{2,1,0:T(8,128)} %direction_ref.3) | copy-start | bytes 98308
  33.3 16.3 %copy-start.2 = (f32[8,32,32]{2,1,0:T(8,128)S(1)}, f32[8,32,32]{2,1,0:T(8,128)}, u32[]{:S(2)}) copy-start(f32[8,32,32]{2,1,0:T(8,128)} %solution_ref.1) | copy-start | bytes 98308
  33.3 16.2 %copy-start.3 = (f32[8,32,32]{2,1,0:T(8,128)S(1)}, f32[8,32,32]{2,1,0:T(8,128)}, u32[]{:S(2)}) copy-start(f32[8,32,32]{2,1,0:T(8,128)} %residual_ref.1) | copy-start | bytes 98308
  33.3 16.2 %copy-start.4 = (f32[256,32]{1,0:T(8,128)S(1)}, f32[256,32]{1,0:T(8,128)}, u32[]{:S(2)}) copy-start(f32[256,32]{1,0:T(8,128)} %constant.5.clone.table_ref) | copy-start | bytes 98308
  33.3 16.2 %copy-start.5 = (f32[32,32]{1,0:T(8,128)S(1)}, f32[32,32]{1,0:T(8,128)}, u32[]{:S(2)}) copy-start(f32[32,32]{1,0:T(8,128)} %noise_ref.1) | copy-start | bytes 12292
  33.3 16.2 %copy-start.8 = (f32[8]{0:T(128)S(1)}, f32[8]{0:T(128)}, u32[]{:S(2)}) copy-start(f32[8]{0:T(128)} %step_ref.1) | copy-start | bytes 100
  33.3 26.6 %copy-start.9 = (f32[8]{0:T(128)S(1)}, f32[8]{0:T(128)}, u32[]{:S(2)}) copy-start(f32[8]{0:T(128)} %old_ref.1) | copy-start | bytes 100
  34.8 2.6 %collective-permute-start.5 = (bf16[8,2,32,128]{3,2,1,0:T(8,128)(2,1)S(1)}, bf16[8,2,32,128]{3,2,1,0:T(8,128)(2,1)S(1)}, u32[]{:S(2)}, u32[]{:S(2)}) collective-permute-start(bf16[8,2,32,128]{3,2,1,0:T(8,128)(2,1)S(1)} %get-tuple-element.30), channel_id=1, source_target_pairs={{0,2},{2,0},{4,6},{6,4},{1,3},{3,1},{5,7},{7,5},{8,10},{10,8},{12,... | collective-permute-start | bytes 393224 | tf_op jit(solution)/shard_map/ppermute | solution.py:600

commit v5 on v4

--- a/solution.py
+++ b/solution.py
@@ -21,6 +21,7 @@
 VMEM = pl.BlockSpec(memory_space=pltpu.VMEM)
 SMEM = pl.BlockSpec(memory_space=pltpu.SMEM)
 HBM = pl.BlockSpec(memory_space=pltpu.HBM)
+ANY = pl.BlockSpec(memory_space=pl.ANY)
 
 
 def params(mib=24):
@@ -82,7 +83,7 @@
         out_ref[:, b] = jnp.broadcast_to(part[None], (tiles, sensors, block))
 
 
-def class_rows(class_ref):
+def class_kernel(class_ref, after_ref, out_ref):
     cells_y, cells_x = class_ref.shape
     cells = cells_x * cells_y
     row = lax.broadcasted_iota(jnp.int32, (cells, cells_x), 0)
@@ -95,7 +96,9 @@
     )
     at = lax.broadcasted_iota(jnp.int32, (cells, cells_y), 0) % cells_y
     own = (at == lax.broadcasted_iota(jnp.int32, (cells, cells_y), 1)).astype(F32)
-    return jnp.dot(by_row * own, jnp.ones((cells_y, LANES), F32), preferred_element_type=F32)
+    out_ref[...] = jnp.dot(
+        by_row * own, jnp.ones((cells_y, LANES), F32), preferred_element_type=F32
+    )
 
 
 def adjoint_of(part, stacked):
@@ -132,13 +135,12 @@
     stride = out_ref.shape[1] // cells_x
     lanes = stacked_ref.shape[1]
     freq_of = freq_lanes(lanes, cols, freqs)
-    classes = class_rows(class_ref)
     stacked = stacked_ref[...]
     acc = adjoint_of(spectra_ref[0], stacked)
     for f in range(1, freqs):
         acc = jnp.where(freq_of == f, adjoint_of(spectra_ref[f], stacked), acc)
     for k in range(out_ref.shape[0]):
-        part = classes if k * LANES == lanes else acc[:, k * LANES : (k + 1) * LANES]
+        part = class_ref[...] if k * LANES == lanes else acc[:, k * LANES : (k + 1) * LANES]
         for x in range(cells_x):
             base = x * stride
             out_ref[k, base : base + cells_y] = part[x * cells_y : (x + 1) * cells_y]
@@ -225,7 +227,6 @@
     near_y_ref,
     kappa_ref,
     sums_ref,
-    halo_ref,
     wide,
     gain,
     one,
@@ -243,15 +244,14 @@
         wide[k, start - 8 : start] = jnp.zeros((8, LANES), F32)
         wide[k, start : start + rows] = scaled_ref[k]
     for side, halo in ((0, before), (1, after)):
-        scale, halo_ref[side, slabs] = coefficients(halo[:, slabs * LANES :], kappa_ref)
-        for k in range(slabs):
-            halo_ref[side, k] = halo[:, k * LANES : (k + 1) * LANES] * scale
+        scale, halo_gain = coefficients(halo[:, slabs * LANES :], kappa_ref)
+        scaled = [halo[:, k * LANES : (k + 1) * LANES] * scale for k in range(slabs)]
         for j in range(DEPTH):
             part = slice(j * cells_x, (j + 1) * cells_x)
             to = pl.ds(start + j + (cells_y if side else -DEPTH), cells_x, stride=stride)
-            gain[to, :] = halo_ref[side, slabs, part]
+            gain[to, :] = halo_gain[part]
             for k in range(slabs):
-                wide[k, to, :] = halo_ref[side, k, part]
+                wide[k, to, :] = scaled[k][part]
     turned = []
     for k in range(slabs):
         old, new = wide.at[k], one.at[k]
@@ -279,9 +279,8 @@
     freqs,
     cols,
     spectra_ref,
-    scaled_ref,
-    own_gain_ref,
-    halo_ref,
+    wide_ref,
+    gain_ref,
     sums_ref,
     far_x_ref,
     near_x_ref,
@@ -295,8 +294,8 @@
     sums,
 ):
     _, _, cells_x, cells_y, all_sensors = spectra_ref.shape
-    slabs, rows, _ = scaled_ref.shape
-    stride = rows // cells_x
+    slabs = wide_ref.shape[0]
+    stride = far_x_ref.shape[0] // DEPTH
     start = stride + 8
     deep = 2 * DEPTH
 
@@ -311,14 +310,11 @@
         scale, beyond_gain = coefficients(beyond[:, slabs * LANES :], kappa_ref)
         for k in range(slabs + 1):
             to = wide.at[end, k] if k < slabs else gain.at[end]
-            inner = scaled_ref.at[k] if k < slabs else own_gain_ref
+            inner = wide_ref.at[k] if k < slabs else gain_ref
+            first = (2 + inside) * stride
             to[base(0) - 8 : base(0)] = jnp.zeros((8, LANES), F32)
             to[base(3 * DEPTH) - 8 : base(3 * DEPTH)] = jnp.zeros((8, LANES), F32)
-            to[base(own) : base(own + deep)] = inner[inside * stride : (inside + deep) * stride]
-            for j in range(DEPTH):
-                part = slice(j * cells_x + inside, j * cells_x + inside + deep)
-                to[pl.ds(base(own) - DEPTH + j, deep, stride=stride), :] = halo_ref[0, k, part]
-                to[pl.ds(base(own) + cells_y + j, deep, stride=stride), :] = halo_ref[1, k, part]
+            to[base(own) - 8 : base(own + deep)] = inner[first - 8 : first + deep * stride]
             to[base(outer) - DEPTH : base(outer + DEPTH) - DEPTH] = (
                 beyond[:, k * LANES : (k + 1) * LANES] * scale if k < slabs else beyond_gain
             )
@@ -500,6 +496,14 @@
     )(direction, noise_weight, forward)
     mine = exchange_half(spec)
     other = lax.ppermute(mine, "sy", partners("sy"))
+    classes = pl.pallas_call(
+        class_kernel,
+        out_shape=jax.ShapeDtypeStruct((cells, LANES), F32),
+        in_specs=[VMEM, ANY],
+        out_specs=VMEM,
+        compiler_params=params(),
+        name="classes",
+    )(class_map.T, mine)
 
     edge = jax.ShapeDtypeStruct((DEPTH * cells_x, wide), BF16)
     end = jax.ShapeDtypeStruct((DEPTH * stride, wide), BF16)
@@ -532,7 +536,7 @@
             out_specs=(VMEM,) * 4,
             compiler_params=params(),
             name="adjoint",
-        )(spectra, stacked, class_map.T)
+        )(spectra, stacked, classes)
         near_y, far_y = swap("sy", near_y, far_y)
         far_x, near_x = pl.pallas_call(
             ends_kernel,
@@ -555,17 +559,16 @@
             compiler_params=params(),
             name="own",
         )(source, class_kappa)
-        sums, halo = pl.pallas_call(
+        sums, around, gains = pl.pallas_call(
             functools.partial(inner_kernel, local_freqs, cols),
             out_shape=(
                 jax.ShapeDtypeStruct((width, all_sensors), F32),
-                jax.ShapeDtypeStruct((2, slabs + 1, DEPTH * cells_x, LANES), F32),
+                jax.ShapeDtypeStruct((slabs, total, LANES), F32),
+                jax.ShapeDtypeStruct((total, LANES), F32),
             ),
             in_specs=[VMEM] * 5 + [SMEM],
-            out_specs=(VMEM,) * 2,
+            out_specs=(VMEM,) * 3,
             scratch_shapes=[
-                pltpu.VMEM((slabs, total, LANES), F32),
-                pltpu.VMEM((total, LANES), F32),
                 pltpu.VMEM((slabs, total, LANES), F32),
                 pltpu.VMEM((slabs, total, LANES), F32),
             ],
@@ -582,7 +585,7 @@
                     jax.ShapeDtypeStruct((halves, group, sensors, block), F32),
                     jax.ShapeDtypeStruct((halves, group, sensors, block), BF16),
                 ),
-                in_specs=[VMEM] * 7 + [SMEM],
+                in_specs=[VMEM] * 6 + [SMEM],
                 out_specs=(VMEM,) * 2,
                 scratch_shapes=[
                     pltpu.VMEM((2, slabs, strip, LANES), F32),
@@ -593,7 +596,7 @@
                 ],
                 compiler_params=params(),
                 name="field",
-            )(spectra, scaled, own_gain, halo, sums, far_x, near_x, class_kappa)
+            )(spectra, around, gains, sums, far_x, near_x, class_kappa)
         )
     keep = jnp.concatenate([piece[0] for piece in pieces], axis=1)
     send = jnp.concatenate([piece[1] for piece in pieces], axis=1)

time: 61.6 us -> 61.4 us (level)
  waiting for transfers between devices: 2.35 us -> 1.33 us
  local copies, waits for them, and re-layouts: 0.06 us -> 0.75 us
    ppermute x1, waiting for transfers between devices: 1.35 us -> 0.33 us  [on_device(): other = lax.ppermute(mine, 'sy', partners('sy'))]
    unnamed x20, local copies, waits for them, and re-layouts: 0.06 us -> 0.75 us
  transfers between devices with their start and end apart: 6 -> 6, of which waited for: 2 -> 2; matrix products, arithmetic and copies ran while one was open for 0% -> 0% of each run, Pallas kernels for 6% -> 7%
where the time goes in v5:
time: 61.4 us; the launch traced here: 61.1 us
  blocking collectives  37.8 us (62%)
  Pallas kernels  12.5 us (20%)
  starting transfers between devices  7.9 us (13%)
  waiting for transfers between devices  1.33 us (2%)
  between operations  0.83 us (1%)
  local copies, waits for them, and re-layouts  0.75 us (1%)
    all_to_all x2, blocking collectives, exchange_half(): lax.all_to_all(flat, ALL_AXES, 0, 0, axis_index_groups=groups, tiled=True)  28.4 us
    all_to_all x1, blocking collectives, on_device(): norms = lax.all_to_all(norms, GRID_AXES, 0, 0, tiled=True)  9.32 us
    ppermute x2, starting transfers between devices, swap(): first = lax.ppermute(toward_partner, axis, near)  4.95 us
    pallas_call x1, Pallas kernels, on_device(): pl.pallas_call(functools.partial(inner_kernel, local_freqs, cols), out_sh...  2.82 us
    pallas_call x1, Pallas kernels, on_device(): pl.pallas_call(functools.partial(adjoint_kernel, local_freqs, cols), out_...  2.35 us
    pallas_call x1, Pallas kernels, on_device(): pl.pallas_call(functools.partial(spectrum_kernel, halves, fq_blocks), out...  1.95 us
    ppermute x1, starting transfers between devices, on_device(): taken = lax.ppermute(send, 'sy', partners('sy'))  1.62 us
    pallas_call x1, Pallas kernels, on_device(): pl.pallas_call(functools.partial(field_kernel, local_freqs, cols), out_sh...  1.42 us
  transfers between devices with their start and end apart: 6, of which 2 were waited for; matrix products, arithmetic and copies ran while one was open for 0% of the time, Pallas kernels for 7%

profile of v5, /device:TPU:0, one launch (start us, length us, event | category | flops | bytes accessed | tf_op | source)
XLA Modules:
  0.0 61.1 jit_solution(16774411739843440160)
XLA Ops:
  0.6 2.0 %spectrum.1 = bf16[8,2,32,128]{3,2,1,0:T(8,128)(2,1)} custom-call(f32[8,32,32]{2,1,0:T(8,128)} %direction_ref.3, f32[32,32]{1,0:T(8,128)} %noise_ref.1, f32[32,256]{1,0:T(8,128)} %constant.4.clone.table_in), custom_call_target="tpu_custom_call" | custom-call | flops 8388608 | bytes 16777216 | tf_op jit(solution)/shard_map/spectrum/pallas_call | solution.py:480
  2.6 0.0 copy-start
  2.6 16.4 %all_to_all.15 = bf16[16,32,128]{2,1,0:T(8,128)(2,1)S(1)} all-to-all(bf16[16,32,128]{2,1,0:T(8,128)(2,1)} %bitcast.10), channel_id=1, replica_groups={{0,1,4,5,8,9,12,13,16,17,20,21,24,25,28,29},{2,3,6,7,10,11,14,15,18,19,..., dimensions={0} | all-to-all | bytes 262144 | tf_op jit(solution)/shard_map/all_to_all | solution.py:447
  19.0 0.0 collective-permute-start
  19.0 0.0 copy-start.6
  19.0 0.7 %copy-done.6 = s32[32,16]{0,1:T(8,128)S(1)} copy-done((s32[32,16]{0,1:T(8,128)S(1)}, s32[32,16]{0,1:T(8,128)}, u32[]{:S(2)}) %copy-start.6) | copy-done | bytes 2072
  19.7 0.3 classes.1.class_ref
  20.0 0.0 copy-start.7
  20.0 0.3 collective-permute-done.other_ref
  20.3 0.3 order.1.stacked_ref
  20.6 0.0 copy-done
  20.6 2.4 %adjoint.1 = (f32[3,768,128]{2,1,0:T(8,128)S(1)}, bf16[96,384]{1,0:T(8,128)(2,1)S(1)}, bf16[96,384]{1,0:T(8,128)(2,1)S(1)}, f32[2,72,384]{2,1,0:T(8,128)S(1)}) custom-call(bf16[8,2,32,16,512]{4,3,2,1,0:T(8,128)(2,1)S(1)} %copy-done, bf16[1024,256]{1,0:T(8,128)(2,1)S(1)} %order.1.stacked_ref, f32[512,128]{1,0:T(8,128)S(1)} %classes.1.class_ref), custom_call_target="tpu_custom_call" | custom-call | tf_op jit(solution)/shard_map/adjoint/pallas_call | solution.py:527
  23.0 0.7 %collective-permute-start.1 = (bf16[96,384]{1,0:T(8,128)(2,1)S(1)}, bf16[96,384]{1,0:T(8,128)(2,1)S(1)}, u32[]{:S(2)}, u32[]{:S(2)}) collective-permute-start(bf16[96,384]{1,0:T(8,128)(2,1)S(1)} %get-tuple-element.23), channel_id=1, source_target_pairs={{2,4},{4,2},{3,5},{5,3},{10,12},{12,10},{11,13},{13,11},{18,20},{2... | collective-permute-start | bytes 221192 | tf_op jit(solution)/shard_map/ppermute | solution.py:431
  23.6 2.2 %collective-permute-start.2 = (bf16[96,384]{1,0:T(8,128)(2,1)S(1)}, bf16[96,384]{1,0:T(8,128)(2,1)S(1)}, u32[]{:S(2)}, u32[]{:S(2)}) collective-permute-start(bf16[96,384]{1,0:T(8,128)(2,1)S(1)} %get-tuple-element.24), channel_id=1, source_target_pairs={{0,2},{2,0},{4,6},{6,4},{1,3},{3,1},{5,7},{7,5},{8,10},{10,8},{12,... | collective-permute-start | bytes 221192 | tf_op jit(solution)/shard_map/ppermute | solution.py:432
  25.8 0.0 copy-done.7
  25.8 0.9 %own.1 = (f32[2,768,128]{2,1,0:T(8,128)S(1)}, f32[768,128]{1,0:T(8,128)S(1)}) custom-call(f32[3,768,128]{2,1,0:T(8,128)S(1)} %get-tuple-element.20.source_ref, f32[8]{0:T(128)S(1)} %copy-done.7), custom_call_target="tpu_custom_call" | custom-call | tf_op jit(solution)/shard_map/own/pallas_call | solution.py:551
  26.7 0.0 collective-permute-done.1.far_y_ref.far_ref
  26.7 0.0 collective-permute-done.2.near_y_ref.near_ref
  26.7 0.1 ends.1
  26.8 0.7 %collective-permute-start.3 = (bf16[72,384]{1,0:T(8,128)(2,1)S(1)}, bf16[72,384]{1,0:T(8,128)(2,1)S(1)}, u32[]{:S(2)}, u32[]{:S(2)}) collective-permute-start(bf16[72,384]{1,0:T(8,128)(2,1)S(1)} %get-tuple-element.29), channel_id=1, source_target_pairs={{8,16},{16,8},{9,17},{17,9},{10,18},{18,10},{11,19},{19,11},{12,20... | collective-permute-start | bytes 165896 | tf_op jit(solution)/shard_map/ppermute | solution.py:431
  27.5 2.8 %collective-permute-start.4 = (bf16[72,384]{1,0:T(8,128)(2,1)S(1)}, bf16[72,384]{1,0:T(8,128)(2,1)S(1)}, u32[]{:S(2)}, u32[]{:S(2)}) collective-permute-start(bf16[72,384]{1,0:T(8,128)(2,1)S(1)} %get-tuple-element.30), channel_id=1, source_target_pairs={{0,8},{8,0},{16,24},{24,16},{1,9},{9,1},{17,25},{25,17},{2,10},{10... | collective-permute-start | bytes 165896 | tf_op jit(solution)/shard_map/ppermute | solution.py:432
  30.3 2.8 %inner.1 = (f32[256,512]{1,0:T(8,128)S(1)}, f32[2,864,128]{2,1,0:T(8,128)S(1)}, f32[864,128]{1,0:T(8,128)S(1)}) custom-call(bf16[8,2,32,16,512]{4,3,2,1,0:T(8,128)(2,1)S(1)} %copy-done, f32[2,768,128]{2,1,0:T(8,128)S(1)} %get-tuple-element.21.scaled_ref, f32[768,128]{1,0:T(8,128)S(1)} %get-tuple-element.22.own_gain_ref, ...), custom_call_target="tpu_custom_call" | custom-call | flops 4294967296 | bytes 8388608 | tf_op jit(solution)/shard_map/inner/pallas_call | solution.py:562
  33.1 0.0 copy-start.1
  33.1 0.0 copy-start.2
  33.1 0.0 copy-start.3
  33.2 0.0 copy-start.4
  33.2 0.0 copy-start.5
  33.2 0.0 copy-start.8
  33.2 0.0 copy-start.9
  33.2 0.0 collective-permute-done.3.far_x_ref
  33.2 0.0 collective-permute-done.4.near_x_ref
  33.2 1.4 %field.1 = (f32[8,2,32,128]{3,2,1,0:T(8,128)S(1)}, bf16[8,2,32,128]{3,2,1,0:T(8,128)(2,1)S(1)}) custom-call(bf16[8,2,32,16,512]{4,3,2,1,0:T(8,128)(2,1)S(1)} %copy-done, f32[2,864,128]{2,1,0:T(8,128)S(1)} %get-tuple-element.25.wide_ref, f32[864,128]{1,0:T(8,128)S(1)} %get-tuple-element.26.gain_ref, f32[256,512]{1,0:T(8,128)S(1)} %get-tuple-element.27.sums_ref, ...), custom_call_target="tpu_custom_call" | custom-call | tf_op jit(solution)/shard_map/field/pallas_call | solution.py:582
  34.6 1.6 %collective-permute-start.5 = (bf16[8,2,32,128]{3,2,1,0:T(8,128)(2,1)S(1)}, bf16[8,2,32,128]{3,2,1,0:T(8,128)(2,1)S(1)}, u32[]{:S(2)}, u32[]{:S(2)}) collective-permute-start(bf16[8,2,32,128]{3,2,1,0:T(8,128)(2,1)S(1)} %get-tuple-element.32), channel_id=1, source_target_pairs={{0,2},{2,0},{4,6},{6,4},{1,3},{3,1},{5,7},{7,5},{8,10},{10,8},{12,... | collective-permute-start | bytes 393224 | tf_op jit(solution)/shard_map/ppermute | solution.py:603
  36.3 1.0 %collective-permute-done.5 = bf16[8,2,32,128]{3,2,1,0:T(8,128)(2,1)S(1)} collective-permute-done((bf16[8,2,32,128]{3,2,1,0:T(8,128)(2,1)S(1)}, bf16[8,2,32,128]{3,2,1,0:T(8,128)(2,1)S(1)}, u32[]{:S(2)}, u32[]{:S(2)}) %collective-permute-start.5) | collective-permute-done | bytes 131104 | tf_op jit(solution)/shard_map/ppermute | solution.py:603
  37.3 12.1 %all_to_all.16 = bf16[16,32,128]{2,1,0:T(8,128)(2,1)S(1)} all-to-all(bf16[16,32,128]{2,1,0:T(8,128)(2,1)S(1)} %bitcast.11), channel_id=1, replica_groups={{0,1,4,5,8,9,12,13,16,17,20,21,24,25,28,29},{2,3,6,7,10,11,14,15,18,19,..., dimensions={0} | all-to-all | bytes 262144 | tf_op jit(solution)/shard_map/all_to_all | solution.py:447
  49.4 0.0 copy-done.1
  49.4 0.0 copy-done.2
  49.4 0.0 copy-done.3
  49.4 0.0 copy-done.4
  49.4 0.0 copy-done.5
  49.4 0.0 copy-done.8
  49.4 1.0 %residual.1 = (f32[8,32,32]{2,1,0:T(8,128)S(1)}, f32[8,32,32]{2,1,0:T(8,128)S(1)}, f32[16,1,128]{2,1,0:T(1,128)S(1)}) custom-call(bf16[8,2,32,128]{3,2,1,0:T(8,128)(2,1)S(1)} %bitcast.8, f32[256,32]{1,0:T(8,128)S(1)} %copy-done.4, f32[32,32]{1,0:T(8,128)S(1)} %copy-done.5, f32[8,32,32]{2,1,0:T(8,128)S(1)} %copy-done.2, f32[8,32,32]{2,1,0:T(8,128)S(1)} %copy-done.3, ...), custom_call_target="tpu_custom_call" | custom-call | tf_op jit(solution)/shard_map/residual/pallas_call | solution.py:605
  50.4 9.3 %all_to_all.17.norms_ref = f32[16,1,128]{2,1,0:T(1,128)S(1)} all-to-all(f32[16,1,128]{2,1,0:T(1,128)S(1)} %get-tuple-element.33), channel_id=1, replica_groups=mesh['sx'=4,'sy'=4,'fq'=2] {'sx','sy'}, dimensions={0} | all-to-all | bytes 16384 | tf_op jit(solution)/shard_map/all_to_all | solution.py:613
  59.7 0.0 copy-done.9
  59.7 1.4 %direction.1 = (f32[8,32,32]{2,1,0:T(8,128)}, f32[8,32,32]{2,1,0:T(8,128)}, f32[8,32,32]{2,1,0:T(8,128)}, f32[8]{0:T(128)}) custom-call(f32[16,1,128]{2,1,0:T(1,128)S(1)} %all_to_all.17.norms_ref, f32[8,32,32]{2,1,0:T(8,128)S(1)} %get-tuple-element.34.solution_ref, f32[8,32,32]{2,1,0:T(8,128)S(1)} %get-tuple-element.35.residual_ref, ...), custom_call_target="tpu_custom_call" | custom-call | tf_op jit(solution)/shard_map/direction/pallas_call | solution.py:614
  (1 shorter events, 0.0 us)
Async XLA Ops:
  2.6 18.0 %copy-start = (bf16[8,2,32,16,512]{4,3,2,1,0:T(8,128)(2,1)S(1)}, bf16[8,2,32,16,512]{4,3,2,1,0:T(8,128)(2,1)}, u32[]{:S(2)}) copy-start(bf16[8,2,32,16,512]{4,3,2,1,0:T(8,128)(2,1)} %spectra_ref.5) | copy-start | bytes 25165828
  19.0 1.3 %collective-permute-start = (bf16[8,2,32,128]{3,2,1,0:T(8,128)(2,1)S(1)}, bf16[8,2,32,128]{3,2,1,0:T(8,128)(2,1)S(1)}, u32[]{:S(2)}, u32[]{:S(2)}) collective-permute-start(bf16[8,2,32,128]{3,2,1,0:T(8,128)(2,1)S(1)} %bitcast.5), channel_id=1, source_target_pairs={{0,2},{2,0},{4,6},{6,4},{1,3},{3,1},{5,7},{7,5},{8,10},{10,8},{12,... | collective-permute-start | bytes 393224 | tf_op jit(solution)/shard_map/ppermute | solution.py:498
  19.0 0.7 %copy-start.6 = (s32[32,16]{0,1:T(8,128)S(1)}, s32[32,16]{0,1:T(8,128)}, u32[]{:S(2)}) copy-start(s32[32,16]{0,1:T(8,128)} %param.13) | copy-start | bytes 6148
  20.0 5.8 %copy-start.7 = (f32[8]{0:T(128)S(1)}, f32[8]{0:T(128)}, u32[]{:S(2)}) copy-start(f32[8]{0:T(128)} %kappa_ref.5) | copy-start | bytes 100
  23.0 3.7 %collective-permute-start.1 = (bf16[96,384]{1,0:T(8,128)(2,1)S(1)}, bf16[96,384]{1,0:T(8,128)(2,1)S(1)}, u32[]{:S(2)}, u32[]{:S(2)}) collective-permute-start(bf16[96,384]{1,0:T(8,128)(2,1)S(1)} %get-tuple-element.23), channel_id=1, source_target_pairs={{2,4},{4,2},{3,5},{5,3},{10,12},{12,10},{11,13},{13,11},{18,20},{2... | collective-permute-start | bytes 221192 | tf_op jit(solution)/shard_map/ppermute | solution.py:431
  23.6 3.1 %collective-permute-start.2 = (bf16[96,384]{1,0:T(8,128)(2,1)S(1)}, bf16[96,384]{1,0:T(8,128)(2,1)S(1)}, u32[]{:S(2)}, u32[]{:S(2)}) collective-permute-start(bf16[96,384]{1,0:T(8,128)(2,1)S(1)} %get-tuple-element.24), channel_id=1, source_target_pairs={{0,2},{2,0},{4,6},{6,4},{1,3},{3,1},{5,7},{7,5},{8,10},{10,8},{12,... | collective-permute-start | bytes 221192 | tf_op jit(solution)/shard_map/ppermute | solution.py:432
  26.8 6.4 %collective-permute-start.3 = (bf16[72,384]{1,0:T(8,128)(2,1)S(1)}, bf16[72,384]{1,0:T(8,128)(2,1)S(1)}, u32[]{:S(2)}, u32[]{:S(2)}) collective-permute-start(bf16[72,384]{1,0:T(8,128)(2,1)S(1)} %get-tuple-element.29), channel_id=1, source_target_pairs={{8,16},{16,8},{9,17},{17,9},{10,18},{18,10},{11,19},{19,11},{12,20... | collective-permute-start | bytes 165896 | tf_op jit(solution)/shard_map/ppermute | solution.py:431
  27.5 5.7 %collective-permute-start.4 = (bf16[72,384]{1,0:T(8,128)(2,1)S(1)}, bf16[72,384]{1,0:T(8,128)(2,1)S(1)}, u32[]{:S(2)}, u32[]{:S(2)}) collective-permute-start(bf16[72,384]{1,0:T(8,128)(2,1)S(1)} %get-tuple-element.30), channel_id=1, source_target_pairs={{0,8},{8,0},{16,24},{24,16},{1,9},{9,1},{17,25},{25,17},{2,10},{10... | collective-permute-start | bytes 165896 | tf_op jit(solution)/shard_map/ppermute | solution.py:432
  33.1 16.2 %copy-start.1 = (f32[8,32,32]{2,1,0:T(8,128)S(1)}, f32[8,32,32]{2,1,0:T(8,128)}, u32[]{:S(2)}) copy-start(f32[8,32,32]{2,1,0:T(8,128)} %direction_ref.3) | copy-start | bytes 98308
  33.1 16.2 %copy-start.2 = (f32[8,32,32]{2,1,0:T(8,128)S(1)}, f32[8,32,32]{2,1,0:T(8,128)}, u32[]{:S(2)}) copy-start(f32[8,32,32]{2,1,0:T(8,128)} %solution_ref.1) | copy-start | bytes 98308
  33.1 16.2 %copy-start.3 = (f32[8,32,32]{2,1,0:T(8,128)S(1)}, f32[8,32,32]{2,1,0:T(8,128)}, u32[]{:S(2)}) copy-start(f32[8,32,32]{2,1,0:T(8,128)} %residual_ref.1) | copy-start | bytes 98308
  33.2 16.2 %copy-start.4 = (f32[256,32]{1,0:T(8,128)S(1)}, f32[256,32]{1,0:T(8,128)}, u32[]{:S(2)}) copy-start(f32[256,32]{1,0:T(8,128)} %constant.5.clone.table_ref) | copy-start | bytes 98308
  33.2 16.2 %copy-start.5 = (f32[32,32]{1,0:T(8,128)S(1)}, f32[32,32]{1,0:T(8,128)}, u32[]{:S(2)}) copy-start(f32[32,32]{1,0:T(8,128)} %noise_ref.1) | copy-start | bytes 12292
  33.2 16.2 %copy-start.8 = (f32[8]{0:T(128)S(1)}, f32[8]{0:T(128)}, u32[]{:S(2)}) copy-start(f32[8]{0:T(128)} %step_ref.1) | copy-start | bytes 100
  33.2 26.5 %copy-start.9 = (f32[8]{0:T(128)S(1)}, f32[8]{0:T(128)}, u32[]{:S(2)}) copy-start(f32[8]{0:T(128)} %old_ref.1) | copy-start | bytes 100
  34.6 2.6 %collective-permute-start.5 = (bf16[8,2,32,128]{3,2,1,0:T(8,128)(2,1)S(1)}, bf16[8,2,32,128]{3,2,1,0:T(8,128)(2,1)S(1)}, u32[]{:S(2)}, u32[]{:S(2)}) collective-permute-start(bf16[8,2,32,128]{3,2,1,0:T(8,128)(2,1)S(1)} %get-tuple-element.32), channel_id=1, source_target_pairs={{0,2},{2,0},{4,6},{6,4},{1,3},{3,1},{5,7},{7,5},{8,10},{10,8},{12,... | collective-permute-start | bytes 393224 | tf_op jit(solution)/shard_map/ppermute | solution.py:603

commit v6 on v5

--- a/solution.py
+++ b/solution.py
@@ -83,7 +83,7 @@
         out_ref[:, b] = jnp.broadcast_to(part[None], (tiles, sensors, block))
 
 
-def class_kernel(class_ref, after_ref, out_ref):
+def class_kernel(class_ref, after_ref, spectra_in, out_ref):
     cells_y, cells_x = class_ref.shape
     cells = cells_x * cells_y
     row = lax.broadcasted_iota(jnp.int32, (cells, cells_x), 0)
@@ -112,7 +112,7 @@
     return (lane_ids(lanes) // (2 * cols)) % freqs
 
 
-def order_kernel(cols, spectra_in, mine_ref, other_ref, stacked_ref):
+def stacked_of(cols, mine_ref, other_ref):
     halves, group, sensors, block = mine_ref.shape
     lanes = group * block
     parts = []
@@ -125,17 +125,17 @@
     turned = jnp.where(
         is_real, pltpu.roll(wide, lanes - cols, 1), -pltpu.roll(wide, cols, 1)
     ).astype(BF16)
-    stacked_ref[...] = jnp.concatenate([direct, turned], axis=0)
+    return jnp.concatenate([direct, turned], axis=0)
 
 
 def adjoint_kernel(
-    freqs, cols, spectra_ref, stacked_ref, class_ref, out_ref, far_ref, near_ref, ends_ref
+    freqs, cols, spectra_ref, mine_ref, other_ref, class_ref, out_ref, far_ref, near_ref, ends_ref
 ):
     _, _, cells_x, cells_y, all_sensors = spectra_ref.shape
     stride = out_ref.shape[1] // cells_x
-    lanes = stacked_ref.shape[1]
+    lanes = mine_ref.shape[1] * mine_ref.shape[3]
     freq_of = freq_lanes(lanes, cols, freqs)
-    stacked = stacked_ref[...]
+    stacked = stacked_of(cols, mine_ref, other_ref)
     acc = adjoint_of(spectra_ref[0], stacked)
     for f in range(1, freqs):
         acc = jnp.where(freq_of == f, adjoint_of(spectra_ref[f], stacked), acc)
@@ -499,11 +499,11 @@
     classes = pl.pallas_call(
         class_kernel,
         out_shape=jax.ShapeDtypeStruct((cells, LANES), F32),
-        in_specs=[VMEM, ANY],
+        in_specs=[VMEM, ANY, HBM],
         out_specs=VMEM,
-        compiler_params=params(),
+        compiler_params=params(48),
         name="classes",
-    )(class_map.T, mine)
+    )(class_map.T, mine, spectra)
 
     edge = jax.ShapeDtypeStruct((DEPTH * cells_x, wide), BF16)
     end = jax.ShapeDtypeStruct((DEPTH * stride, wide), BF16)
@@ -513,17 +513,6 @@
     pieces = []
     for i in range(chunks):
         at = slice(i * group, (i + 1) * group)
-        stacked = pl.pallas_call(
-            functools.partial(order_kernel, cols),
-            out_shape=jax.ShapeDtypeStruct((2 * all_sensors, width), BF16),
-            in_specs=[HBM, VMEM, VMEM],
-            out_specs=VMEM,
-            compiler_params=params(48),
-            cost_estimate=pl.CostEstimate(
-                flops=2 * spectra.size, bytes_accessed=4 * spectra.size, transcendentals=0
-            ),
-            name="order",
-        )(spectra, mine[:, at], other[:, at])
         source, far_y, near_y, ends = pl.pallas_call(
             functools.partial(adjoint_kernel, local_freqs, cols),
             out_shape=(
@@ -532,11 +521,11 @@
                 edge,
                 jax.ShapeDtypeStruct((2, DEPTH * stride, wide), F32),
             ),
-            in_specs=[VMEM] * 3,
+            in_specs=[VMEM] * 4,
             out_specs=(VMEM,) * 4,
             compiler_params=params(),
             name="adjoint",
-        )(spectra, stacked, classes)
+        )(spectra, mine[:, at], other[:, at], classes)
         near_y, far_y = swap("sy", near_y, far_y)
         far_x, near_x = pl.pallas_call(
             ends_kernel,

time: 61.4 us -> 61.2 us (level)
  no operation moved by 1% of the time
where the time goes in v6:
time: 61.2 us; the launch traced here: 60.8 us
  blocking collectives  37.8 us (62%)
  Pallas kernels  12.2 us (20%)
  starting transfers between devices  7.89 us (13%)
  waiting for transfers between devices  1.34 us (2%)
  between operations  0.81 us (1%)
  local copies, waits for them, and re-layouts  0.75 us (1%)
    all_to_all x2, blocking collectives, exchange_half(): lax.all_to_all(flat, ALL_AXES, 0, 0, axis_index_groups=groups, tiled=True)  28.5 us
    all_to_all x1, blocking collectives, on_device(): norms = lax.all_to_all(norms, GRID_AXES, 0, 0, tiled=True)  9.32 us
    ppermute x2, starting transfers between devices, swap(): first = lax.ppermute(toward_partner, axis, near)  4.95 us
    pallas_call x1, Pallas kernels, on_device(): pl.pallas_call(functools.partial(inner_kernel, local_freqs, cols), out_sh...  2.83 us
    pallas_call x1, Pallas kernels, on_device(): pl.pallas_call(functools.partial(adjoint_kernel, local_freqs, cols), out_...  2.37 us
    pallas_call x1, Pallas kernels, on_device(): pl.pallas_call(functools.partial(spectrum_kernel, halves, fq_blocks), out...  1.95 us
    ppermute x1, starting transfers between devices, on_device(): taken = lax.ppermute(send, 'sy', partners('sy'))  1.61 us
    pallas_call x1, Pallas kernels, on_device(): pl.pallas_call(functools.partial(field_kernel, local_freqs, cols), out_sh...  1.42 us
  transfers between devices with their start and end apart: 6, of which 2 were waited for; matrix products, arithmetic and copies ran while one was open for 0% of the time, Pallas kernels for 7%

profile of v6, /device:TPU:0, one launch (start us, length us, event | category | flops | bytes accessed | tf_op | source)
XLA Modules:
  0.0 60.8 jit_solution(11156922503084063347)
XLA Ops:
  0.6 2.0 %spectrum.1 = bf16[8,2,32,128]{3,2,1,0:T(8,128)(2,1)} custom-call(f32[8,32,32]{2,1,0:T(8,128)} %direction_ref.3, f32[32,32]{1,0:T(8,128)} %noise_ref.1, f32[32,256]{1,0:T(8,128)} %constant.4.clone.table_in), custom_call_target="tpu_custom_call" | custom-call | flops 8388608 | bytes 16777216 | tf_op jit(solution)/shard_map/spectrum/pallas_call | solution.py:480
  2.6 0.0 copy-start
  2.6 16.4 %all_to_all.15 = bf16[16,32,128]{2,1,0:T(8,128)(2,1)S(1)} all-to-all(bf16[16,32,128]{2,1,0:T(8,128)(2,1)} %bitcast.10), channel_id=1, replica_groups={{0,1,4,5,8,9,12,13,16,17,20,21,24,25,28,29},{2,3,6,7,10,11,14,15,18,19,..., dimensions={0} | all-to-all | bytes 262144 | tf_op jit(solution)/shard_map/all_to_all | solution.py:447
  19.0 0.0 collective-permute-start
  19.0 0.0 copy-start.6
  19.0 0.7 %copy-done.6 = s32[32,16]{0,1:T(8,128)S(1)} copy-done((s32[32,16]{0,1:T(8,128)S(1)}, s32[32,16]{0,1:T(8,128)}, u32[]{:S(2)}) %copy-start.6) | copy-done | bytes 2072
  19.7 0.0 copy-start.7
  19.7 0.3 classes.1.class_ref
  20.0 0.3 collective-permute-done.other_ref
  20.3 0.0 copy-done
  20.3 2.4 %adjoint.1 = (f32[3,768,128]{2,1,0:T(8,128)S(1)}, bf16[96,384]{1,0:T(8,128)(2,1)S(1)}, bf16[96,384]{1,0:T(8,128)(2,1)S(1)}, f32[2,72,384]{2,1,0:T(8,128)S(1)}) custom-call(bf16[8,2,32,16,512]{4,3,2,1,0:T(8,128)(2,1)S(1)} %copy-done, bf16[8,2,32,128]{3,2,1,0:T(8,128)(2,1)S(1)} %bitcast.7, bf16[8,2,32,128]{3,2,1,0:T(8,128)(2,1)S(1)} %collective-permute-done.other_ref, ...), custom_call_target="tpu_custom_call" | custom-call | tf_op jit(solution)/shard_map/adjoint/pallas_call | solution.py:516
  22.7 0.7 %collective-permute-start.1 = (bf16[96,384]{1,0:T(8,128)(2,1)S(1)}, bf16[96,384]{1,0:T(8,128)(2,1)S(1)}, u32[]{:S(2)}, u32[]{:S(2)}) collective-permute-start(bf16[96,384]{1,0:T(8,128)(2,1)S(1)} %get-tuple-element.23), channel_id=1, source_target_pairs={{2,4},{4,2},{3,5},{5,3},{10,12},{12,10},{11,13},{13,11},{18,20},{2... | collective-permute-start | bytes 221192 | tf_op jit(solution)/shard_map/ppermute | solution.py:431
  23.4 2.2 %collective-permute-start.2 = (bf16[96,384]{1,0:T(8,128)(2,1)S(1)}, bf16[96,384]{1,0:T(8,128)(2,1)S(1)}, u32[]{:S(2)}, u32[]{:S(2)}) collective-permute-start(bf16[96,384]{1,0:T(8,128)(2,1)S(1)} %get-tuple-element.24), channel_id=1, source_target_pairs={{0,2},{2,0},{4,6},{6,4},{1,3},{3,1},{5,7},{7,5},{8,10},{10,8},{12,... | collective-permute-start | bytes 221192 | tf_op jit(solution)/shard_map/ppermute | solution.py:432
  25.6 0.0 copy-done.7
  25.6 0.9 %own.1 = (f32[2,768,128]{2,1,0:T(8,128)S(1)}, f32[768,128]{1,0:T(8,128)S(1)}) custom-call(f32[3,768,128]{2,1,0:T(8,128)S(1)} %get-tuple-element.20.source_ref, f32[8]{0:T(128)S(1)} %copy-done.7), custom_call_target="tpu_custom_call" | custom-call | tf_op jit(solution)/shard_map/own/pallas_call | solution.py:540
  26.4 0.0 collective-permute-done.1.far_y_ref.far_ref
  26.5 0.0 collective-permute-done.2.near_y_ref.near_ref
  26.5 0.1 ends.1
  26.6 0.7 %collective-permute-start.3 = (bf16[72,384]{1,0:T(8,128)(2,1)S(1)}, bf16[72,384]{1,0:T(8,128)(2,1)S(1)}, u32[]{:S(2)}, u32[]{:S(2)}) collective-permute-start(bf16[72,384]{1,0:T(8,128)(2,1)S(1)} %get-tuple-element.29), channel_id=1, source_target_pairs={{8,16},{16,8},{9,17},{17,9},{10,18},{18,10},{11,19},{19,11},{12,20... | collective-permute-start | bytes 165896 | tf_op jit(solution)/shard_map/ppermute | solution.py:431
  27.3 2.8 %collective-permute-start.4 = (bf16[72,384]{1,0:T(8,128)(2,1)S(1)}, bf16[72,384]{1,0:T(8,128)(2,1)S(1)}, u32[]{:S(2)}, u32[]{:S(2)}) collective-permute-start(bf16[72,384]{1,0:T(8,128)(2,1)S(1)} %get-tuple-element.30), channel_id=1, source_target_pairs={{0,8},{8,0},{16,24},{24,16},{1,9},{9,1},{17,25},{25,17},{2,10},{10... | collective-permute-start | bytes 165896 | tf_op jit(solution)/shard_map/ppermute | solution.py:432
  30.0 2.8 %inner.1 = (f32[256,512]{1,0:T(8,128)S(1)}, f32[2,864,128]{2,1,0:T(8,128)S(1)}, f32[864,128]{1,0:T(8,128)S(1)}) custom-call(bf16[8,2,32,16,512]{4,3,2,1,0:T(8,128)(2,1)S(1)} %copy-done, f32[2,768,128]{2,1,0:T(8,128)S(1)} %get-tuple-element.21.scaled_ref, f32[768,128]{1,0:T(8,128)S(1)} %get-tuple-element.22.own_gain_ref, ...), custom_call_target="tpu_custom_call" | custom-call | flops 4294967296 | bytes 8388608 | tf_op jit(solution)/shard_map/inner/pallas_call | solution.py:551
  32.9 0.0 copy-start.1
  32.9 0.0 copy-start.2
  32.9 0.0 copy-start.3
  32.9 0.0 copy-start.4
  32.9 0.0 copy-start.5
  32.9 0.0 copy-start.8
  32.9 0.0 copy-start.9
  33.0 0.0 collective-permute-done.3.far_x_ref
  33.0 0.0 collective-permute-done.4.near_x_ref
  33.0 1.4 %field.1 = (f32[8,2,32,128]{3,2,1,0:T(8,128)S(1)}, bf16[8,2,32,128]{3,2,1,0:T(8,128)(2,1)S(1)}) custom-call(bf16[8,2,32,16,512]{4,3,2,1,0:T(8,128)(2,1)S(1)} %copy-done, f32[2,864,128]{2,1,0:T(8,128)S(1)} %get-tuple-element.25.wide_ref, f32[864,128]{1,0:T(8,128)S(1)} %get-tuple-element.26.gain_ref, f32[256,512]{1,0:T(8,128)S(1)} %get-tuple-element.27.sums_ref, ...), custom_call_target="tpu_custom_call" | custom-call | tf_op jit(solution)/shard_map/field/pallas_call | solution.py:571
  34.4 1.6 %collective-permute-start.5 = (bf16[8,2,32,128]{3,2,1,0:T(8,128)(2,1)S(1)}, bf16[8,2,32,128]{3,2,1,0:T(8,128)(2,1)S(1)}, u32[]{:S(2)}, u32[]{:S(2)}) collective-permute-start(bf16[8,2,32,128]{3,2,1,0:T(8,128)(2,1)S(1)} %get-tuple-element.32), channel_id=1, source_target_pairs={{0,2},{2,0},{4,6},{6,4},{1,3},{3,1},{5,7},{7,5},{8,10},{10,8},{12,... | collective-permute-start | bytes 393224 | tf_op jit(solution)/shard_map/ppermute | solution.py:592
  36.0 1.0 %collective-permute-done.5 = bf16[8,2,32,128]{3,2,1,0:T(8,128)(2,1)S(1)} collective-permute-done((bf16[8,2,32,128]{3,2,1,0:T(8,128)(2,1)S(1)}, bf16[8,2,32,128]{3,2,1,0:T(8,128)(2,1)S(1)}, u32[]{:S(2)}, u32[]{:S(2)}) %collective-permute-start.5) | collective-permute-done | bytes 131104 | tf_op jit(solution)/shard_map/ppermute | solution.py:592
  37.0 12.1 %all_to_all.16 = bf16[16,32,128]{2,1,0:T(8,128)(2,1)S(1)} all-to-all(bf16[16,32,128]{2,1,0:T(8,128)(2,1)S(1)} %bitcast.11), channel_id=1, replica_groups={{0,1,4,5,8,9,12,13,16,17,20,21,24,25,28,29},{2,3,6,7,10,11,14,15,18,19,..., dimensions={0} | all-to-all | bytes 262144 | tf_op jit(solution)/shard_map/all_to_all | solution.py:447
  49.1 0.0 copy-done.1
  49.1 0.0 copy-done.2
  49.1 0.0 copy-done.3
  49.1 0.0 copy-done.4
  49.1 0.0 copy-done.5
  49.1 0.0 copy-done.8
  49.2 1.0 %residual.1 = (f32[8,32,32]{2,1,0:T(8,128)S(1)}, f32[8,32,32]{2,1,0:T(8,128)S(1)}, f32[16,1,128]{2,1,0:T(1,128)S(1)}) custom-call(bf16[8,2,32,128]{3,2,1,0:T(8,128)(2,1)S(1)} %bitcast.8, f32[256,32]{1,0:T(8,128)S(1)} %copy-done.4, f32[32,32]{1,0:T(8,128)S(1)} %copy-done.5, f32[8,32,32]{2,1,0:T(8,128)S(1)} %copy-done.2, f32[8,32,32]{2,1,0:T(8,128)S(1)} %copy-done.3, ...), custom_call_target="tpu_custom_call" | custom-call | tf_op jit(solution)/shard_map/residual/pallas_call | solution.py:594
  50.2 9.3 %all_to_all.17.norms_ref = f32[16,1,128]{2,1,0:T(1,128)S(1)} all-to-all(f32[16,1,128]{2,1,0:T(1,128)S(1)} %get-tuple-element.33), channel_id=1, replica_groups=mesh['sx'=4,'sy'=4,'fq'=2] {'sx','sy'}, dimensions={0} | all-to-all | bytes 16384 | tf_op jit(solution)/shard_map/all_to_all | solution.py:602
  59.5 0.0 copy-done.9
  59.5 1.4 %direction.1 = (f32[8,32,32]{2,1,0:T(8,128)}, f32[8,32,32]{2,1,0:T(8,128)}, f32[8,32,32]{2,1,0:T(8,128)}, f32[8]{0:T(128)}) custom-call(f32[16,1,128]{2,1,0:T(1,128)S(1)} %all_to_all.17.norms_ref, f32[8,32,32]{2,1,0:T(8,128)S(1)} %get-tuple-element.34.solution_ref, f32[8,32,32]{2,1,0:T(8,128)S(1)} %get-tuple-element.35.residual_ref, ...), custom_call_target="tpu_custom_call" | custom-call | tf_op jit(solution)/shard_map/direction/pallas_call | solution.py:603
  (1 shorter events, 0.0 us)
Async XLA Ops:
  2.6 17.7 %copy-start = (bf16[8,2,32,16,512]{4,3,2,1,0:T(8,128)(2,1)S(1)}, bf16[8,2,32,16,512]{4,3,2,1,0:T(8,128)(2,1)}, u32[]{:S(2)}) copy-start(bf16[8,2,32,16,512]{4,3,2,1,0:T(8,128)(2,1)} %spectra_ref.5) | copy-start | bytes 25165828
  19.0 1.3 %collective-permute-start = (bf16[8,2,32,128]{3,2,1,0:T(8,128)(2,1)S(1)}, bf16[8,2,32,128]{3,2,1,0:T(8,128)(2,1)S(1)}, u32[]{:S(2)}, u32[]{:S(2)}) collective-permute-start(bf16[8,2,32,128]{3,2,1,0:T(8,128)(2,1)S(1)} %bitcast.5), channel_id=1, source_target_pairs={{0,2},{2,0},{4,6},{6,4},{1,3},{3,1},{5,7},{7,5},{8,10},{10,8},{12,... | collective-permute-start | bytes 393224 | tf_op jit(solution)/shard_map/ppermute | solution.py:498
  19.0 0.7 %copy-start.6 = (s32[32,16]{0,1:T(8,128)S(1)}, s32[32,16]{0,1:T(8,128)}, u32[]{:S(2)}) copy-start(s32[32,16]{0,1:T(8,128)} %param.13) | copy-start | bytes 6148
  19.7 5.9 %copy-start.7 = (f32[8]{0:T(128)S(1)}, f32[8]{0:T(128)}, u32[]{:S(2)}) copy-start(f32[8]{0:T(128)} %kappa_ref.5) | copy-start | bytes 100
  22.7 3.7 %collective-permute-start.1 = (bf16[96,384]{1,0:T(8,128)(2,1)S(1)}, bf16[96,384]{1,0:T(8,128)(2,1)S(1)}, u32[]{:S(2)}, u32[]{:S(2)}) collective-permute-start(bf16[96,384]{1,0:T(8,128)(2,1)S(1)} %get-tuple-element.23), channel_id=1, source_target_pairs={{2,4},{4,2},{3,5},{5,3},{10,12},{12,10},{11,13},{13,11},{18,20},{2... | collective-permute-start | bytes 221192 | tf_op jit(solution)/shard_map/ppermute | solution.py:431
  23.4 3.1 %collective-permute-start.2 = (bf16[96,384]{1,0:T(8,128)(2,1)S(1)}, bf16[96,384]{1,0:T(8,128)(2,1)S(1)}, u32[]{:S(2)}, u32[]{:S(2)}) collective-permute-start(bf16[96,384]{1,0:T(8,128)(2,1)S(1)} %get-tuple-element.24), channel_id=1, source_target_pairs={{0,2},{2,0},{4,6},{6,4},{1,3},{3,1},{5,7},{7,5},{8,10},{10,8},{12,... | collective-permute-start | bytes 221192 | tf_op jit(solution)/shard_map/ppermute | solution.py:432
  26.6 6.4 %collective-permute-start.3 = (bf16[72,384]{1,0:T(8,128)(2,1)S(1)}, bf16[72,384]{1,0:T(8,128)(2,1)S(1)}, u32[]{:S(2)}, u32[]{:S(2)}) collective-permute-start(bf16[72,384]{1,0:T(8,128)(2,1)S(1)} %get-tuple-element.29), channel_id=1, source_target_pairs={{8,16},{16,8},{9,17},{17,9},{10,18},{18,10},{11,19},{19,11},{12,20... | collective-permute-start | bytes 165896 | tf_op jit(solution)/shard_map/ppermute | solution.py:431
  27.3 5.7 %collective-permute-start.4 = (bf16[72,384]{1,0:T(8,128)(2,1)S(1)}, bf16[72,384]{1,0:T(8,128)(2,1)S(1)}, u32[]{:S(2)}, u32[]{:S(2)}) collective-permute-start(bf16[72,384]{1,0:T(8,128)(2,1)S(1)} %get-tuple-element.30), channel_id=1, source_target_pairs={{0,8},{8,0},{16,24},{24,16},{1,9},{9,1},{17,25},{25,17},{2,10},{10... | collective-permute-start | bytes 165896 | tf_op jit(solution)/shard_map/ppermute | solution.py:432
  32.9 16.2 %copy-start.1 = (f32[8,32,32]{2,1,0:T(8,128)S(1)}, f32[8,32,32]{2,1,0:T(8,128)}, u32[]{:S(2)}) copy-start(f32[8,32,32]{2,1,0:T(8,128)} %direction_ref.3) | copy-start | bytes 98308
  32.9 16.2 %copy-start.2 = (f32[8,32,32]{2,1,0:T(8,128)S(1)}, f32[8,32,32]{2,1,0:T(8,128)}, u32[]{:S(2)}) copy-start(f32[8,32,32]{2,1,0:T(8,128)} %solution_ref.1) | copy-start | bytes 98308
  32.9 16.2 %copy-start.3 = (f32[8,32,32]{2,1,0:T(8,128)S(1)}, f32[8,32,32]{2,1,0:T(8,128)}, u32[]{:S(2)}) copy-start(f32[8,32,32]{2,1,0:T(8,128)} %residual_ref.1) | copy-start | bytes 98308
  32.9 16.2 %copy-start.4 = (f32[256,32]{1,0:T(8,128)S(1)}, f32[256,32]{1,0:T(8,128)}, u32[]{:S(2)}) copy-start(f32[256,32]{1,0:T(8,128)} %constant.5.clone.table_ref) | copy-start | bytes 98308
  32.9 16.2 %copy-start.5 = (f32[32,32]{1,0:T(8,128)S(1)}, f32[32,32]{1,0:T(8,128)}, u32[]{:S(2)}) copy-start(f32[32,32]{1,0:T(8,128)} %noise_ref.1) | copy-start | bytes 12292
  32.9 16.2 %copy-start.8 = (f32[8]{0:T(128)S(1)}, f32[8]{0:T(128)}, u32[]{:S(2)}) copy-start(f32[8]{0:T(128)} %step_ref.1) | copy-start | bytes 100
  32.9 26.5 %copy-start.9 = (f32[8]{0:T(128)S(1)}, f32[8]{0:T(128)}, u32[]{:S(2)}) copy-start(f32[8]{0:T(128)} %old_ref.1) | copy-start | bytes 100
  34.4 2.6 %collective-permute-start.5 = (bf16[8,2,32,128]{3,2,1,0:T(8,128)(2,1)S(1)}, bf16[8,2,32,128]{3,2,1,0:T(8,128)(2,1)S(1)}, u32[]{:S(2)}, u32[]{:S(2)}) collective-permute-start(bf16[8,2,32,128]{3,2,1,0:T(8,128)(2,1)S(1)} %get-tuple-element.32), channel_id=1, source_target_pairs={{0,2},{2,0},{4,6},{6,4},{1,3},{3,1},{5,7},{7,5},{8,10},{10,8},{12,... | collective-permute-start | bytes 393224 | tf_op jit(solution)/shard_map/ppermute | solution.py:592

commit v7 on v6

--- a/solution.py
+++ b/solution.py
@@ -11,7 +11,6 @@
 
 SWEEPS = 4
 DEPTH = SWEEPS - 1
-HIGHEST = lax.Precision.HIGHEST
 F32 = jnp.float32
 BF16 = jnp.bfloat16
 GRID_AXES = ("sx", "sy")
@@ -37,7 +36,11 @@
     forward = np.repeat(pair.reshape(2 * freq_count, time_steps), local_cols, 0)
     doubling = np.where(np.arange(freq_count) == 0, 1.0, 2.0)[:, None, None]
     inverse = np.repeat((pair * doubling).reshape(2 * freq_count, time_steps), local_cols, 0)
-    return forward.T.astype(np.float32), inverse.astype(np.float32)
+    coarse = inverse.astype(jnp.bfloat16)
+    fine = (inverse - coarse.astype(np.float64)).astype(jnp.bfloat16)
+    rough = forward.T.astype(jnp.bfloat16)
+    rest = (forward.T - rough.astype(np.float64)).astype(jnp.bfloat16)
+    return np.stack([rough, rest]), np.concatenate([coarse, coarse, fine], axis=0)
 
 
 def by_side(axis, low, high):
@@ -69,9 +72,15 @@
         ((direction_in, direction_ref), (noise_in, noise_ref), (table_in, table_ref)), sems
     )
     cols, sensors, steps = direction_ref.shape
-    lanes = table_ref.shape[1]
+    lanes = table_ref.shape[2]
     weighted = (noise_ref[...][None] * direction_ref[...]).reshape(cols * sensors, steps)
-    full = jnp.dot(weighted, table_ref[...], precision=HIGHEST, preferred_element_type=F32)
+    coarse = weighted.astype(BF16)
+    fine = (weighted - coarse.astype(F32)).astype(BF16)
+    full = (
+        jnp.dot(fine, table_ref[0], preferred_element_type=F32)
+        + jnp.dot(coarse, table_ref[1], preferred_element_type=F32)
+        + jnp.dot(coarse, table_ref[0], preferred_element_type=F32)
+    )
     col_of = lane_ids(lanes) % cols
     spec = full[0:sensors]
     for col in range(1, cols):
@@ -376,7 +385,11 @@
     spectrum = jnp.concatenate(parts, axis=1)
     col_of = lane_ids(spectrum.shape[1]) % cols
     left = jnp.concatenate([jnp.where(col_of == c, spectrum, 0.0) for c in range(cols)], axis=0)
-    returned = jnp.dot(left, table_ref[...], precision=HIGHEST, preferred_element_type=F32)
+    coarse = left.astype(BF16)
+    fine = (left - coarse.astype(F32)).astype(BF16)
+    returned = jnp.dot(
+        jnp.concatenate([coarse, fine, coarse], axis=1), table_ref[...], preferred_element_type=F32
+    )
     lane = lane_ids(LANES)
     norms = jnp.zeros((1, LANES), F32)
     for c in range(cols):
@@ -485,7 +498,7 @@
         scratch_shapes=[
             held,
             pltpu.VMEM(noise_weight.shape, F32),
-            pltpu.VMEM(forward.shape, F32),
+            pltpu.VMEM(forward.shape, BF16),
             pltpu.SemaphoreType.DMA((3,)),
         ],
         compiler_params=params(62),

time: 61.2 us -> 61 us (level)
  no operation moved by 1% of the time
where the time goes in v7:
time: 61 us; the launch traced here: 60.6 us
  blocking collectives  37.8 us (62%)
  Pallas kernels  12 us (20%)
  starting transfers between devices  7.9 us (13%)
  waiting for transfers between devices  1.34 us (2%)
  between operations  0.81 us (1%)
  local copies, waits for them, and re-layouts  0.75 us (1%)
    all_to_all x2, blocking collectives, exchange_half(): lax.all_to_all(flat, ALL_AXES, 0, 0, axis_index_groups=groups, tiled=True)  28.5 us
    all_to_all x1, blocking collectives, on_device(): norms = lax.all_to_all(norms, GRID_AXES, 0, 0, tiled=True)  9.32 us
    ppermute x2, starting transfers between devices, swap(): first = lax.ppermute(toward_partner, axis, near)  4.95 us
    pallas_call x1, Pallas kernels, on_device(): pl.pallas_call(functools.partial(inner_kernel, local_freqs, cols), out_sh...  2.83 us
    pallas_call x1, Pallas kernels, on_device(): pl.pallas_call(functools.partial(adjoint_kernel, local_freqs, cols), out_...  2.37 us
    pallas_call x1, Pallas kernels, on_device(): pl.pallas_call(functools.partial(spectrum_kernel, halves, fq_blocks), out...  1.84 us
    ppermute x1, starting transfers between devices, on_device(): taken = lax.ppermute(send, 'sy', partners('sy'))  1.61 us
    pallas_call x1, Pallas kernels, on_device(): pl.pallas_call(functools.partial(field_kernel, local_freqs, cols), out_sh...  1.42 us
  transfers between devices with their start and end apart: 6, of which 2 were waited for; matrix products, arithmetic and copies ran while one was open for 0% of the time, Pallas kernels for 7%

profile of v7, /device:TPU:0, one launch (start us, length us, event | category | flops | bytes accessed | tf_op | source)
XLA Modules:
  0.0 60.6 jit_solution(6823040307044705618)
XLA Ops:
  0.6 1.8 %spectrum.1 = bf16[8,2,32,128]{3,2,1,0:T(8,128)(2,1)} custom-call(f32[8,32,32]{2,1,0:T(8,128)} %direction_ref.3, f32[32,32]{1,0:T(8,128)} %noise_ref.1, bf16[2,32,256]{2,1,0:T(8,128)(2,1)} %constant.4.clone.table_in), custom_call_target="tpu_custom_call" | custom-call | flops 8388608 | bytes 16777216 | tf_op jit(solution)/shard_map/spectrum/pallas_call | solution.py:493
  2.5 0.0 copy-start
  2.5 16.4 %all_to_all.15 = bf16[16,32,128]{2,1,0:T(8,128)(2,1)S(1)} all-to-all(bf16[16,32,128]{2,1,0:T(8,128)(2,1)} %bitcast.10), channel_id=1, replica_groups={{0,1,4,5,8,9,12,13,16,17,20,21,24,25,28,29},{2,3,6,7,10,11,14,15,18,19,..., dimensions={0} | all-to-all | bytes 262144 | tf_op jit(solution)/shard_map/all_to_all | solution.py:460
  18.9 0.0 collective-permute-start
  18.9 0.0 copy-start.6
  18.9 0.7 %copy-done.6 = s32[32,16]{0,1:T(8,128)S(1)} copy-done((s32[32,16]{0,1:T(8,128)S(1)}, s32[32,16]{0,1:T(8,128)}, u32[]{:S(2)}) %copy-start.6) | copy-done | bytes 2072
  19.6 0.0 copy-start.7
  19.6 0.3 classes.1.class_ref
  19.9 0.3 collective-permute-done.other_ref
  20.2 0.0 copy-done
  20.2 2.4 %adjoint.1 = (f32[3,768,128]{2,1,0:T(8,128)S(1)}, bf16[96,384]{1,0:T(8,128)(2,1)S(1)}, bf16[96,384]{1,0:T(8,128)(2,1)S(1)}, f32[2,72,384]{2,1,0:T(8,128)S(1)}) custom-call(bf16[8,2,32,16,512]{4,3,2,1,0:T(8,128)(2,1)S(1)} %copy-done, bf16[8,2,32,128]{3,2,1,0:T(8,128)(2,1)S(1)} %bitcast.7, bf16[8,2,32,128]{3,2,1,0:T(8,128)(2,1)S(1)} %collective-permute-done.other_ref, ...), custom_call_target="tpu_custom_call" | custom-call | tf_op jit(solution)/shard_map/adjoint/pallas_call | solution.py:529
  22.6 0.7 %collective-permute-start.1 = (bf16[96,384]{1,0:T(8,128)(2,1)S(1)}, bf16[96,384]{1,0:T(8,128)(2,1)S(1)}, u32[]{:S(2)}, u32[]{:S(2)}) collective-permute-start(bf16[96,384]{1,0:T(8,128)(2,1)S(1)} %get-tuple-element.23), channel_id=1, source_target_pairs={{2,4},{4,2},{3,5},{5,3},{10,12},{12,10},{11,13},{13,11},{18,20},{2... | collective-permute-start | bytes 221192 | tf_op jit(solution)/shard_map/ppermute | solution.py:444
  23.3 2.2 %collective-permute-start.2 = (bf16[96,384]{1,0:T(8,128)(2,1)S(1)}, bf16[96,384]{1,0:T(8,128)(2,1)S(1)}, u32[]{:S(2)}, u32[]{:S(2)}) collective-permute-start(bf16[96,384]{1,0:T(8,128)(2,1)S(1)} %get-tuple-element.24), channel_id=1, source_target_pairs={{0,2},{2,0},{4,6},{6,4},{1,3},{3,1},{5,7},{7,5},{8,10},{10,8},{12,... | collective-permute-start | bytes 221192 | tf_op jit(solution)/shard_map/ppermute | solution.py:445
  25.4 0.0 copy-done.7
  25.4 0.9 %own.1 = (f32[2,768,128]{2,1,0:T(8,128)S(1)}, f32[768,128]{1,0:T(8,128)S(1)}) custom-call(f32[3,768,128]{2,1,0:T(8,128)S(1)} %get-tuple-element.20.source_ref, f32[8]{0:T(128)S(1)} %copy-done.7), custom_call_target="tpu_custom_call" | custom-call | tf_op jit(solution)/shard_map/own/pallas_call | solution.py:553
  26.3 0.0 collective-permute-done.1.far_y_ref.far_ref
  26.3 0.0 collective-permute-done.2.near_y_ref.near_ref
  26.3 0.1 ends.1
  26.5 0.7 %collective-permute-start.3 = (bf16[72,384]{1,0:T(8,128)(2,1)S(1)}, bf16[72,384]{1,0:T(8,128)(2,1)S(1)}, u32[]{:S(2)}, u32[]{:S(2)}) collective-permute-start(bf16[72,384]{1,0:T(8,128)(2,1)S(1)} %get-tuple-element.29), channel_id=1, source_target_pairs={{8,16},{16,8},{9,17},{17,9},{10,18},{18,10},{11,19},{19,11},{12,20... | collective-permute-start | bytes 165896 | tf_op jit(solution)/shard_map/ppermute | solution.py:444
  27.1 2.8 %collective-permute-start.4 = (bf16[72,384]{1,0:T(8,128)(2,1)S(1)}, bf16[72,384]{1,0:T(8,128)(2,1)S(1)}, u32[]{:S(2)}, u32[]{:S(2)}) collective-permute-start(bf16[72,384]{1,0:T(8,128)(2,1)S(1)} %get-tuple-element.30), channel_id=1, source_target_pairs={{0,8},{8,0},{16,24},{24,16},{1,9},{9,1},{17,25},{25,17},{2,10},{10... | collective-permute-start | bytes 165896 | tf_op jit(solution)/shard_map/ppermute | solution.py:445
  29.9 2.8 %inner.1 = (f32[256,512]{1,0:T(8,128)S(1)}, f32[2,864,128]{2,1,0:T(8,128)S(1)}, f32[864,128]{1,0:T(8,128)S(1)}) custom-call(bf16[8,2,32,16,512]{4,3,2,1,0:T(8,128)(2,1)S(1)} %copy-done, f32[2,768,128]{2,1,0:T(8,128)S(1)} %get-tuple-element.21.scaled_ref, f32[768,128]{1,0:T(8,128)S(1)} %get-tuple-element.22.own_gain_ref, ...), custom_call_target="tpu_custom_call" | custom-call | flops 4294967296 | bytes 8388608 | tf_op jit(solution)/shard_map/inner/pallas_call | solution.py:564
  32.8 0.0 copy-start.1
  32.8 0.0 copy-start.2
  32.8 0.0 copy-start.3
  32.8 0.0 copy-start.4
  32.8 0.0 copy-start.5
  32.8 0.0 copy-start.8
  32.8 0.0 copy-start.9
  32.8 0.0 collective-permute-done.3.far_x_ref
  32.8 0.0 collective-permute-done.4.near_x_ref
  32.9 1.4 %field.1 = (f32[8,2,32,128]{3,2,1,0:T(8,128)S(1)}, bf16[8,2,32,128]{3,2,1,0:T(8,128)(2,1)S(1)}) custom-call(bf16[8,2,32,16,512]{4,3,2,1,0:T(8,128)(2,1)S(1)} %copy-done, f32[2,864,128]{2,1,0:T(8,128)S(1)} %get-tuple-element.25.wide_ref, f32[864,128]{1,0:T(8,128)S(1)} %get-tuple-element.26.gain_ref, f32[256,512]{1,0:T(8,128)S(1)} %get-tuple-element.27.sums_ref, ...), custom_call_target="tpu_custom_call" | custom-call | tf_op jit(solution)/shard_map/field/pallas_call | solution.py:584
  34.3 1.6 %collective-permute-start.5 = (bf16[8,2,32,128]{3,2,1,0:T(8,128)(2,1)S(1)}, bf16[8,2,32,128]{3,2,1,0:T(8,128)(2,1)S(1)}, u32[]{:S(2)}, u32[]{:S(2)}) collective-permute-start(bf16[8,2,32,128]{3,2,1,0:T(8,128)(2,1)S(1)} %get-tuple-element.32), channel_id=1, source_target_pairs={{0,2},{2,0},{4,6},{6,4},{1,3},{3,1},{5,7},{7,5},{8,10},{10,8},{12,... | collective-permute-start | bytes 393224 | tf_op jit(solution)/shard_map/ppermute | solution.py:605
  35.9 1.0 %collective-permute-done.5 = bf16[8,2,32,128]{3,2,1,0:T(8,128)(2,1)S(1)} collective-permute-done((bf16[8,2,32,128]{3,2,1,0:T(8,128)(2,1)S(1)}, bf16[8,2,32,128]{3,2,1,0:T(8,128)(2,1)S(1)}, u32[]{:S(2)}, u32[]{:S(2)}) %collective-permute-start.5) | collective-permute-done | bytes 131104 | tf_op jit(solution)/shard_map/ppermute | solution.py:605
  36.9 12.1 %all_to_all.16 = bf16[16,32,128]{2,1,0:T(8,128)(2,1)S(1)} all-to-all(bf16[16,32,128]{2,1,0:T(8,128)(2,1)S(1)} %bitcast.11), channel_id=1, replica_groups={{0,1,4,5,8,9,12,13,16,17,20,21,24,25,28,29},{2,3,6,7,10,11,14,15,18,19,..., dimensions={0} | all-to-all | bytes 262144 | tf_op jit(solution)/shard_map/all_to_all | solution.py:460
  49.0 0.0 copy-done.1
  49.0 0.0 copy-done.2
  49.0 0.0 copy-done.3
  49.0 0.0 copy-done.4
  49.0 0.0 copy-done.5
  49.0 0.0 copy-done.8
  49.0 0.9 %residual.1 = (f32[8,32,32]{2,1,0:T(8,128)S(1)}, f32[8,32,32]{2,1,0:T(8,128)S(1)}, f32[16,1,128]{2,1,0:T(1,128)S(1)}) custom-call(bf16[8,2,32,128]{3,2,1,0:T(8,128)(2,1)S(1)} %bitcast.8, bf16[768,32]{1,0:T(8,128)(2,1)S(1)} %copy-done.2, f32[32,32]{1,0:T(8,128)S(1)} %copy-done.5, f32[8,32,32]{2,1,0:T(8,128)S(1)} %copy-done.3, f32[8,32,32]{2,1,0:T(8,128)S(1)} %copy-done.4, ...), custom_call_target="tpu_custom_call" | custom-call | tf_op jit(solution)/shard_map/residual/pallas_call | solution.py:607
  49.9 9.3 %all_to_all.17.norms_ref = f32[16,1,128]{2,1,0:T(1,128)S(1)} all-to-all(f32[16,1,128]{2,1,0:T(1,128)S(1)} %get-tuple-element.33), channel_id=1, replica_groups=mesh['sx'=4,'sy'=4,'fq'=2] {'sx','sy'}, dimensions={0} | all-to-all | bytes 16384 | tf_op jit(solution)/shard_map/all_to_all | solution.py:615
  59.3 0.0 copy-done.9
  59.3 1.4 %direction.1 = (f32[8,32,32]{2,1,0:T(8,128)}, f32[8,32,32]{2,1,0:T(8,128)}, f32[8,32,32]{2,1,0:T(8,128)}, f32[8]{0:T(128)}) custom-call(f32[16,1,128]{2,1,0:T(1,128)S(1)} %all_to_all.17.norms_ref, f32[8,32,32]{2,1,0:T(8,128)S(1)} %get-tuple-element.34.solution_ref, f32[8,32,32]{2,1,0:T(8,128)S(1)} %get-tuple-element.35.residual_ref, ...), custom_call_target="tpu_custom_call" | custom-call | tf_op jit(solution)/shard_map/direction/pallas_call | solution.py:616
  (1 shorter events, 0.0 us)
Async XLA Ops:
  2.5 17.7 %copy-start = (bf16[8,2,32,16,512]{4,3,2,1,0:T(8,128)(2,1)S(1)}, bf16[8,2,32,16,512]{4,3,2,1,0:T(8,128)(2,1)}, u32[]{:S(2)}) copy-start(bf16[8,2,32,16,512]{4,3,2,1,0:T(8,128)(2,1)} %spectra_ref.5) | copy-start | bytes 25165828
  18.9 1.3 %collective-permute-start = (bf16[8,2,32,128]{3,2,1,0:T(8,128)(2,1)S(1)}, bf16[8,2,32,128]{3,2,1,0:T(8,128)(2,1)S(1)}, u32[]{:S(2)}, u32[]{:S(2)}) collective-permute-start(bf16[8,2,32,128]{3,2,1,0:T(8,128)(2,1)S(1)} %bitcast.5), channel_id=1, source_target_pairs={{0,2},{2,0},{4,6},{6,4},{1,3},{3,1},{5,7},{7,5},{8,10},{10,8},{12,... | collective-permute-start | bytes 393224 | tf_op jit(solution)/shard_map/ppermute | solution.py:511
  18.9 0.7 %copy-start.6 = (s32[32,16]{0,1:T(8,128)S(1)}, s32[32,16]{0,1:T(8,128)}, u32[]{:S(2)}) copy-start(s32[32,16]{0,1:T(8,128)} %param.13) | copy-start | bytes 6148
  19.6 5.9 %copy-start.7 = (f32[8]{0:T(128)S(1)}, f32[8]{0:T(128)}, u32[]{:S(2)}) copy-start(f32[8]{0:T(128)} %kappa_ref.5) | copy-start | bytes 100
  22.6 3.7 %collective-permute-start.1 = (bf16[96,384]{1,0:T(8,128)(2,1)S(1)}, bf16[96,384]{1,0:T(8,128)(2,1)S(1)}, u32[]{:S(2)}, u32[]{:S(2)}) collective-permute-start(bf16[96,384]{1,0:T(8,128)(2,1)S(1)} %get-tuple-element.23), channel_id=1, source_target_pairs={{2,4},{4,2},{3,5},{5,3},{10,12},{12,10},{11,13},{13,11},{18,20},{2... | collective-permute-start | bytes 221192 | tf_op jit(solution)/shard_map/ppermute | solution.py:444
  23.3 3.1 %collective-permute-start.2 = (bf16[96,384]{1,0:T(8,128)(2,1)S(1)}, bf16[96,384]{1,0:T(8,128)(2,1)S(1)}, u32[]{:S(2)}, u32[]{:S(2)}) collective-permute-start(bf16[96,384]{1,0:T(8,128)(2,1)S(1)} %get-tuple-element.24), channel_id=1, source_target_pairs={{0,2},{2,0},{4,6},{6,4},{1,3},{3,1},{5,7},{7,5},{8,10},{10,8},{12,... | collective-permute-start | bytes 221192 | tf_op jit(solution)/shard_map/ppermute | solution.py:445
  26.5 6.4 %collective-permute-start.3 = (bf16[72,384]{1,0:T(8,128)(2,1)S(1)}, bf16[72,384]{1,0:T(8,128)(2,1)S(1)}, u32[]{:S(2)}, u32[]{:S(2)}) collective-permute-start(bf16[72,384]{1,0:T(8,128)(2,1)S(1)} %get-tuple-element.29), channel_id=1, source_target_pairs={{8,16},{16,8},{9,17},{17,9},{10,18},{18,10},{11,19},{19,11},{12,20... | collective-permute-start | bytes 165896 | tf_op jit(solution)/shard_map/ppermute | solution.py:444
  27.1 5.7 %collective-permute-start.4 = (bf16[72,384]{1,0:T(8,128)(2,1)S(1)}, bf16[72,384]{1,0:T(8,128)(2,1)S(1)}, u32[]{:S(2)}, u32[]{:S(2)}) collective-permute-start(bf16[72,384]{1,0:T(8,128)(2,1)S(1)} %get-tuple-element.30), channel_id=1, source_target_pairs={{0,8},{8,0},{16,24},{24,16},{1,9},{9,1},{17,25},{25,17},{2,10},{10... | collective-permute-start | bytes 165896 | tf_op jit(solution)/shard_map/ppermute | solution.py:445
  32.8 16.2 %copy-start.1 = (f32[8,32,32]{2,1,0:T(8,128)S(1)}, f32[8,32,32]{2,1,0:T(8,128)}, u32[]{:S(2)}) copy-start(f32[8,32,32]{2,1,0:T(8,128)} %direction_ref.3) | copy-start | bytes 98308
  32.8 16.2 %copy-start.2 = (bf16[768,32]{1,0:T(8,128)(2,1)S(1)}, bf16[768,32]{1,0:T(8,128)(2,1)}, u32[]{:S(2)}) copy-start(bf16[768,32]{1,0:T(8,128)(2,1)} %constant.5.clone.table_ref) | copy-start | bytes 147460
  32.8 16.2 %copy-start.3 = (f32[8,32,32]{2,1,0:T(8,128)S(1)}, f32[8,32,32]{2,1,0:T(8,128)}, u32[]{:S(2)}) copy-start(f32[8,32,32]{2,1,0:T(8,128)} %solution_ref.1) | copy-start | bytes 98308
  32.8 16.2 %copy-start.4 = (f32[8,32,32]{2,1,0:T(8,128)S(1)}, f32[8,32,32]{2,1,0:T(8,128)}, u32[]{:S(2)}) copy-start(f32[8,32,32]{2,1,0:T(8,128)} %residual_ref.1) | copy-start | bytes 98308
  32.8 16.2 %copy-start.5 = (f32[32,32]{1,0:T(8,128)S(1)}, f32[32,32]{1,0:T(8,128)}, u32[]{:S(2)}) copy-start(f32[32,32]{1,0:T(8,128)} %noise_ref.1) | copy-start | bytes 12292
  32.8 16.2 %copy-start.8 = (f32[8]{0:T(128)S(1)}, f32[8]{0:T(128)}, u32[]{:S(2)}) copy-start(f32[8]{0:T(128)} %step_ref.1) | copy-start | bytes 100
  32.8 26.4 %copy-start.9 = (f32[8]{0:T(128)S(1)}, f32[8]{0:T(128)}, u32[]{:S(2)}) copy-start(f32[8]{0:T(128)} %old_ref.1) | copy-start | bytes 100
  34.3 2.6 %collective-permute-start.5 = (bf16[8,2,32,128]{3,2,1,0:T(8,128)(2,1)S(1)}, bf16[8,2,32,128]{3,2,1,0:T(8,128)(2,1)S(1)}, u32[]{:S(2)}, u32[]{:S(2)}) collective-permute-start(bf16[8,2,32,128]{3,2,1,0:T(8,128)(2,1)S(1)} %get-tuple-element.32), channel_id=1, source_target_pairs={{0,2},{2,0},{4,6},{6,4},{1,3},{3,1},{5,7},{7,5},{8,10},{10,8},{12,... | collective-permute-start | bytes 393224 | tf_op jit(solution)/shard_map/ppermute | solution.py:605

commit v8 on v7

--- a/solution.py
+++ b/solution.py
@@ -390,17 +390,16 @@
     returned = jnp.dot(
         jnp.concatenate([coarse, fine, coarse], axis=1), table_ref[...], preferred_element_type=F32
     )
-    lane = lane_ids(LANES)
-    norms = jnp.zeros((1, LANES), F32)
+    squares = []
     for c in range(cols):
         product = direction_ref[c] + noise_ref[...] * returned[c * sensors : (c + 1) * sensors]
         new_residual = residual_ref[c] - step_ref[c] * product
         new_residual_ref[c] = new_residual
         new_solution_ref[c] = solution_ref[c] + step_ref[c] * direction_ref[c]
-        norm = jnp.sum(
-            jnp.sum(new_residual * new_residual, axis=0, keepdims=True), axis=1, keepdims=True
-        )
-        norms = jnp.where(lane == c, norm, norms)
+        squares.append(jnp.sum(new_residual * new_residual, axis=0, keepdims=True))
+    norms = jnp.sum(jnp.concatenate(squares, axis=0), axis=1, keepdims=True)
+    on_lane = lax.broadcasted_iota(jnp.int32, (cols, LANES), 0) == lane_ids(LANES)
+    norms = jnp.sum(jnp.where(on_lane, norms, 0.0), axis=0, keepdims=True)
     norm_ref[...] = jnp.broadcast_to(norms[None], norm_ref.shape)
 
 

time: 61 us -> 61 us (level)
  no operation moved by 1% of the time
where the time goes in v8:
time: 61 us; the launch traced here: 60.6 us
  blocking collectives  37.8 us (62%)
  Pallas kernels  12 us (20%)
  starting transfers between devices  7.9 us (13%)
  waiting for transfers between devices  1.34 us (2%)
  between operations  0.81 us (1%)
  local copies, waits for them, and re-layouts  0.75 us (1%)
    all_to_all x2, blocking collectives, exchange_half(): lax.all_to_all(flat, ALL_AXES, 0, 0, axis_index_groups=groups, tiled=True)  28.5 us
    all_to_all x1, blocking collectives, on_device(): norms = lax.all_to_all(norms, GRID_AXES, 0, 0, tiled=True)  9.31 us
    ppermute x2, starting transfers between devices, swap(): first = lax.ppermute(toward_partner, axis, near)  4.95 us
    pallas_call x1, Pallas kernels, on_device(): pl.pallas_call(functools.partial(inner_kernel, local_freqs, cols), out_sh...  2.83 us
    pallas_call x1, Pallas kernels, on_device(): pl.pallas_call(functools.partial(adjoint_kernel, local_freqs, cols), out_...  2.37 us
    pallas_call x1, Pallas kernels, on_device(): pl.pallas_call(functools.partial(spectrum_kernel, halves, fq_blocks), out...  1.84 us
    ppermute x1, starting transfers between devices, on_device(): taken = lax.ppermute(send, 'sy', partners('sy'))  1.61 us
    pallas_call x1, Pallas kernels, on_device(): pl.pallas_call(functools.partial(field_kernel, local_freqs, cols), out_sh...  1.42 us
  transfers between devices with their start and end apart: 6, of which 2 were waited for; matrix products, arithmetic and copies ran while one was open for 0% of the time, Pallas kernels for 7%

profile of v8, /device:TPU:0, one launch (start us, length us, event | category | flops | bytes accessed | tf_op | source)
XLA Modules:
  0.0 60.6 jit_solution(13495479691509862381)
XLA Ops:
  0.6 1.8 %spectrum.1 = bf16[8,2,32,128]{3,2,1,0:T(8,128)(2,1)} custom-call(f32[8,32,32]{2,1,0:T(8,128)} %direction_ref.3, f32[32,32]{1,0:T(8,128)} %noise_ref.1, bf16[2,32,256]{2,1,0:T(8,128)(2,1)} %constant.4.clone.table_in), custom_call_target="tpu_custom_call" | custom-call | flops 8388608 | bytes 16777216 | tf_op jit(solution)/shard_map/spectrum/pallas_call | solution.py:492
  2.5 0.0 copy-start
  2.5 16.4 %all_to_all.15 = bf16[16,32,128]{2,1,0:T(8,128)(2,1)S(1)} all-to-all(bf16[16,32,128]{2,1,0:T(8,128)(2,1)} %bitcast.10), channel_id=1, replica_groups={{0,1,4,5,8,9,12,13,16,17,20,21,24,25,28,29},{2,3,6,7,10,11,14,15,18,19,..., dimensions={0} | all-to-all | bytes 262144 | tf_op jit(solution)/shard_map/all_to_all | solution.py:459
  18.9 0.0 collective-permute-start
  18.9 0.0 copy-start.6
  18.9 0.7 %copy-done.6 = s32[32,16]{0,1:T(8,128)S(1)} copy-done((s32[32,16]{0,1:T(8,128)S(1)}, s32[32,16]{0,1:T(8,128)}, u32[]{:S(2)}) %copy-start.6) | copy-done | bytes 2072
  19.6 0.0 copy-start.7
  19.6 0.3 classes.1.class_ref
  19.9 0.3 collective-permute-done.other_ref
  20.2 0.0 copy-done
  20.2 2.4 %adjoint.1 = (f32[3,768,128]{2,1,0:T(8,128)S(1)}, bf16[96,384]{1,0:T(8,128)(2,1)S(1)}, bf16[96,384]{1,0:T(8,128)(2,1)S(1)}, f32[2,72,384]{2,1,0:T(8,128)S(1)}) custom-call(bf16[8,2,32,16,512]{4,3,2,1,0:T(8,128)(2,1)S(1)} %copy-done, bf16[8,2,32,128]{3,2,1,0:T(8,128)(2,1)S(1)} %bitcast.7, bf16[8,2,32,128]{3,2,1,0:T(8,128)(2,1)S(1)} %collective-permute-done.other_ref, ...), custom_call_target="tpu_custom_call" | custom-call | tf_op jit(solution)/shard_map/adjoint/pallas_call | solution.py:528
  22.6 0.7 %collective-permute-start.1 = (bf16[96,384]{1,0:T(8,128)(2,1)S(1)}, bf16[96,384]{1,0:T(8,128)(2,1)S(1)}, u32[]{:S(2)}, u32[]{:S(2)}) collective-permute-start(bf16[96,384]{1,0:T(8,128)(2,1)S(1)} %get-tuple-element.23), channel_id=1, source_target_pairs={{2,4},{4,2},{3,5},{5,3},{10,12},{12,10},{11,13},{13,11},{18,20},{2... | collective-permute-start | bytes 221192 | tf_op jit(solution)/shard_map/ppermute | solution.py:443
  23.3 2.2 %collective-permute-start.2 = (bf16[96,384]{1,0:T(8,128)(2,1)S(1)}, bf16[96,384]{1,0:T(8,128)(2,1)S(1)}, u32[]{:S(2)}, u32[]{:S(2)}) collective-permute-start(bf16[96,384]{1,0:T(8,128)(2,1)S(1)} %get-tuple-element.24), channel_id=1, source_target_pairs={{0,2},{2,0},{4,6},{6,4},{1,3},{3,1},{5,7},{7,5},{8,10},{10,8},{12,... | collective-permute-start | bytes 221192 | tf_op jit(solution)/shard_map/ppermute | solution.py:444
  25.4 0.0 copy-done.7
  25.4 0.9 %own.1 = (f32[2,768,128]{2,1,0:T(8,128)S(1)}, f32[768,128]{1,0:T(8,128)S(1)}) custom-call(f32[3,768,128]{2,1,0:T(8,128)S(1)} %get-tuple-element.20.source_ref, f32[8]{0:T(128)S(1)} %copy-done.7), custom_call_target="tpu_custom_call" | custom-call | tf_op jit(solution)/shard_map/own/pallas_call | solution.py:552
  26.3 0.0 collective-permute-done.1.far_y_ref.far_ref
  26.3 0.0 collective-permute-done.2.near_y_ref.near_ref
  26.3 0.1 ends.1
  26.5 0.7 %collective-permute-start.3 = (bf16[72,384]{1,0:T(8,128)(2,1)S(1)}, bf16[72,384]{1,0:T(8,128)(2,1)S(1)}, u32[]{:S(2)}, u32[]{:S(2)}) collective-permute-start(bf16[72,384]{1,0:T(8,128)(2,1)S(1)} %get-tuple-element.29), channel_id=1, source_target_pairs={{8,16},{16,8},{9,17},{17,9},{10,18},{18,10},{11,19},{19,11},{12,20... | collective-permute-start | bytes 165896 | tf_op jit(solution)/shard_map/ppermute | solution.py:443
  27.1 2.8 %collective-permute-start.4 = (bf16[72,384]{1,0:T(8,128)(2,1)S(1)}, bf16[72,384]{1,0:T(8,128)(2,1)S(1)}, u32[]{:S(2)}, u32[]{:S(2)}) collective-permute-start(bf16[72,384]{1,0:T(8,128)(2,1)S(1)} %get-tuple-element.30), channel_id=1, source_target_pairs={{0,8},{8,0},{16,24},{24,16},{1,9},{9,1},{17,25},{25,17},{2,10},{10... | collective-permute-start | bytes 165896 | tf_op jit(solution)/shard_map/ppermute | solution.py:444
  29.9 2.8 %inner.1 = (f32[256,512]{1,0:T(8,128)S(1)}, f32[2,864,128]{2,1,0:T(8,128)S(1)}, f32[864,128]{1,0:T(8,128)S(1)}) custom-call(bf16[8,2,32,16,512]{4,3,2,1,0:T(8,128)(2,1)S(1)} %copy-done, f32[2,768,128]{2,1,0:T(8,128)S(1)} %get-tuple-element.21.scaled_ref, f32[768,128]{1,0:T(8,128)S(1)} %get-tuple-element.22.own_gain_ref, ...), custom_call_target="tpu_custom_call" | custom-call | flops 4294967296 | bytes 8388608 | tf_op jit(solution)/shard_map/inner/pallas_call | solution.py:563
  32.8 0.0 copy-start.1
  32.8 0.0 copy-start.2
  32.8 0.0 copy-start.3
  32.8 0.0 copy-start.4
  32.8 0.0 copy-start.5
  32.8 0.0 copy-start.8
  32.8 0.0 copy-start.9
  32.8 0.0 collective-permute-done.3.far_x_ref
  32.8 0.0 collective-permute-done.4.near_x_ref
  32.9 1.4 %field.1 = (f32[8,2,32,128]{3,2,1,0:T(8,128)S(1)}, bf16[8,2,32,128]{3,2,1,0:T(8,128)(2,1)S(1)}) custom-call(bf16[8,2,32,16,512]{4,3,2,1,0:T(8,128)(2,1)S(1)} %copy-done, f32[2,864,128]{2,1,0:T(8,128)S(1)} %get-tuple-element.25.wide_ref, f32[864,128]{1,0:T(8,128)S(1)} %get-tuple-element.26.gain_ref, f32[256,512]{1,0:T(8,128)S(1)} %get-tuple-element.27.sums_ref, ...), custom_call_target="tpu_custom_call" | custom-call | tf_op jit(solution)/shard_map/field/pallas_call | solution.py:583
  34.3 1.6 %collective-permute-start.5 = (bf16[8,2,32,128]{3,2,1,0:T(8,128)(2,1)S(1)}, bf16[8,2,32,128]{3,2,1,0:T(8,128)(2,1)S(1)}, u32[]{:S(2)}, u32[]{:S(2)}) collective-permute-start(bf16[8,2,32,128]{3,2,1,0:T(8,128)(2,1)S(1)} %get-tuple-element.32), channel_id=1, source_target_pairs={{0,2},{2,0},{4,6},{6,4},{1,3},{3,1},{5,7},{7,5},{8,10},{10,8},{12,... | collective-permute-start | bytes 393224 | tf_op jit(solution)/shard_map/ppermute | solution.py:604
  35.9 1.0 %collective-permute-done.5 = bf16[8,2,32,128]{3,2,1,0:T(8,128)(2,1)S(1)} collective-permute-done((bf16[8,2,32,128]{3,2,1,0:T(8,128)(2,1)S(1)}, bf16[8,2,32,128]{3,2,1,0:T(8,128)(2,1)S(1)}, u32[]{:S(2)}, u32[]{:S(2)}) %collective-permute-start.5) | collective-permute-done | bytes 131104 | tf_op jit(solution)/shard_map/ppermute | solution.py:604
  36.9 12.1 %all_to_all.16 = bf16[16,32,128]{2,1,0:T(8,128)(2,1)S(1)} all-to-all(bf16[16,32,128]{2,1,0:T(8,128)(2,1)S(1)} %bitcast.11), channel_id=1, replica_groups={{0,1,4,5,8,9,12,13,16,17,20,21,24,25,28,29},{2,3,6,7,10,11,14,15,18,19,..., dimensions={0} | all-to-all | bytes 262144 | tf_op jit(solution)/shard_map/all_to_all | solution.py:459
  49.0 0.0 copy-done.1
  49.0 0.0 copy-done.2
  49.0 0.0 copy-done.3
  49.0 0.0 copy-done.4
  49.0 0.0 copy-done.5
  49.0 0.0 copy-done.8
  49.0 0.9 %residual.1 = (f32[8,32,32]{2,1,0:T(8,128)S(1)}, f32[8,32,32]{2,1,0:T(8,128)S(1)}, f32[16,1,128]{2,1,0:T(1,128)S(1)}) custom-call(bf16[8,2,32,128]{3,2,1,0:T(8,128)(2,1)S(1)} %bitcast.8, bf16[768,32]{1,0:T(8,128)(2,1)S(1)} %copy-done.2, f32[32,32]{1,0:T(8,128)S(1)} %copy-done.5, f32[8,32,32]{2,1,0:T(8,128)S(1)} %copy-done.3, f32[8,32,32]{2,1,0:T(8,128)S(1)} %copy-done.4, ...), custom_call_target="tpu_custom_call" | custom-call | tf_op jit(solution)/shard_map/residual/pallas_call | solution.py:606
  49.9 9.3 %all_to_all.17.norms_ref = f32[16,1,128]{2,1,0:T(1,128)S(1)} all-to-all(f32[16,1,128]{2,1,0:T(1,128)S(1)} %get-tuple-element.33), channel_id=1, replica_groups=mesh['sx'=4,'sy'=4,'fq'=2] {'sx','sy'}, dimensions={0} | all-to-all | bytes 16384 | tf_op jit(solution)/shard_map/all_to_all | solution.py:614
  59.3 0.0 copy-done.9
  59.3 1.4 %direction.1 = (f32[8,32,32]{2,1,0:T(8,128)}, f32[8,32,32]{2,1,0:T(8,128)}, f32[8,32,32]{2,1,0:T(8,128)}, f32[8]{0:T(128)}) custom-call(f32[16,1,128]{2,1,0:T(1,128)S(1)} %all_to_all.17.norms_ref, f32[8,32,32]{2,1,0:T(8,128)S(1)} %get-tuple-element.34.solution_ref, f32[8,32,32]{2,1,0:T(8,128)S(1)} %get-tuple-element.35.residual_ref, ...), custom_call_target="tpu_custom_call" | custom-call | tf_op jit(solution)/shard_map/direction/pallas_call | solution.py:615
  (1 shorter events, 0.0 us)
Async XLA Ops:
  2.5 17.7 %copy-start = (bf16[8,2,32,16,512]{4,3,2,1,0:T(8,128)(2,1)S(1)}, bf16[8,2,32,16,512]{4,3,2,1,0:T(8,128)(2,1)}, u32[]{:S(2)}) copy-start(bf16[8,2,32,16,512]{4,3,2,1,0:T(8,128)(2,1)} %spectra_ref.5) | copy-start | bytes 25165828
  18.9 1.3 %collective-permute-start = (bf16[8,2,32,128]{3,2,1,0:T(8,128)(2,1)S(1)}, bf16[8,2,32,128]{3,2,1,0:T(8,128)(2,1)S(1)}, u32[]{:S(2)}, u32[]{:S(2)}) collective-permute-start(bf16[8,2,32,128]{3,2,1,0:T(8,128)(2,1)S(1)} %bitcast.5), channel_id=1, source_target_pairs={{0,2},{2,0},{4,6},{6,4},{1,3},{3,1},{5,7},{7,5},{8,10},{10,8},{12,... | collective-permute-start | bytes 393224 | tf_op jit(solution)/shard_map/ppermute | solution.py:510
  18.9 0.7 %copy-start.6 = (s32[32,16]{0,1:T(8,128)S(1)}, s32[32,16]{0,1:T(8,128)}, u32[]{:S(2)}) copy-start(s32[32,16]{0,1:T(8,128)} %param.13) | copy-start | bytes 6148
  19.6 5.9 %copy-start.7 = (f32[8]{0:T(128)S(1)}, f32[8]{0:T(128)}, u32[]{:S(2)}) copy-start(f32[8]{0:T(128)} %kappa_ref.5) | copy-start | bytes 100
  22.6 3.7 %collective-permute-start.1 = (bf16[96,384]{1,0:T(8,128)(2,1)S(1)}, bf16[96,384]{1,0:T(8,128)(2,1)S(1)}, u32[]{:S(2)}, u32[]{:S(2)}) collective-permute-start(bf16[96,384]{1,0:T(8,128)(2,1)S(1)} %get-tuple-element.23), channel_id=1, source_target_pairs={{2,4},{4,2},{3,5},{5,3},{10,12},{12,10},{11,13},{13,11},{18,20},{2... | collective-permute-start | bytes 221192 | tf_op jit(solution)/shard_map/ppermute | solution.py:443
  23.3 3.1 %collective-permute-start.2 = (bf16[96,384]{1,0:T(8,128)(2,1)S(1)}, bf16[96,384]{1,0:T(8,128)(2,1)S(1)}, u32[]{:S(2)}, u32[]{:S(2)}) collective-permute-start(bf16[96,384]{1,0:T(8,128)(2,1)S(1)} %get-tuple-element.24), channel_id=1, source_target_pairs={{0,2},{2,0},{4,6},{6,4},{1,3},{3,1},{5,7},{7,5},{8,10},{10,8},{12,... | collective-permute-start | bytes 221192 | tf_op jit(solution)/shard_map/ppermute | solution.py:444
  26.5 6.4 %collective-permute-start.3 = (bf16[72,384]{1,0:T(8,128)(2,1)S(1)}, bf16[72,384]{1,0:T(8,128)(2,1)S(1)}, u32[]{:S(2)}, u32[]{:S(2)}) collective-permute-start(bf16[72,384]{1,0:T(8,128)(2,1)S(1)} %get-tuple-element.29), channel_id=1, source_target_pairs={{8,16},{16,8},{9,17},{17,9},{10,18},{18,10},{11,19},{19,11},{12,20... | collective-permute-start | bytes 165896 | tf_op jit(solution)/shard_map/ppermute | solution.py:443
  27.1 5.7 %collective-permute-start.4 = (bf16[72,384]{1,0:T(8,128)(2,1)S(1)}, bf16[72,384]{1,0:T(8,128)(2,1)S(1)}, u32[]{:S(2)}, u32[]{:S(2)}) collective-permute-start(bf16[72,384]{1,0:T(8,128)(2,1)S(1)} %get-tuple-element.30), channel_id=1, source_target_pairs={{0,8},{8,0},{16,24},{24,16},{1,9},{9,1},{17,25},{25,17},{2,10},{10... | collective-permute-start | bytes 165896 | tf_op jit(solution)/shard_map/ppermute | solution.py:444
  32.8 16.2 %copy-start.1 = (f32[8,32,32]{2,1,0:T(8,128)S(1)}, f32[8,32,32]{2,1,0:T(8,128)}, u32[]{:S(2)}) copy-start(f32[8,32,32]{2,1,0:T(8,128)} %direction_ref.3) | copy-start | bytes 98308
  32.8 16.2 %copy-start.2 = (bf16[768,32]{1,0:T(8,128)(2,1)S(1)}, bf16[768,32]{1,0:T(8,128)(2,1)}, u32[]{:S(2)}) copy-start(bf16[768,32]{1,0:T(8,128)(2,1)} %constant.5.clone.table_ref) | copy-start | bytes 147460
  32.8 16.2 %copy-start.3 = (f32[8,32,32]{2,1,0:T(8,128)S(1)}, f32[8,32,32]{2,1,0:T(8,128)}, u32[]{:S(2)}) copy-start(f32[8,32,32]{2,1,0:T(8,128)} %solution_ref.1) | copy-start | bytes 98308
  32.8 16.2 %copy-start.4 = (f32[8,32,32]{2,1,0:T(8,128)S(1)}, f32[8,32,32]{2,1,0:T(8,128)}, u32[]{:S(2)}) copy-start(f32[8,32,32]{2,1,0:T(8,128)} %residual_ref.1) | copy-start | bytes 98308
  32.8 16.2 %copy-start.5 = (f32[32,32]{1,0:T(8,128)S(1)}, f32[32,32]{1,0:T(8,128)}, u32[]{:S(2)}) copy-start(f32[32,32]{1,0:T(8,128)} %noise_ref.1) | copy-start | bytes 12292
  32.8 16.2 %copy-start.8 = (f32[8]{0:T(128)S(1)}, f32[8]{0:T(128)}, u32[]{:S(2)}) copy-start(f32[8]{0:T(128)} %step_ref.1) | copy-start | bytes 100
  32.8 26.4 %copy-start.9 = (f32[8]{0:T(128)S(1)}, f32[8]{0:T(128)}, u32[]{:S(2)}) copy-start(f32[8]{0:T(128)} %old_ref.1) | copy-start | bytes 100
  34.3 2.6 %collective-permute-start.5 = (bf16[8,2,32,128]{3,2,1,0:T(8,128)(2,1)S(1)}, bf16[8,2,32,128]{3,2,1,0:T(8,128)(2,1)S(1)}, u32[]{:S(2)}, u32[]{:S(2)}) collective-permute-start(bf16[8,2,32,128]{3,2,1,0:T(8,128)(2,1)S(1)} %get-tuple-element.32), channel_id=1, source_target_pairs={{0,2},{2,0},{4,6},{6,4},{1,3},{3,1},{5,7},{7,5},{8,10},{10,8},{12,... | collective-permute-start | bytes 393224 | tf_op jit(solution)/shard_map/ppermute | solution.py:604
